TPU v7x, 32 devices: a whole 2x2x4 slice. The times are simulated.
32 devices in a mesh: row: 16 (over z, x, core), col: 2 (over y).
Axes of the slice: x: 2, y: 2, z: 4, core: 2. Of those that a mesh axis runs over, the one named last changes fastest.
Arguments:
- row_emb: bfloat16 [16384, 256], P('row'), may hold values from -1.5 to 1.5
- col_emb: bfloat16 [2048, 256], P('col'), may hold values from -1.5 to 1.5
- counts: int32 [2, 16384, 2048], P(None, 'row', 'col'), may hold values from 0 to 2025, as said below
- row_totals: int32 [16384], P('row'), may hold values from 1 to 4096
- col_totals: int32 [2048], P('col'), may hold values from 1 to 4096
- row_ids: int32 [2, 16384], replicated, may hold values from 0 to 16383, as said below
- col_ids: int32 [2, 2048], P(None, 'col'), may hold values from 0 to 2047, as said below
Outputs:
- grad_rows: float32 [16384, 256], P('row')
- grad_cols: float32 [2048, 256], P('col')
Inputs may be any that keep to these rules, and one draw needn't show every extreme that they name: `row_ids`: for each step a permutation of 0 to 16383; position p of it holds an item whose id divided by 1024 (rounded down) equals p modulo 16384 / 1024. `col_ids`: for each step and each c, positions c * 1024 to (c + 1) * 1024 - 1 hold a permutation of the items c * 1024 to (c + 1) * 1024 - 1. `counts`: about half of the entries are zero.
All inputs are finite; a program needn't handle non-finite values.
Results may differ from a plain program's by a relative error of at most 0.0037.
Values may be sent and summed in bfloat16 or wider, within the bound.
No kernel may reach another device: no remote copies, remote signals or barrier semaphores. Data moves between devices by JAX's collectives and lax.ppermute only.
A program may use at most 64 MiB of HBM per device.

v0:
```python
import math

import jax
import jax.numpy as jnp
from jax import lax
from jax.sharding import PartitionSpec as P

log_total = 8.0


def block_slope(scores, block_counts, row_log, col_log):
    counted = block_counts.astype(jnp.float32)
    offset = log_total - row_log.astype(jnp.float32)[:, None] - col_log[None, :]
    fitted = (0.1 + 0.25 * jnp.sqrt(counted)) * (
        scores - jnp.log(jnp.maximum(counted, 1.0)) - offset
    )
    hinge = jax.nn.sigmoid(scores - offset)
    return jnp.where(block_counts > 0, fitted, hinge)


def local(row_emb, col_emb, counts, row_totals, col_totals, row_ids, col_ids):
    owners = lax.axis_size("row")
    block_rows = row_emb.shape[0]
    block_cols = col_emb.shape[0]
    width = row_emb.shape[1]
    share = block_rows // owners
    step_count = counts.shape[0]
    myself = lax.axis_index("row")
    layout = row_ids.reshape(step_count, owners, share, owners)
    wanted = lax.dynamic_index_in_dim(layout, myself, axis=3, keepdims=False) - myself * block_rows
    wanted = jnp.transpose(wanted, (0, 2, 1))
    sending = row_emb[wanted]
    log_rows = jnp.log(row_totals.astype(jnp.float32)).astype(jnp.bfloat16)[wanted]
    fetched, fetched_logs = (
        lax.all_to_all(sending, "row", split_axis=2, concat_axis=2, tiled=True),
        lax.all_to_all(log_rows, "row", split_axis=2, concat_axis=2, tiled=True),
    )
    fetched = fetched.reshape(step_count, block_rows, width)
    fetched_logs = fetched_logs.reshape(step_count, block_rows)
    col_local = col_ids - lax.axis_index("col") * block_cols
    col_logs = jnp.log(col_totals.astype(jnp.float32))
    scale = (step_count * math.sqrt(owners * block_rows * lax.axis_size("col") * block_cols)) ** (
        -0.5
    )
    row_terms = []
    col_accum = jnp.zeros((block_cols, width), jnp.float32)
    for step in range(step_count):
        step_rows = fetched[step]
        columns = col_emb[col_local[step]]
        scores = lax.dot_general(
            step_rows, columns, (((1,), (1,)), ((), ())), preferred_element_type=jnp.float32
        )
        slope = block_slope(scores, counts[step], fetched_logs[step], col_logs[col_local[step]])
        weights = (slope * scale).astype(jnp.bfloat16)
        row_terms.append(jnp.dot(weights, columns, preferred_element_type=jnp.float32))
        col_term = lax.dot_general(
            weights, step_rows, (((0,), (0,)), ((), ())), preferred_element_type=jnp.float32
        )
        col_accum = col_accum.at[col_local[step]].add(col_term)
    row_partial = jnp.stack(row_terms).reshape(step_count, share, owners, width)
    empty_rows = jnp.zeros((block_rows, width), jnp.float32)
    routed = lax.all_to_all(row_partial, "row", split_axis=2, concat_axis=2, tiled=True)
    collected = empty_rows.at[wanted.reshape(-1)].add(routed.reshape(-1, width))
    grad_rows = lax.psum(collected, "col")
    grad_cols = lax.psum(col_accum, "row")
    return (grad_rows, grad_cols)


def solution(mesh):
    in_specs = (
        P("row", None),
        P("col", None),
        P(None, "row", "col"),
        P("row"),
        P("col"),
        P(),
        P(None, "col"),
    )
    out_specs = (P("row", None), P("col", None))
    return jax.shard_map(local, mesh=mesh, in_specs=in_specs, out_specs=out_specs, check_vma=False)
```

profile of v0, /device:TPU:0, one launch (start us, length us, event | category | flops | bytes accessed | tf_op | source)
XLA Modules:
  0.0 267.6 jit_solution(15605398765873177811)
XLA Ops:
  7.2 0.7 log_convert_fusion
  7.9 1.3 reshape.158
  9.2 0.9 subtract_reduce_fusion
  10.2 0.1 copy.31
  10.3 0.1 reshape.163
  10.3 13.1 %gather_fusion.2 = bf16[2048]{0:T(1024)(128)(2,1)S(1)} fusion(bf16[1024]{0:T(1024)(128)(2,1)S(1)} %log_convert_fusion, s32[2048]{0:T(1024)S(1)} %broadcast_clamp_fusion), kind=kCustom, calls=%fused_computation.2 | custom fusion | bytes 16384 | tf_op jit(solution)/shard_map/gather | solution.py:33
  23.4 0.1 reshape.178
  23.5 0.7 copy.34
  24.2 7.4 %all-to-all-start.1 = ((bf16[2,64,16]{1,0,2:T(2,128)(2,1)}), bf16[2,64,16]{1,0,2:T(2,128)(2,1)S(1)}, u32[]{:S(2)}, u32[]{:S(2)}) async-start(bf16[2,64,16]{1,0,2:T(2,128)(2,1)} %copy.34), calls=%async_computation.1 | async-start | bytes 16384 | tf_op jit(solution)/shard_map/all_to_all | solution.py:36
  31.6 7.5 %gather_fusion = bf16[2048,256]{1,0:T(8,128)(2,1)S(1)} fusion(bf16[1024,256]{1,0:T(8,128)(2,1)S(1)} %copy-done, s32[2048]{0:T(1024)S(1)} %broadcast_clamp_fusion), kind=kCustom, calls=%fused_computation | custom fusion | bytes 2105344 | tf_op jit(solution)/shard_map/gather | solution.py:32
  39.1 1.3 copy.32
  40.5 6.0 %all-to-all-start = ((bf16[2,64,16,256]{3,1,0,2:T(8,128)(2,1)}), bf16[2,64,16,256]{3,1,0,2:T(8,128)(2,1)S(1)}, u32[]{:S(2)}, u32[]{:S(2)}) async-start(bf16[2,64,16,256]{3,1,0,2:T(8,128)(2,1)} %copy.32), calls=%async_computation | async-start | bytes 2097152 | tf_op jit(solution)/shard_map/all_to_all | solution.py:35
  46.6 4.5 %gather_fusion.3 = f32[1024]{0:T(1024)S(1)} fusion(f32[1024]{0:T(1024)S(1)} %convert_log_fusion, s32[1024]{0:T(1024)S(1)} %broadcast_clamp_fusion.2), kind=kCustom, calls=%fused_computation.3 | custom fusion | bytes 12288 | tf_op jit(solution)/shard_map/gather | solution.py:53
  51.1 4.5 %gather_fusion.5 = f32[1024]{0:T(1024)S(1)} fusion(f32[1024]{0:T(1024)S(1)} %convert_log_fusion, s32[1024]{0:T(1024)S(1)} %broadcast_clamp_fusion.1), kind=kCustom, calls=%fused_computation.5 | custom fusion | bytes 12288 | tf_op jit(solution)/shard_map/gather | solution.py:53
  55.7 5.0 %gather_fusion.4 = bf16[1024,256]{1,0:T(8,128)(2,1)} fusion(bf16[1024,256]{1,0:T(8,128)(2,1)S(1)} %copy-done.1, s32[1024]{0:T(1024)S(1)} %broadcast_clamp_fusion.1), kind=kCustom, calls=%fused_computation.4 | custom fusion | bytes 1052672 | tf_op jit(solution)/shard_map/gather | solution.py:49
  60.6 4.9 %gather_fusion.1 = bf16[1024,256]{1,0:T(8,128)(2,1)} fusion(bf16[1024,256]{1,0:T(8,128)(2,1)S(1)} %copy-done.1, s32[1024]{0:T(1024)S(1)} %broadcast_clamp_fusion.2), kind=kCustom, calls=%fused_computation.1 | custom fusion | bytes 1052672 | tf_op jit(solution)/shard_map/gather | solution.py:49
  65.6 0.1 copy.39
  65.7 0.1 sub.96
  65.8 0.1 copy.36
  65.9 0.1 sub.88
  65.9 3.5 %all-to-all-done = bf16[2,64,16,256]{3,1,0,2:T(8,128)(2,1)S(1)} async-done(((bf16[2,64,16,256]{3,1,0,2:T(8,128)(2,1)}), bf16[2,64,16,256]{3,1,0,2:T(8,128)(2,1)S(1)}, u32[]{:S(2)}, u32[]{:S(2)}) %all-to-all-start) | async-done | bytes 1048608 | tf_op jit(solution)/shard_map/all_to_all | solution.py:35
  69.4 0.1 fusion.20
  69.5 0.3 copy.43
  69.8 0.3 copy.45
  70.1 5.7 %fusion.11 = bf16[1024,1024]{1,0:T(8,128)(2,1)S(1)} fusion(s32[2,1024,1024]{2,1,0:T(8,128)} %param.9, f32[1024]{0:T(1024)S(1)} %gather_fusion.5, f32[1024]{0:T(1024)S(1)} %sub.96, bf16[1024,256]{1,0:T(8,128)(2,1)S(1)} %bitcast.51, bf16[1024,256]{1,0:T(8,128)(2,1)S(1)} %copy-done.4), kind=kOutput, calls=%fused_computation.24 | convolution fusion | flops 553648128 | bytes 7348224 | tf_op jit(solution)/shard_map/dot_general | solution.py:50
  75.8 0.7 fusion.23
  76.6 0.6 copy.41
  77.2 0.1 copy-done.3
  77.3 3.9 %fusion.3 = bf16[1024,1024]{1,0:T(8,128)(2,1)S(1)} fusion(s32[2,1024,1024]{2,1,0:T(8,128)S(1)} %bitcast.62, f32[1024]{0:T(1024)S(1)} %gather_fusion.3, f32[1024]{0:T(1024)S(1)} %sub.88, bf16[1024,256]{1,0:T(8,128)(2,1)S(1)} %bitcast.53, bf16[1024,256]{1,0:T(8,128)(2,1)S(1)} %copy-done.3), kind=kOutput, calls=%fused_computation.16 | convolution fusion | flops 553648128 | bytes 7348224 | tf_op jit(solution)/shard_map/dot_general | solution.py:50
  81.2 0.7 fusion.22
  82.0 0.6 copy.40
  82.6 1.5 pad_maximum_fusion
  84.1 6.9 %all-to-all-start.2 = ((f32[2,64,16,256]{3,1,0,2:T(8,128)}), f32[2,64,16,256]{3,1,0,2:T(8,128)}, u32[]{:S(2)}, u32[]{:S(2)}) async-start(f32[2,64,16,256]{3,1,0,2:T(8,128)} %pad_maximum_fusion), calls=%async_computation.2 | async-start | bytes 4194304 | tf_op jit(solution)/shard_map/all_to_all | solution.py:62
  91.1 2.3 fusion.24
  93.4 6.3 %scatter_custom_fusion.1 = f32[1024,256]{1,0:T(8,128)S(1)} fusion(s32[1024]{0:T(1024)S(1)} %bitcast.59, f32[1024,256]{1,0:T(8,128)S(1)} %fusion.24, f32[]{:T(128)} %constant.11.clone.1), kind=kCustom, calls=%fused_computation.33 | custom fusion | flops 262144 | bytes 1048580 | tf_op jit(solution)/shard_map/scatter-add | solution.py:59
  99.7 2.3 fusion.25
  102.1 6.5 %scatter_fusion = f32[1024,256]{1,0:T(8,128)S(1)} fusion(f32[1024,256]{1,0:T(8,128)S(1)} %scatter_custom_fusion.1, s32[1024]{0:T(1024)S(1)} %bitcast.57, f32[1024,256]{1,0:T(8,128)S(1)} %fusion.25), kind=kCustom, calls=%fused_computation.8 | custom fusion | flops 262144 | bytes 3149824 | tf_op jit(solution)/shard_map/scatter-add | solution.py:59
  108.5 1.0 copy-done.2
  109.5 0.0 all-reduce.3.cloned.1.call-start
  109.6 0.1 copy.30
  109.7 0.1 reshape.159
  109.8 25.0 %all-to-all-done.2 = f32[2,64,16,256]{3,1,0,2:T(8,128)} async-done(((f32[2,64,16,256]{3,1,0,2:T(8,128)}), f32[2,64,16,256]{3,1,0,2:T(8,128)}, u32[]{:S(2)}, u32[]{:S(2)}) %all-to-all-start.2) | async-done | bytes 2097184 | tf_op jit(solution)/shard_map/all_to_all | solution.py:62
  134.8 2.8 %copy.42 = f32[2,64,16,256]{3,2,1,0:T(8,128)S(1)} copy(f32[2,64,16,256]{3,1,0,2:T(8,128)} %all-to-all-done.2) | data formatting | bytes 4194304 | tf_op jit(solution)/shard_map/all_to_all | solution.py:62
  137.6 12.5 %scatter_custom_fusion = f32[1024,256]{1,0:T(8,128)} fusion(s32[2048]{0:T(1024)S(1)} %bitcast.60, f32[2048,256]{1,0:T(8,128)S(1)} %bitcast.48, f32[]{:T(128)} %constant.11.clone.1), kind=kCustom, calls=%fused_computation.35 | custom fusion | flops 524288 | bytes 1048580 | tf_op jit(solution)/shard_map/scatter-add | solution.py:63
  150.2 63.9 %all-reduce.5.cloned.1.call-done = f32[1024,256]{1,0:T(8,128)} async-done(((f32[1024,256]{1,0:T(8,128)}), f32[1024,256]{1,0:T(8,128)}) %all-reduce.5.cloned.1.call-update) | async-done | bytes 1048592 | tf_op jit(solution)/shard_map/psum | solution.py:65
  214.1 42.2 %all-reduce.3.cloned.1.call-done = f32[1024,256]{1,0:T(8,128)} async-done(((f32[1024,256]{1,0:T(8,128)}), f32[1024,256]{1,0:T(8,128)}) %all-reduce.3.cloned.1.call-update) | async-done | bytes 1048592 | tf_op jit(solution)/shard_map/psum | solution.py:64
  256.3 2.3 copy.52
  258.5 2.3 copy.53
  (35 shorter events, 0.2 us)
Async XLA Ops:
  7.2 24.4 %copy-start = (bf16[1024,256]{1,0:T(8,128)(2,1)S(1)}, bf16[1024,256]{1,0:T(8,128)(2,1)}, u32[]{:S(2)}) copy-start(bf16[1024,256]{1,0:T(8,128)(2,1)} %param.7) | copy-start | bytes 1572868
  24.2 16.2 %all-to-all-start.1 = ((bf16[2,64,16]{1,0,2:T(2,128)(2,1)}), bf16[2,64,16]{1,0,2:T(2,128)(2,1)S(1)}, u32[]{:S(2)}, u32[]{:S(2)}) async-start(bf16[2,64,16]{1,0,2:T(2,128)(2,1)} %copy.34), calls=%async_computation.1 | async-start | bytes 16384 | tf_op jit(solution)/shard_map/all_to_all | solution.py:36
  39.1 7.4 %copy-start.6 = (s32[1024]{0:T(1024)S(1)}, s32[1024]{0:T(1024)}, u32[]{:S(2)}) copy-start(s32[1024]{0:T(1024)} %param.11) | copy-start | bytes 12292
  39.1 7.4 %copy-start.5 = (s32[2,1024]{1,0:T(2,128)S(1)}, s32[2,1024]{1,0:T(2,128)}, u32[]{:S(2)}) copy-start(s32[2,1024]{1,0:T(2,128)} %param.13) | copy-start | bytes 24580
  40.5 29.0 %all-to-all-start = ((bf16[2,64,16,256]{3,1,0,2:T(8,128)(2,1)}), bf16[2,64,16,256]{3,1,0,2:T(8,128)(2,1)S(1)}, u32[]{:S(2)}, u32[]{:S(2)}) async-start(bf16[2,64,16,256]{3,1,0,2:T(8,128)(2,1)} %copy.32), calls=%async_computation | async-start | bytes 2097152 | tf_op jit(solution)/shard_map/all_to_all | solution.py:35
  46.6 9.1 %copy-start.1 = (bf16[1024,256]{1,0:T(8,128)(2,1)S(1)}, bf16[1024,256]{1,0:T(8,128)(2,1)}, u32[]{:S(2)}) copy-start(bf16[1024,256]{1,0:T(8,128)(2,1)} %param.8) | copy-start | bytes 1572868
  65.6 4.5 %copy-start.4 = (bf16[1024,256]{1,0:T(8,128)(2,1)S(1)}, bf16[1024,256]{1,0:T(8,128)(2,1)}, u32[]{:S(2)}) copy-start(bf16[1024,256]{1,0:T(8,128)(2,1)} %gather_fusion.4) | copy-start | bytes 1572868
  69.5 7.7 %slice-start = ((s8[8388608]{0:T(1024)(128)(4,1)}), s8[4194304]{0:T(1024)(128)(4,1)S(1)}, s32[]{:S(2)}) async-start(s8[8388608]{0:T(1024)(128)(4,1)} %bitcast.61), calls=%async_computation.5 | async-start | bytes 8388608
  70.1 7.1 %slice-start.1 = ((s8[8388608]{0:T(1024)(128)(4,1)}), s8[4194304]{0:T(1024)(128)(4,1)S(1)}, s32[]{:S(2)}) async-start(s8[8388608]{0:T(1024)(128)(4,1)} %bitcast.61), calls=%async_computation.6 | async-start | bytes 8388608
  75.8 5.4 %copy-start.7 = (bf16[1024,1024]{1,0:T(8,128)(2,1)}, bf16[1024,1024]{1,0:T(8,128)(2,1)S(1)}, u32[]{:S(2)}) copy-start(bf16[1024,1024]{1,0:T(8,128)(2,1)S(1)} %fusion.11) | copy-start | bytes 6291460
  75.8 1.4 copy-start.3
  81.2 1.4 copy-start.8
  84.1 50.7 %all-to-all-start.2 = ((f32[2,64,16,256]{3,1,0,2:T(8,128)}), f32[2,64,16,256]{3,1,0,2:T(8,128)}, u32[]{:S(2)}, u32[]{:S(2)}) async-start(f32[2,64,16,256]{3,1,0,2:T(8,128)} %pad_maximum_fusion), calls=%async_computation.2 | async-start | bytes 4194304 | tf_op jit(solution)/shard_map/all_to_all | solution.py:62
  91.0 123.0 %all-reduce.5.cloned.1.call-start = ((), (), s32[]{:S(2)}) async-start(), calls=%async_computation.4 | async-start | bytes 2097152 | tf_op jit(solution)/shard_map/psum | solution.py:65
  108.5 1.0 copy-start.2
  109.5 146.7 %all-reduce.3.cloned.1.call-start = ((), (), s32[]{:S(2)}) async-start(), calls=%async_computation.3 | async-start | bytes 2097152 | tf_op jit(solution)/shard_map/psum | solution.py:64
Sparse Core Ops, SparseCore 0:
  109.6 104.3 all-reduce.4
  216.9 39.2 all-reduce.2
where the time goes:
time: 268 us
  waiting for transfers between devices  135 us (50%)
  local copies, waits for them, and re-layouts  53.9 us (20%)
  other arithmetic  28.5 us (11%)
  starting transfers between devices  20.4 us (8%)
  matrix products  15.7 us (6%)
  between operations  14.4 us (5%)
    psum x1, waiting for transfers between devices, local(): grad_cols = lax.psum(col_accum, 'row')  63.9 us
    psum x1, waiting for transfers between devices, local(): grad_rows = lax.psum(collected, 'col')  42.2 us
    all_to_all x1, waiting for transfers between devices, local(): lax.all_to_all(row_partial, 'row', split_axis=2, concat_axis=2, tiled=True)  25 us
    gather x3, local copies, waits for them, and re-layouts, local(): jnp.log(row_totals.astype(jnp.float32)).astype(jnp.bfloat16)[wanted]  13.9 us
    scatter-add x2, other arithmetic, local(): col_accum = col_accum.at[col_local[step]].add(col_term)  12.8 us
    scatter-add x1, other arithmetic, local(): collected = empty_rows.at[wanted.reshape(-1)].add(routed.reshape(-1, width))  12.5 us
    gather x2, local copies, waits for them, and re-layouts, local(): columns = col_emb[col_local[step]]  9.91 us
    dot_general x2, matrix products, local(): lax.dot_general(step_rows, columns, (((1,), (1,)), ((), ())), preferred_e...  9.64 us
  transfers between devices with their start and end apart: 5, of which 4 were waited for; matrix products, arithmetic and copies ran while one was open for 23% of the time, Pallas kernels for 0%

commit v1 on v0

v1 whole, which is shorter than its diff:
```python
import functools
import math

import jax
import jax.numpy as jnp
from jax import lax
from jax.experimental import pallas as pl
from jax.experimental.pallas import tpu as pltpu
from jax.sharding import PartitionSpec as P

log_total = 8.0
f32 = jnp.float32
bf16 = jnp.bfloat16
MIB = 1 << 20


def nt(a, b):
    return lax.dot_general(a, b, (((1,), (1,)), ((), ())), preferred_element_type=f32)


def tn(a, b):
    return lax.dot_general(a, b, (((0,), (0,)), ((), ())), preferred_element_type=f32)


def nn(a, b):
    return jnp.dot(a, b, preferred_element_type=f32)


def iota(shape, dim):
    return lax.broadcasted_iota(jnp.int32, shape, dim)


def ones_where(cond):
    return jnp.where(cond, 1.0, 0.0).astype(bf16)


def split_index(ids, size):
    local = ids & (size - 1)
    return (local >> 5).astype(f32).astype(bf16), (local & 31).astype(f32).astype(bf16)


def swap_halves(x, half):
    width = x.shape[1] // 2
    a, b = x[:, :width], x[:, width:]
    first = jnp.where(half == 0, a, b)
    second = jnp.where(half == 0, b, a)
    return jnp.concatenate([first, second], axis=1)


def kernel_call(body, outs, *args, vmem=32, cost=None, **kw):
    return pl.pallas_call(
        body,
        out_shape=outs,
        compiler_params=pltpu.CompilerParams(vmem_limit_bytes=vmem * MIB),
        cost_estimate=cost,
        **kw,
    )(*args)


def cost(flops, nbytes):
    return pl.CostEstimate(flops=int(flops), bytes_accessed=int(nbytes), transcendentals=0)


class Plan:
    def __init__(self, owners, cols, steps, block, width):
        self.owners = owners
        self.cols = cols
        self.steps = steps
        self.block = block
        self.width = width
        self.half = width // 2
        self.chips = owners // 2
        self.share = block // owners
        self.pair = 2 * self.share
        self.far_bit = self.chips // 2
        self.near = [m for m in range(self.chips) if not m & self.far_bit]
        self.far = [m for m in range(self.chips) if m & self.far_bit]
        self.deep = min(4, self.chips)
        self.wide = self.chips // self.deep
        self.msg_rows = steps * self.pair + 16


def fetch_kernel(p, ids_ref, own_ref, oth_ref, tot_own_ref, tot_oth_ref, *msgs):
    r = lax.axis_index("row")
    half = lax.axis_index("col") % 2
    lines = p.steps * p.owners * 8
    group = 128 // p.owners
    hi, lo = split_index(ids_ref[...].reshape(lines, 128), p.block)
    sub = iota((p.pair, 128), 0)
    lane = iota((p.pair, 128), 1)
    owner = r ^ (sub // p.share)
    inner = sub % p.share
    pick = ones_where((lane % p.owners == owner) & (lane // p.owners == inner % group))
    sub2 = iota((p.pair, lines), 0) % p.share
    lane2 = iota((p.pair, lines), 1)
    keep = lane2 % 8 == sub2 // group
    line = iota((lines, 128), 0)
    slot = iota((lines, 128), 1)
    step_ok = line // (p.owners * 8) == slot // p.chips
    dest = (line // 8) % p.owners
    route = ones_where(step_ok & (dest == (r ^ (2 * (slot % p.chips)))))

    def column(digit):
        picked = jnp.where(keep, nt(pick, digit), 0.0).astype(bf16)
        return nn(picked, route)

    index = (column(hi) * 32.0 + column(lo)).astype(jnp.int32)
    logs = jnp.zeros((16, p.chips * p.share), f32)
    log_row = iota((16, p.chips * p.share), 0)
    items = iota((p.share, p.block), 1)
    tables = [swap_halves(own_ref[...], half), swap_halves(oth_ref[...], half)]
    totals = [tot_own_ref, tot_oth_ref]
    for jj in range(2):
        table_log = jnp.log(totals[jj][...].astype(f32)).astype(bf16)
        table_log = jnp.broadcast_to(table_log, (16, p.block))
        for s in range(p.steps):
            pieces = []
            for m in range(p.chips):
                n = s * p.chips + m
                col = index[jj * p.share : (jj + 1) * p.share, n : n + 1]
                pieces.append(ones_where(items == col))
            onehot = jnp.concatenate(pieces, axis=0)
            rows = nn(onehot, tables[jj]).astype(bf16)
            logs = logs + jnp.where(log_row == s * 2 + jj, nt(table_log, onehot), 0.0)
            for m in range(p.chips):
                at = s * p.pair + jj * p.share
                w = msgs[m].shape[1]
                msgs[m][at : at + p.share, :] = rows[m * p.share : (m + 1) * p.share, :w]
    base = p.steps * p.pair
    for m in range(p.chips):
        tile = (m * p.share) // 128 * 128
        msgs[m][base : base + 16, :128] = logs[:, tile : tile + 128].astype(bf16)
        if msgs[m].shape[1] > 128:
            msgs[m][base : base + 16, 128:] = jnp.zeros((16, msgs[m].shape[1] - 128), bf16)


def fetch(p, ids, own, oth, tot_own, tot_oth):
    outs = []
    for m in range(p.chips):
        w = p.half if m & p.far_bit else p.width
        outs.append(jax.ShapeDtypeStruct((p.msg_rows, w), bf16))
    return kernel_call(
        functools.partial(fetch_kernel, p), outs, ids, own, oth, tot_own, tot_oth, vmem=40,
        cost=cost(4 * 2 * 512 * 1024 * 256, 4 * MIB),
    )


def columns_kernel(p, ids_ref, emb_ref, tot_ref, cols_ref, logs_ref):
    half = lax.axis_index("col") % 2
    block = emb_ref.shape[0]
    table = swap_halves(emb_ref[...], half)
    local = (ids_ref[...] & (block - 1)).astype(f32)
    sub8 = iota((8, block), 0)
    stack = jnp.zeros((8, block), f32)
    for s in range(p.steps):
        stack = jnp.where(sub8 == s, jnp.broadcast_to(local[s : s + 1, :], (8, block)), stack)
    index = stack.T.astype(jnp.int32)
    logs = jnp.log(tot_ref[...].astype(f32))
    first = logs.astype(bf16).astype(f32)
    second = (logs - first).astype(bf16).astype(f32)
    third = logs - first - second
    sub16 = iota((16, block), 0)
    digits = jnp.where(sub16 == 0, first, jnp.where(sub16 == 1, second, jnp.where(sub16 == 2, third, 0.0)))
    digits = digits.astype(bf16)
    items = iota((block, block), 1)
    out = jnp.zeros((8, block), f32)
    for s in range(p.steps):
        onehot = ones_where(items == index[:, s : s + 1])
        cols_ref[s] = nn(onehot, table).astype(bf16)
        got = nt(digits, onehot)
        row = got[0:1, :] + got[1:2, :] + got[2:3, :]
        out = jnp.where(sub8 == s, jnp.broadcast_to(row, (8, block)), out)
    logs_ref[...] = out


def columns(p, ids, emb, tot):
    block, width = emb.shape
    outs = [
        jax.ShapeDtypeStruct((p.steps, block, width), bf16),
        jax.ShapeDtypeStruct((8, block), f32),
    ]
    return kernel_call(
        functools.partial(columns_kernel, p), outs, ids, emb, tot, vmem=40,
        cost=cost(2 * 2 * 1024 * 1024 * 256, 2 * MIB),
    )


def factors_kernel(p, scale, counts_ref, gain_ref, shift_ref):
    r = lax.axis_index("row")
    for m in range(p.chips):
        for jj in range(2):
            owner = r ^ (2 * m + jj)
            x = counts_ref[0, pl.ds(owner, p.share, stride=p.owners), :].astype(f32)
            safe = jnp.maximum(x, 1.0)
            root = safe * lax.rsqrt(safe)
            gain = jnp.where(x > 0.0, (0.1 * scale) + (0.25 * scale) * root, 0.0)
            at = (2 * m + jj) * p.share
            gain_ref[0, at : at + p.share, :] = gain
            shift_ref[0, at : at + p.share, :] = jnp.log(safe)


def factors(p, scale, counts):
    steps, rows, width = counts.shape
    tile = 128
    spec = pl.BlockSpec((1, rows, tile), lambda s, t: (s, 0, t))
    shape = jax.ShapeDtypeStruct(counts.shape, f32)
    return kernel_call(
        functools.partial(factors_kernel, p, scale), [shape, shape], counts, vmem=24,
        grid=(steps, width // tile), in_specs=[spec], out_specs=[spec, spec],
        cost=cost(40 * counts.size, 12 * counts.size),
    )


def grads_kernel(p, scale, masks, split, *refs):
    count = len(masks)
    n_in = count * (2 if split else 1)
    msgs = refs[:n_in]
    cols_ref, col_logs_ref, gain_ref, shift_ref = refs[n_in : n_in + 4]
    keep_ref, side_ref, core_ref, diag_ref, acc_ref = refs[n_in + 4 : n_in + 9]
    rows_ref, logs_ref = refs[n_in + 9 :]
    s, t = pl.program_id(0), pl.program_id(1)
    base = p.steps * p.pair

    @pl.when((s == 0) & (t == 0))
    def _():
        for i, m in enumerate(masks):
            own = msgs[i]
            logs = own[base : base + 16, :128].astype(f32).T
            off = (m * p.share) % 128
            for step in range(p.steps):
                dst = i * p.pair
                src = step * p.pair
                if split:
                    other = msgs[count + i]
                    rows_ref[step, dst : dst + p.pair, : p.half] = own[src : src + p.pair, :]
                    rows_ref[step, dst : dst + p.pair, p.half :] = other[src : src + p.pair, :]
                else:
                    rows_ref[step, dst : dst + p.pair, :] = own[src : src + p.pair, :]
                for jj in range(2):
                    col = logs[off : off + p.share, step * 2 + jj : step * 2 + jj + 1]
                    at = dst + jj * p.share
                    logs_ref[step, at : at + p.share, :] = jnp.broadcast_to(
                        col - log_total, (p.share, 128)
                    )

    tile = gain_ref.shape[1]
    at = pl.multiple_of(t * tile, tile)
    x = rows_ref[s, pl.ds(at, tile), :]
    cols = cols_ref[s]
    row_logs = logs_ref[s, pl.ds(at, tile), :][:, :1]
    col_logs = col_logs_ref[pl.ds(s, 1), :]
    z = nt(x, cols) + (row_logs + col_logs)
    gain = gain_ref[0]
    fitted = gain * (z - shift_ref[0])
    hinge = (0.5 * scale) * jnp.tanh(0.5 * z) + (0.5 * scale)
    weights = jnp.where(gain > 0.0, fitted, hinge).astype(bf16)
    g = nn(weights, cols)
    for i in range(tile // p.pair):
        lo = i * p.pair
        mid = lo + p.share
        hi = mid + p.share
        keep_ref[0, i] = g[lo:mid, : p.half]
        side_ref[0, i] = g[lo:mid, p.half :].astype(bf16)
        core_ref[0, i] = g[mid:hi, : p.half].astype(bf16)
        diag_ref[0, i] = g[mid:hi, p.half :].astype(bf16)
    c = tn(weights, x)

    @pl.when(t == 0)
    def _():
        acc_ref[0] = c

    @pl.when(t != 0)
    def _():
        acc_ref[0] += c


def grads(p, scale, masks, split, msgs, cols, col_logs, gain, shift):
    count = len(masks)
    block = cols.shape[1]
    tile = min(256, count * p.pair)
    per = tile // p.pair
    tiles = count * p.pair // tile
    first = masks[0] * p.pair // tile
    whole = lambda a: pl.BlockSpec(a.shape, lambda s, t: (0,) * a.ndim)
    factor = pl.BlockSpec((1, tile, block), lambda s, t: (s, first + t, 0))
    piece = pl.BlockSpec((1, per, p.share, p.half), lambda s, t: (s, t, 0, 0))
    shape = (p.steps, count, p.share, p.half)
    outs = [jax.ShapeDtypeStruct(shape, f32)] + [jax.ShapeDtypeStruct(shape, bf16)] * 3
    outs.append(jax.ShapeDtypeStruct((p.steps, block, p.width), f32))
    return kernel_call(
        functools.partial(grads_kernel, p, scale, masks, split), outs,
        *msgs, cols, col_logs, gain, shift, vmem=48,
        grid=(p.steps, tiles),
        in_specs=[whole(a) for a in (*msgs, cols, col_logs)] + [factor, factor],
        out_specs=[piece] * 4 + [pl.BlockSpec((1, block, p.width), lambda s, t: (s, 0, 0))],
        scratch_shapes=[
            pltpu.VMEM((p.steps, count * p.pair, p.width), bf16),
            pltpu.VMEM((p.steps, count * p.pair, 128), f32),
        ],
        cost=cost(3 * 2 * p.steps * 512 * 1024 * 256, 10 * MIB),
    )


def merge_kernel(p, keep_ref, side_ref, core_ref, diag_ref, *outs):
    for i, out in enumerate(outs):
        for s in range(p.steps):
            out[s, 0] = (keep_ref[s, i] + side_ref[s, i].astype(f32)).astype(bf16)
            out[s, 1] = (core_ref[s, i].astype(f32) + diag_ref[s, i].astype(f32)).astype(bf16)


def merge(p, keep, side, core, diag):
    outs = [jax.ShapeDtypeStruct((p.steps, 2, p.share, p.half), bf16)] * keep.shape[1]
    return kernel_call(
        functools.partial(merge_kernel, p), outs, keep, side, core, diag, vmem=16,
        cost=cost(MIB, 2 * MIB),
    )


def collect_kernel(p, ids_ref, *refs):
    msgs, out_ref = refs[:-1], refs[-1]
    r = lax.axis_index("row")
    lines = p.steps * p.owners * 8
    group = 128 // p.owners
    slots = p.steps * p.chips
    hi, lo = split_index(ids_ref[...].reshape(lines, 128), p.block)
    lane = iota((128, p.pair), 0)
    inner = iota((128, p.pair), 1) % p.share
    pick = ones_where((lane % p.owners == r) & (lane // p.owners == inner % group))
    line = iota((lines, p.pair), 0)
    keep = line % 8 == (iota((lines, p.pair), 1) % p.share) // group
    slot = iota((slots, lines), 0)
    line2 = iota((slots, lines), 1)
    step_ok = line2 // (p.owners * 8) == slot // p.chips
    source = (line2 // 8) % p.owners
    routes = [ones_where(step_ok & (source == (r ^ (2 * (slot % p.chips) + jj)))) for jj in range(2)]

    def row(digit):
        picked = jnp.where(keep, nn(digit, pick), 0.0).astype(bf16)
        first = nn(routes[0], picked)
        second = nn(routes[1], picked)
        return jnp.where(iota((slots, p.pair), 1) < p.share, first, second)

    index = (row(hi) * 32.0 + row(lo)).astype(jnp.int32)
    items = iota((p.block, p.pair), 0)
    acc = jnp.zeros((p.block, p.half), f32)
    for s in range(p.steps):
        for m in range(0, p.chips, 2):
            n = s * p.chips + m
            onehot = jnp.concatenate(
                [ones_where(items == index[n + k : n + k + 1, :]) for k in range(2)], axis=1
            )
            rows = jnp.concatenate([msgs[m + k][s].reshape(p.pair, p.half) for k in range(2)], axis=0)
            acc = acc + nn(onehot, rows)
    out_ref[...] = acc.astype(bf16)


def collect(p, ids, msgs):
    return kernel_call(
        functools.partial(collect_kernel, p),
        jax.ShapeDtypeStruct((p.block, p.half), bf16), ids, *msgs, vmem=32,
        cost=cost(2 * 1024 * 2048 * 256, 2 * MIB),
    )


def join_kernel(own_ref, oth_ref, out_ref):
    half = lax.axis_index("col") % 2
    a, b = own_ref[...].astype(f32), oth_ref[...].astype(f32)
    width = a.shape[1]
    out_ref[:, :width] = jnp.where(half == 0, a, b)
    out_ref[:, width:] = jnp.where(half == 0, b, a)


def place_kernel(p, ids_ref, near_ref, far_ref, mine_ref, other_ref, acc_ref):
    r = lax.axis_index("row")
    block = near_ref.shape[1]
    local = ids_ref[...] & (block - 1)
    items = iota((block, block), 0)
    for s in range(p.steps):
        total = near_ref[s] + far_ref[s]
        top = total.astype(bf16)
        rest = (total - top.astype(f32)).astype(bf16)
        onehot = ones_where(items == local[s : s + 1, :])
        term = nn(onehot, top) + nn(onehot, rest)
        if s == 0:
            acc_ref[...] = term
        else:
            acc_ref[...] += term
    part = block // 2
    mine_ref[...] = acc_ref[pl.ds(pl.multiple_of((r % 2) * part, part), part), :]
    other_ref[...] = acc_ref[pl.ds(pl.multiple_of((1 - r % 2) * part, part), part), :]


def place(p, ids, near, far):
    block, width = near.shape[1:]
    out = jax.ShapeDtypeStruct((block // 2, width), f32)
    return kernel_call(
        functools.partial(place_kernel, p), [out, out], ids, near, far, vmem=40,
        scratch_shapes=[pltpu.VMEM((block, width), f32)],
        cost=cost(4 * 2 * 1024 * 1024 * 256, 5 * MIB),
    )


def spread_kernel(parts, stride, count, *refs):
    mine, arrived = refs[0], refs[1 : 1 + count]
    outs, acc_ref = refs[1 + count : -1], refs[-1]
    here = (lax.axis_index("row") // stride) % parts
    total = mine[...]
    for a in arrived:
        total = total + a[...].astype(f32)
    acc_ref[...] = total
    size = outs[0].shape[0]
    for k, out in enumerate(outs):
        at = pl.multiple_of((here ^ k) * size, size)
        out[...] = acc_ref[pl.ds(at, size), :].astype(out.dtype)


def spread(parts, stride, mine, arrived):
    rows, width = mine.shape
    size = rows // parts
    outs = [jax.ShapeDtypeStruct((size, width), bf16 if (parts == 1 or k) else f32) for k in range(parts)]
    return kernel_call(
        functools.partial(spread_kernel, parts, stride, len(arrived)), outs, mine, *arrived, vmem=16,
        scratch_shapes=[pltpu.VMEM((rows, width), f32)],
        cost=cost(MIB, MIB),
    )


def gather_kernel(parts, stride, unswap, *refs):
    pieces, out = refs[:-1], refs[-1]
    here = (lax.axis_index("row") // stride) % parts
    half = lax.axis_index("col") % 2
    size = pieces[0].shape[0]
    for k, piece in enumerate(pieces):
        at = pl.multiple_of((here ^ k) * size, size)
        value = piece[...].astype(out.dtype)
        if unswap:
            value = swap_halves(value, half)
        out[pl.ds(at, size), :] = value


def gather(stride, pieces, dtype=bf16, unswap=False):
    parts = len(pieces)
    rows, width = pieces[0].shape
    return kernel_call(
        functools.partial(gather_kernel, parts, stride, unswap),
        jax.ShapeDtypeStruct((parts * rows, width), dtype), *pieces, vmem=16,
        cost=cost(MIB, MIB),
    )


def local(row_emb, col_emb, counts, row_totals, col_totals, row_ids, col_ids):
    owners = lax.axis_size("row")
    cols_n = lax.axis_size("col")
    block, width = row_emb.shape
    block_cols = col_emb.shape[0]
    steps = counts.shape[0]
    p = Plan(owners, cols_n, steps, block, width)
    scale = (steps * math.sqrt(owners * block * cols_n * block_cols)) ** (-0.5)

    def row_swap(x, mask):
        return lax.ppermute(x, "row", [(i, i ^ mask) for i in range(owners)])

    def col_swap(x, mask=1):
        return lax.ppermute(x, "col", [(i, i ^ mask) for i in range(cols_n)])

    def diag_swap(x):
        perm = [
            (i * cols_n + j, (i ^ 1) * cols_n + (j ^ 1)) for i in range(owners) for j in range(cols_n)
        ]
        return lax.ppermute(x, ("row", "col"), perm)

    ids = row_ids.reshape(steps, owners * block // 128, 128)
    totals = row_totals.reshape(1, block)
    msgs = fetch(p, ids, row_emb, row_swap(row_emb, 1), totals, row_swap(totals, 1))
    got = [msgs[m] if m == 0 else row_swap(msgs[m], 2 * m) for m in range(p.chips)]
    cols, col_logs = columns(p, col_ids, col_emb, col_totals.reshape(1, block_cols))
    gain, shift = factors(p, scale, counts)
    near_in = [got[m] for m in p.near]
    far_in = [got[m] for m in p.far] + [col_swap(got[m]) for m in p.far]

    back = {}
    sums = []
    for masks, split, inputs in ((p.near, False, near_in), (p.far, True, far_in)):
        keep, side, core, diag, acc = grads(p, scale, masks, split, inputs, cols, col_logs, gain, shift)
        sums.append(acc)
        outs = merge(p, keep, col_swap(side), row_swap(core, 1), diag_swap(diag))
        for m, out in zip(masks, outs):
            back[m] = out if m == 0 else row_swap(out, 2 * m)

    mine, other = place(p, col_ids, *sums)
    arrived = [row_swap(other, 1)]
    for parts, stride in ((p.wide, 2), (p.deep, 2 * p.wide)):
        mine, *others = spread(parts, stride, mine, arrived)
        arrived = [row_swap(o, (k + 1) * stride) for k, o in enumerate(others)]
    (piece,) = spread(1, 1, mine, arrived)
    for parts, stride in ((p.deep, 2 * p.wide), (p.wide, 2)):
        piece = gather(stride, [piece] + [row_swap(piece, k * stride) for k in range(1, parts)])
    grad_cols = gather(1, [piece, row_swap(piece, 1)], f32, True)

    rows = collect(p, ids, [back[m] for m in range(p.chips)])
    if cols_n > 2:
        total = rows.astype(f32)
        for mask in range(2, cols_n, 2):
            total = total + col_swap(rows, mask).astype(f32)
        rows = total.astype(bf16)
    grad_rows = kernel_call(
        join_kernel, jax.ShapeDtypeStruct((block, width), f32), rows, col_swap(rows), vmem=16,
        cost=cost(MIB, 2 * MIB),
    )
    return grad_rows, grad_cols


def solution(mesh):
    in_specs = (
        P("row", None),
        P("col", None),
        P(None, "row", "col"),
        P("row"),
        P("col"),
        P(),
        P(None, "col"),
    )
    out_specs = (P("row", None), P("col", None))
    return jax.shard_map(local, mesh=mesh, in_specs=in_specs, out_specs=out_specs, check_vma=False)
```

time: 268 us -> 111 us (0.41)
  waiting for transfers between devices: 135 us -> 14 us
  local copies, waits for them, and re-layouts: 53.9 us -> 12.6 us
  Pallas kernels: 0 us -> 34.1 us
  other arithmetic: 28.5 us -> 0 us
  starting transfers between devices: 20.4 us -> 48.4 us
  matrix products: 15.7 us -> 0 us
  between operations: 14.4 us -> 0.85 us
    psum x2 -> x0, waiting for transfers between devices: 106 us -> none  [the longest x1 63.9 us: local(): grad_cols = lax.psum(col_accum, 'row')]
    ppermute x0 -> x37, starting transfers between devices: none -> 48.4 us  [the longest x28 38.8 us: row_swap(): return lax.ppermute(x, 'row', [(i, i ^ mask) for i in range(owners)])]
    gather x9 -> x0, local copies, waits for them, and re-layouts: 41.7 us -> none  [the longest x3 13.9 us: local(): jnp.log(row_totals.astype(jnp.float32)).astype(jnp.bfloat16)[wanted]]
    pallas_call x0 -> x16, Pallas kernels: none -> 34.1 us  [kernel_call(): pl.pallas_call(body, out_shape=outs, compiler_params=pltpu.CompilerParams...]
    all_to_all x3 -> x0, waiting for transfers between devices: 28.5 us -> none  [the longest x1 25 us: local(): lax.all_to_all(row_partial, 'row', split_axis=2, concat_axis=2, tiled=True)]
    scatter-add x3 -> x0, other arithmetic: 25.3 us -> none  [the longest x2 12.8 us: local(): col_accum = col_accum.at[col_local[step]].add(col_term)]
    all_to_all x3 -> x0, starting transfers between devices: 20.3 us -> none  [the longest x1 7.36 us: local(): lax.all_to_all(log_rows, 'row', split_axis=2, concat_axis=2, tiled=True)]
    dot_general x6 -> x0, matrix products: 15.7 us -> none  [the longest x2 9.64 us: local(): lax.dot_general(step_rows, columns, (((1,), (1,)), ((), ())), preferred_e...]
  transfers between devices with their start and end apart: 5 -> 37, of which waited for: 4 -> 9; matrix products, arithmetic and copies ran while one was open for 23% -> 1% of each run, Pallas kernels for 0% -> 19%
where the time goes in v1:
time: 111 us; the launch traced here: 110 us
  starting transfers between devices  48.4 us (44%)
  Pallas kernels  34.1 us (31%)
  waiting for transfers between devices  14 us (13%)
  local copies, waits for them, and re-layouts  12.6 us (11%)
    ppermute x28, starting transfers between devices, row_swap(): return lax.ppermute(x, 'row', [(i, i ^ mask) for i in range(owners)])  38.8 us
    pallas_call x16, Pallas kernels, kernel_call(): pl.pallas_call(body, out_shape=outs, compiler_params=pltpu.CompilerParams...  34.1 us
    unnamed x17, local copies, waits for them, and re-layouts  12.6 us
    ppermute x28, waiting for transfers between devices, row_swap(): return lax.ppermute(x, 'row', [(i, i ^ mask) for i in range(owners)])  7.86 us
    ppermute x7, starting transfers between devices, col_swap(): return lax.ppermute(x, 'col', [(i, i ^ mask) for i in range(cols_n)])  7.38 us
    ppermute x7, waiting for transfers between devices, col_swap(): return lax.ppermute(x, 'col', [(i, i ^ mask) for i in range(cols_n)])  5.31 us
    ppermute x2, starting transfers between devices, diag_swap(): return lax.ppermute(x, ('row', 'col'), perm)  2.26 us
  transfers between devices with their start and end apart: 37, of which 9 were waited for; matrix products, arithmetic and copies ran while one was open for 1% of the time, Pallas kernels for 19%

profile of v1, /device:TPU:0, one launch (start us, length us, event | category | flops | bytes accessed | tf_op | source)
XLA Modules:
  0.0 109.9 jit_solution(4997692770481519258)
XLA Ops:
  0.7 0.5 collective-permute-start
  1.2 0.9 copy.11
  2.2 0.8 collective-permute-done.1.tot_oth_ref
  2.9 1.0 copy-done.3
  4.0 0.7 copy-done.6
  4.7 2.8 %shard_map.86 = (bf16[272,256]{1,0:T(8,128)(2,1)S(1)}, bf16[272,256]{1,0:T(8,128)(2,1)S(1)}, bf16[272,256]{1,0:T(8,128)(2,1)S(1)}, bf16[272,256]{1,0:T(8,128)(2,...) custom-call(s32[2,128,128]{2,1,0:T(8,128)S(1)} %bitcast.6, ...), custom_call_target="tpu_custom_call" | custom-call | flops 1073741824 | bytes 4194304 | tf_op jit(solution)/shard_map/pallas_call | solution.py:51
  7.5 4.0 %collective-permute-start.11 = (bf16[272,128]{1,0:T(8,128)(2,1)S(1)}, bf16[272,128]{1,0:T(8,128)(2,1)S(1)}, u32[]{:S(2)}, u32[]{:S(2)}) collective-permute-start(bf16[272,128]{1,0:T(8,128)(2,1)S(1)} %get-tuple-element.56), channel_id=1, source_target_pairs={{0,16},{2,18},{4,20},{6,22},{8,24},{10,26},{12,28},{14,30},{16,0},... | collective-permute-start | bytes 208904 | tf_op jit(solution)/shard_map/ppermute | solution.py:461
  11.5 1.3 %collective-permute-start.12 = (bf16[272,128]{1,0:T(8,128)(2,1)S(1)}, bf16[272,128]{1,0:T(8,128)(2,1)S(1)}, u32[]{:S(2)}, u32[]{:S(2)}) collective-permute-start(bf16[272,128]{1,0:T(8,128)(2,1)S(1)} %get-tuple-element.57), channel_id=1, source_target_pairs={{0,20},{2,22},{4,16},{6,18},{8,28},{10,30},{12,24},{14,26},{16,4},... | collective-permute-start | bytes 208904 | tf_op jit(solution)/shard_map/ppermute | solution.py:461
  12.8 3.6 %collective-permute-start.13 = (bf16[272,128]{1,0:T(8,128)(2,1)S(1)}, bf16[272,128]{1,0:T(8,128)(2,1)S(1)}, u32[]{:S(2)}, u32[]{:S(2)}) collective-permute-start(bf16[272,128]{1,0:T(8,128)(2,1)S(1)} %get-tuple-element.58), channel_id=1, source_target_pairs={{0,24},{2,26},{4,28},{6,30},{8,16},{10,18},{12,20},{14,22},{16,8},... | collective-permute-start | bytes 208904 | tf_op jit(solution)/shard_map/ppermute | solution.py:461
  16.4 3.4 %copy-done.2 = s32[2,1024,1024]{2,1,0:T(8,128)S(1)} copy-done((s32[2,1024,1024]{2,1,0:T(8,128)S(1)}, s32[2,1024,1024]{2,1,0:T(8,128)}, u32[]{:S(2)}) %copy-start.2) | copy-done | bytes 8388632
  19.7 8.3 %shard_map.88 = (f32[2,1024,1024]{2,1,0:T(8,128)S(1)}, f32[2,1024,1024]{2,1,0:T(8,128)S(1)}) custom-call(s32[2,1024,1024]{2,1,0:T(8,128)S(1)} %copy-done.2), custom_call_target="tpu_custom_call" | custom-call | flops 83886080 | bytes 25165824 | tf_op jit(solution)/shard_map/pallas_call | solution.py:51
  28.1 3.3 %copy-done = f32[2,1024,1024]{2,1,0:T(8,128)} copy-done((f32[2,1024,1024]{2,1,0:T(8,128)}, f32[2,1024,1024]{2,1,0:T(8,128)S(1)}, u32[]{:S(2)}) %copy-start) | copy-done | bytes 8388632
  31.4 3.3 %copy-done.1 = f32[2,1024,1024]{2,1,0:T(8,128)} copy-done((f32[2,1024,1024]{2,1,0:T(8,128)}, f32[2,1024,1024]{2,1,0:T(8,128)S(1)}, u32[]{:S(2)}) %copy-start.1) | copy-done | bytes 8388632
  34.7 1.7 %collective-permute-start.15 = (bf16[272,128]{1,0:T(8,128)(2,1)S(1)}, bf16[272,128]{1,0:T(8,128)(2,1)S(1)}, u32[]{:S(2)}, u32[]{:S(2)}) collective-permute-start(bf16[272,128]{1,0:T(8,128)(2,1)S(1)} %collective-permute-done.11.refs_0_), channel_id=1, source_target_pairs={{0,1},{1,0},{2,3},{3,2},{4,5},{5,4},{6,7},{7,6},{8,9},{9,8},{10,11... | collective-permute-start | bytes 208904 | tf_op jit(solution)/shard_map/ppermute | solution.py:464
  36.7 1.7 %collective-permute-start.17 = (bf16[272,128]{1,0:T(8,128)(2,1)S(1)}, bf16[272,128]{1,0:T(8,128)(2,1)S(1)}, u32[]{:S(2)}, u32[]{:S(2)}) collective-permute-start(bf16[272,128]{1,0:T(8,128)(2,1)S(1)} %collective-permute-done.13.refs_2_), channel_id=1, source_target_pairs={{0,1},{1,0},{2,3},{3,2},{4,5},{5,4},{6,7},{7,6},{8,9},{9,8},{10,11... | collective-permute-start | bytes 208904 | tf_op jit(solution)/shard_map/ppermute | solution.py:464
  38.7 2.6 %shard_map.87 = (bf16[2,1024,256]{2,1,0:T(8,128)(2,1)S(1)}, f32[8,1024]{1,0:T(8,128)S(1)}) custom-call(s32[2,1024]{1,0:T(2,128)S(1)} %copy-done.5, bf16[1024,256]{1,0:T(8,128)(2,1)S(1)} %copy-done.4, s32[1,1024]{1,0:T(1,128)S(1)} %bitcast.10), custom_call_target="tpu_custom_call" | custom-call | flops 1073741824 | bytes 2097152 | tf_op jit(solution)/shard_map/pallas_call | solution.py:51
  41.4 1.7 %collective-permute-start.2 = (bf16[272,256]{1,0:T(8,128)(2,1)S(1)}, bf16[272,256]{1,0:T(8,128)(2,1)S(1)}, u32[]{:S(2)}, u32[]{:S(2)}) collective-permute-start(bf16[272,256]{1,0:T(8,128)(2,1)S(1)} %get-tuple-element.41), channel_id=1, source_target_pairs={{0,4},{2,6},{4,0},{6,2},{8,12},{10,14},{12,8},{14,10},{16,20},{18,... | collective-permute-start | bytes 417800 | tf_op jit(solution)/shard_map/ppermute | solution.py:461
  43.1 1.8 %collective-permute-start.4 = (bf16[272,256]{1,0:T(8,128)(2,1)S(1)}, bf16[272,256]{1,0:T(8,128)(2,1)S(1)}, u32[]{:S(2)}, u32[]{:S(2)}) collective-permute-start(bf16[272,256]{1,0:T(8,128)(2,1)S(1)} %get-tuple-element.43), channel_id=1, source_target_pairs={{0,12},{2,14},{4,8},{6,10},{8,4},{10,6},{12,0},{14,2},{16,28},{18,... | collective-permute-start | bytes 417800 | tf_op jit(solution)/shard_map/ppermute | solution.py:461
  45.0 6.7 %shard_map.91 = (f32[2,4,64,128]{3,2,1,0:T(8,128)S(1)}, bf16[2,4,64,128]{3,2,1,0:T(8,128)(2,1)S(1)}, bf16[2,4,64,128]{3,2,1,0:T(8,128)(2,1)S(1)}, bf16[2,4,64,128]{3,2,1,0:T(8,128)(2,1)S(1)}, f32[2,1024,256]{2,1,0:T(8,128)S(1)}) custom-call(bf16[272,128]{1,0:T(8,128)(2,1)S(1)} %collective-permute-done.11.refs_0_, ...), custom_call_target="tpu_custom_call" | custom-call | flops 1610612736 | bytes 10485760 | tf_op jit(solution)/shard_map/pallas_call | solution.py:51
  51.7 6.9 %shard_map.89 = (f32[2,4,64,128]{3,2,1,0:T(8,128)S(1)}, bf16[2,4,64,128]{3,2,1,0:T(8,128)(2,1)S(1)}, bf16[2,4,64,128]{3,2,1,0:T(8,128)(2,1)S(1)}, bf16[2,4,64,128]{3,2,1,0:T(8,128)(2,1)S(1)}, f32[2,1024,256]{2,1,0:T(8,128)S(1)}) custom-call(bf16[272,256]{1,0:T(8,128)(2,1)S(1)} %get-tuple-element.40.refs_0_, ...), custom_call_target="tpu_custom_call" | custom-call | flops 1610612736 | bytes 10485760 | tf_op jit(solution)/shard_map/pallas_call | solution.py:51
  58.5 2.7 %shard_map.95 = (f32[512,256]{1,0:T(8,128)S(1)}, f32[512,256]{1,0:T(8,128)S(1)}) custom-call(s32[2,1024]{1,0:T(2,128)S(1)} %copy-done.5, f32[2,1024,256]{2,1,0:T(8,128)S(1)} %get-tuple-element.68.near_ref, f32[2,1024,256]{2,1,0:T(8,128)S(1)} %get-tuple-element.69.far_ref), custom_call_target="tpu_custom_call" | custom-call | flops 2147483648 | bytes 5242880 | tf_op jit(solution)/shard_map/pallas_call | solution.py:51
  61.3 1.8 %collective-permute-start.5 = (bf16[2,4,64,128]{3,2,1,0:T(8,128)(2,1)S(1)}, bf16[2,4,64,128]{3,2,1,0:T(8,128)(2,1)S(1)}, u32[]{:S(2)}, u32[]{:S(2)}) collective-permute-start(bf16[2,4,64,128]{3,2,1,0:T(8,128)(2,1)S(1)} %get-tuple-element.49), channel_id=1, source_target_pairs={{0,1},{1,0},{2,3},{3,2},{4,5},{5,4},{6,7},{7,6},{8,9},{9,8},{10,11... | collective-permute-start | bytes 393224 | tf_op jit(solution)/shard_map/ppermute | solution.py:464
  63.3 1.7 %collective-permute-start.28 = (bf16[256,256]{1,0:T(8,128)(2,1)S(1)}, bf16[256,256]{1,0:T(8,128)(2,1)S(1)}, u32[]{:S(2)}, u32[]{:S(2)}) collective-permute-start(bf16[256,256]{1,0:T(8,128)(2,1)S(1)} %get-tuple-element.73), channel_id=1, source_target_pairs={{0,4},{2,6},{4,0},{6,2},{8,12},{10,14},{12,8},{14,10},{16,20},{18,... | collective-permute-start | bytes 393224 | tf_op jit(solution)/shard_map/ppermute | solution.py:461
  65.1 1.6 %collective-permute-start.7 = (bf16[2,4,64,128]{3,2,1,0:T(8,128)(2,1)S(1)}, bf16[2,4,64,128]{3,2,1,0:T(8,128)(2,1)S(1)}, u32[]{:S(2)}, u32[]{:S(2)}) collective-permute-start(bf16[2,4,64,128]{3,2,1,0:T(8,128)(2,1)S(1)} %get-tuple-element.51), channel_id=1, source_target_pairs={{0,3},{1,2},{2,1},{3,0},{4,7},{5,6},{6,5},{7,4},{8,11},{9,10},{10,... | collective-permute-start | bytes 393224 | tf_op jit(solution)/shard_map/ppermute | solution.py:470
  67.2 1.7 %collective-permute-done.28.refs_1_ = bf16[256,256]{1,0:T(8,128)(2,1)S(1)} collective-permute-done((bf16[256,256]{1,0:T(8,128)(2,1)S(1)}, bf16[256,256]{1,0:T(8,128)(2,1)S(1)}, u32[]{:S(2)}, u32[]{:S(2)}) %collective-permute-start.28) | collective-permute-done | bytes 131104 | tf_op jit(solution)/shard_map/ppermute | solution.py:461
  68.9 0.6 collective-permute-start.21
  69.7 0.8 collective-permute-done.7.diag_ref
  70.5 3.3 %collective-permute-start.30 = (bf16[64,256]{1,0:T(8,128)(2,1)S(1)}, bf16[64,256]{1,0:T(8,128)(2,1)S(1)}, u32[]{:S(2)}, u32[]{:S(2)}) collective-permute-start(bf16[64,256]{1,0:T(8,128)(2,1)S(1)} %get-tuple-element.76), channel_id=1, source_target_pairs={{0,16},{2,18},{4,20},{6,22},{8,24},{10,26},{12,28},{14,30},{16,0},... | collective-permute-start | bytes 98312 | tf_op jit(solution)/shard_map/ppermute | solution.py:461
  73.8 3.5 %collective-permute-start.31 = (bf16[64,256]{1,0:T(8,128)(2,1)S(1)}, bf16[64,256]{1,0:T(8,128)(2,1)S(1)}, u32[]{:S(2)}, u32[]{:S(2)}) collective-permute-start(bf16[64,256]{1,0:T(8,128)(2,1)S(1)} %get-tuple-element.77), channel_id=1, source_target_pairs={{0,24},{2,26},{4,28},{6,30},{8,16},{10,18},{12,20},{14,22},{16,8},... | collective-permute-start | bytes 98312 | tf_op jit(solution)/shard_map/ppermute | solution.py:461
  77.4 1.6 %collective-permute-start.8 = (bf16[2,2,64,128]{3,2,1,0:T(8,128)(2,1)S(1)}, bf16[2,2,64,128]{3,2,1,0:T(8,128)(2,1)S(1)}, u32[]{:S(2)}, u32[]{:S(2)}) collective-permute-start(bf16[2,2,64,128]{3,2,1,0:T(8,128)(2,1)S(1)} %get-tuple-element.53), channel_id=1, source_target_pairs={{0,4},{2,6},{4,0},{6,2},{8,12},{10,14},{12,8},{14,10},{16,20},{18,... | collective-permute-start | bytes 196616 | tf_op jit(solution)/shard_map/ppermute | solution.py:461
  78.9 0.6 collective-permute-done.31.refs_3_
  79.6 2.1 %collective-permute-start.32 = (bf16[64,256]{1,0:T(8,128)(2,1)S(1)}, bf16[64,256]{1,0:T(8,128)(2,1)S(1)}, u32[]{:S(2)}, u32[]{:S(2)}) collective-permute-start(bf16[64,256]{1,0:T(8,128)(2,1)S(1)} %shard_map.98.refs_0_), channel_id=1, source_target_pairs={{0,8},{2,10},{4,12},{6,14},{8,0},{10,2},{12,4},{14,6},{16,24},{18,... | collective-permute-start | bytes 98312 | tf_op jit(solution)/shard_map/ppermute | solution.py:461
  81.7 2.1 %collective-permute-start.33 = (bf16[64,256]{1,0:T(8,128)(2,1)S(1)}, bf16[64,256]{1,0:T(8,128)(2,1)S(1)}, u32[]{:S(2)}, u32[]{:S(2)}) collective-permute-start(bf16[64,256]{1,0:T(8,128)(2,1)S(1)} %shard_map.98.refs_0_), channel_id=1, source_target_pairs={{0,16},{2,18},{4,20},{6,22},{8,24},{10,26},{12,28},{14,30},{16,0},... | collective-permute-start | bytes 98312 | tf_op jit(solution)/shard_map/ppermute | solution.py:461
  83.8 1.4 %collective-permute-start.34 = (bf16[64,256]{1,0:T(8,128)(2,1)S(1)}, bf16[64,256]{1,0:T(8,128)(2,1)S(1)}, u32[]{:S(2)}, u32[]{:S(2)}) collective-permute-start(bf16[64,256]{1,0:T(8,128)(2,1)S(1)} %shard_map.98.refs_0_), channel_id=1, source_target_pairs={{0,24},{2,26},{4,28},{6,30},{8,16},{10,18},{12,20},{14,22},{16,8},... | collective-permute-start | bytes 98312 | tf_op jit(solution)/shard_map/ppermute | solution.py:461
  85.2 1.5 %collective-permute-start.10 = (bf16[2,2,64,128]{3,2,1,0:T(8,128)(2,1)S(1)}, bf16[2,2,64,128]{3,2,1,0:T(8,128)(2,1)S(1)}, u32[]{:S(2)}, u32[]{:S(2)}) collective-permute-start(bf16[2,2,64,128]{3,2,1,0:T(8,128)(2,1)S(1)} %get-tuple-element.55), channel_id=1, source_target_pairs={{0,12},{2,14},{4,8},{6,10},{8,4},{10,6},{12,0},{14,2},{16,28},{18,... | collective-permute-start | bytes 196616 | tf_op jit(solution)/shard_map/ppermute | solution.py:461
  86.8 2.4 %collective-permute-start.22 = (bf16[2,2,64,128]{3,2,1,0:T(8,128)(2,1)S(1)}, bf16[2,2,64,128]{3,2,1,0:T(8,128)(2,1)S(1)}, u32[]{:S(2)}, u32[]{:S(2)}) collective-permute-start(bf16[2,2,64,128]{3,2,1,0:T(8,128)(2,1)S(1)} %get-tuple-element.64), channel_id=1, source_target_pairs={{0,16},{2,18},{4,20},{6,22},{8,24},{10,26},{12,28},{14,30},{16,0},... | collective-permute-start | bytes 196616 | tf_op jit(solution)/shard_map/ppermute | solution.py:461
  89.2 0.5 collective-permute-start.23
  89.7 2.9 %collective-permute-start.24 = (bf16[2,2,64,128]{3,2,1,0:T(8,128)(2,1)S(1)}, bf16[2,2,64,128]{3,2,1,0:T(8,128)(2,1)S(1)}, u32[]{:S(2)}, u32[]{:S(2)}) collective-permute-start(bf16[2,2,64,128]{3,2,1,0:T(8,128)(2,1)S(1)} %get-tuple-element.66), channel_id=1, source_target_pairs={{0,24},{2,26},{4,28},{6,30},{8,16},{10,18},{12,20},{14,22},{16,8},... | collective-permute-start | bytes 196616 | tf_op jit(solution)/shard_map/ppermute | solution.py:461
  92.6 1.9 %collective-permute-start.25 = (bf16[2,2,64,128]{3,2,1,0:T(8,128)(2,1)S(1)}, bf16[2,2,64,128]{3,2,1,0:T(8,128)(2,1)S(1)}, u32[]{:S(2)}, u32[]{:S(2)}) collective-permute-start(bf16[2,2,64,128]{3,2,1,0:T(8,128)(2,1)S(1)} %get-tuple-element.67), channel_id=1, source_target_pairs={{0,28},{2,30},{4,24},{6,26},{8,20},{10,22},{12,16},{14,18},{16,12}... | collective-permute-start | bytes 196616 | tf_op jit(solution)/shard_map/ppermute | solution.py:461
  94.5 0.6 collective-permute-start.35
  95.1 1.4 %collective-permute-done.22.refs_4_ = bf16[2,2,64,128]{3,2,1,0:T(8,128)(2,1)S(1)} collective-permute-done((bf16[2,2,64,128]{3,2,1,0:T(8,128)(2,1)S(1)}, bf16[2,2,64,128]{3,2,1,0:T(8,128)(2,1)S(1)}, u32[]{:S(2)}, u32[]{:S(2)}) %collective-permute-start.22) | collective-permute-done | bytes 65568 | tf_op jit(solution)/shard_map/ppermute | solution.py:461
  96.5 1.6 %collective-permute-done.23.refs_5_ = bf16[2,2,64,128]{3,2,1,0:T(8,128)(2,1)S(1)} collective-permute-done((bf16[2,2,64,128]{3,2,1,0:T(8,128)(2,1)S(1)}, bf16[2,2,64,128]{3,2,1,0:T(8,128)(2,1)S(1)}, u32[]{:S(2)}, u32[]{:S(2)}) %collective-permute-start.23) | collective-permute-done | bytes 65568 | tf_op jit(solution)/shard_map/ppermute | solution.py:461
  98.1 1.6 %collective-permute-done.25.refs_7_ = bf16[2,2,64,128]{3,2,1,0:T(8,128)(2,1)S(1)} collective-permute-done((bf16[2,2,64,128]{3,2,1,0:T(8,128)(2,1)S(1)}, bf16[2,2,64,128]{3,2,1,0:T(8,128)(2,1)S(1)}, u32[]{:S(2)}, u32[]{:S(2)}) %collective-permute-start.25) | collective-permute-done | bytes 65568 | tf_op jit(solution)/shard_map/ppermute | solution.py:461
  99.7 1.6 %shard_map.93.own_ref = bf16[1024,128]{1,0:T(8,128)(2,1)S(1)} custom-call(s32[2,128,128]{2,1,0:T(8,128)S(1)} %bitcast.7, bf16[2,2,64,128]{3,2,1,0:T(8,128)(2,1)S(1)} %get-tuple-element.52.refs_0_, bf16[2,2,64,128]{3,2,1,0:T(8,128)(2,1)S(1)} %collective-permute-done.8.refs_1_, bf16[2,2,64,128]{3,2,1,0:T(8,128)(2,1)S(1)} %collective-permute-done.9.refs_2_, ...), custom_call_target="tpu_custom_call" | custom-call | flops 1073741824 | bytes 2097152 | tf_op jit(solution)/shard_map/pallas_call | solution.py:51
  101.3 1.0 collective-permute-start.26
  102.5 5.3 %collective-permute-done.26.oth_ref = bf16[1024,128]{1,0:T(8,128)(2,1)S(1)} collective-permute-done((bf16[1024,128]{1,0:T(8,128)(2,1)S(1)}, bf16[1024,128]{1,0:T(8,128)(2,1)S(1)}, u32[]{:S(2)}, u32[]{:S(2)}) %collective-permute-start.26) | collective-permute-done | bytes 262176 | tf_op jit(solution)/shard_map/ppermute | solution.py:464
  107.7 1.1 %shard_map.94 = f32[1024,256]{1,0:T(8,128)} custom-call(bf16[1024,128]{1,0:T(8,128)(2,1)S(1)} %shard_map.93.own_ref, bf16[1024,128]{1,0:T(8,128)(2,1)S(1)} %collective-permute-done.26.oth_ref), custom_call_target="tpu_custom_call" | custom-call | flops 1048576 | bytes 2097152 | tf_op jit(solution)/shard_map/pallas_call | solution.py:51
  108.8 1.1 shard_map.101
  (59 shorter events, 2.1 us)
Async XLA Ops:
  0.6 38.1 %copy-start.5 = (s32[2,1024]{1,0:T(2,128)S(1)}, s32[2,1024]{1,0:T(2,128)}, u32[]{:S(2)}) copy-start(s32[2,1024]{1,0:T(2,128)} %ids_ref.3) | copy-start | bytes 24580
  0.6 38.1 %copy-start.7 = (s32[1024]{0:T(1024)S(1)}, s32[1024]{0:T(1024)}, u32[]{:S(2)}) copy-start(s32[1024]{0:T(1024)} %param.11) | copy-start | bytes 12292
  0.7 2.3 %collective-permute-start = (bf16[1024,256]{1,0:T(8,128)(2,1)}, bf16[1024,256]{1,0:T(8,128)(2,1)S(1)}, u32[]{:S(2)}, u32[]{:S(2)}) collective-permute-start(bf16[1024,256]{1,0:T(8,128)(2,1)} %own_ref.1), channel_id=1, source_target_pairs={{0,2},{2,0},{4,6},{6,4},{8,10},{10,8},{12,14},{14,12},{16,18},{18,... | collective-permute-start | bytes 1572872 | tf_op jit(solution)/shard_map/ppermute | solution.py:461
  1.2 1.8 %collective-permute-start.1 = (s32[1,1024]{1,0:T(1,128)}, s32[1,1024]{1,0:T(1,128)S(1)}, u32[]{:S(2)}, u32[]{:S(2)}) collective-permute-start(s32[1,1024]{1,0:T(1,128)} %bitcast.8), channel_id=1, source_target_pairs={{0,2},{2,0},{4,6},{6,4},{8,10},{10,8},{12,14},{14,12},{16,18},{18,... | collective-permute-start | bytes 12296 | tf_op jit(solution)/shard_map/ppermute | solution.py:461
  2.9 1.0 copy-start.3
  4.0 0.7 copy-start.6
  4.7 34.1 %copy-start.4 = (bf16[1024,256]{1,0:T(8,128)(2,1)S(1)}, bf16[1024,256]{1,0:T(8,128)(2,1)}, u32[]{:S(2)}) copy-start(bf16[1024,256]{1,0:T(8,128)(2,1)} %emb_ref.1) | copy-start | bytes 1572868
  7.5 27.2 %collective-permute-start.11 = (bf16[272,128]{1,0:T(8,128)(2,1)S(1)}, bf16[272,128]{1,0:T(8,128)(2,1)S(1)}, u32[]{:S(2)}, u32[]{:S(2)}) collective-permute-start(bf16[272,128]{1,0:T(8,128)(2,1)S(1)} %get-tuple-element.56), channel_id=1, source_target_pairs={{0,16},{2,18},{4,20},{6,22},{8,24},{10,26},{12,28},{14,30},{16,0},... | collective-permute-start | bytes 208904 | tf_op jit(solution)/shard_map/ppermute | solution.py:461
  11.5 24.9 %collective-permute-start.12 = (bf16[272,128]{1,0:T(8,128)(2,1)S(1)}, bf16[272,128]{1,0:T(8,128)(2,1)S(1)}, u32[]{:S(2)}, u32[]{:S(2)}) collective-permute-start(bf16[272,128]{1,0:T(8,128)(2,1)S(1)} %get-tuple-element.57), channel_id=1, source_target_pairs={{0,20},{2,22},{4,16},{6,18},{8,28},{10,30},{12,24},{14,26},{16,4},... | collective-permute-start | bytes 208904 | tf_op jit(solution)/shard_map/ppermute | solution.py:461
  12.8 24.0 %collective-permute-start.13 = (bf16[272,128]{1,0:T(8,128)(2,1)S(1)}, bf16[272,128]{1,0:T(8,128)(2,1)S(1)}, u32[]{:S(2)}, u32[]{:S(2)}) collective-permute-start(bf16[272,128]{1,0:T(8,128)(2,1)S(1)} %get-tuple-element.58), channel_id=1, source_target_pairs={{0,24},{2,26},{4,28},{6,30},{8,16},{10,18},{12,20},{14,22},{16,8},... | collective-permute-start | bytes 208904 | tf_op jit(solution)/shard_map/ppermute | solution.py:461
  16.4 22.1 %collective-permute-start.14 = (bf16[272,128]{1,0:T(8,128)(2,1)S(1)}, bf16[272,128]{1,0:T(8,128)(2,1)S(1)}, u32[]{:S(2)}, u32[]{:S(2)}) collective-permute-start(bf16[272,128]{1,0:T(8,128)(2,1)S(1)} %get-tuple-element.59), channel_id=1, source_target_pairs={{0,28},{2,30},{4,24},{6,26},{8,20},{10,22},{12,16},{14,18},{16,12}... | collective-permute-start | bytes 208904 | tf_op jit(solution)/shard_map/ppermute | solution.py:461
  16.4 3.4 %copy-start.2 = (s32[2,1024,1024]{2,1,0:T(8,128)S(1)}, s32[2,1024,1024]{2,1,0:T(8,128)}, u32[]{:S(2)}) copy-start(s32[2,1024,1024]{2,1,0:T(8,128)} %counts_ref.1) | copy-start | bytes 25165828
  28.1 3.3 %copy-start = (f32[2,1024,1024]{2,1,0:T(8,128)}, f32[2,1024,1024]{2,1,0:T(8,128)S(1)}, u32[]{:S(2)}) copy-start(f32[2,1024,1024]{2,1,0:T(8,128)S(1)} %get-tuple-element.46.refs_6_.refs_10_) | copy-start | bytes 25165828
  31.4 3.3 %copy-start.1 = (f32[2,1024,1024]{2,1,0:T(8,128)}, f32[2,1024,1024]{2,1,0:T(8,128)S(1)}, u32[]{:S(2)}) copy-start(f32[2,1024,1024]{2,1,0:T(8,128)S(1)} %get-tuple-element.47.refs_7_.refs_11_) | copy-start | bytes 25165828
  34.7 8.5 %collective-permute-start.15 = (bf16[272,128]{1,0:T(8,128)(2,1)S(1)}, bf16[272,128]{1,0:T(8,128)(2,1)S(1)}, u32[]{:S(2)}, u32[]{:S(2)}) collective-permute-start(bf16[272,128]{1,0:T(8,128)(2,1)S(1)} %collective-permute-done.11.refs_0_), channel_id=1, source_target_pairs={{0,1},{1,0},{2,3},{3,2},{4,5},{5,4},{6,7},{7,6},{8,9},{9,8},{10,11... | collective-permute-start | bytes 208904 | tf_op jit(solution)/shard_map/ppermute | solution.py:464
  36.4 6.7 %collective-permute-start.16 = (bf16[272,128]{1,0:T(8,128)(2,1)S(1)}, bf16[272,128]{1,0:T(8,128)(2,1)S(1)}, u32[]{:S(2)}, u32[]{:S(2)}) collective-permute-start(bf16[272,128]{1,0:T(8,128)(2,1)S(1)} %collective-permute-done.12.refs_1_), channel_id=1, source_target_pairs={{0,1},{1,0},{2,3},{3,2},{4,5},{5,4},{6,7},{7,6},{8,9},{9,8},{10,11... | collective-permute-start | bytes 208904 | tf_op jit(solution)/shard_map/ppermute | solution.py:464
  36.7 8.2 %collective-permute-start.17 = (bf16[272,128]{1,0:T(8,128)(2,1)S(1)}, bf16[272,128]{1,0:T(8,128)(2,1)S(1)}, u32[]{:S(2)}, u32[]{:S(2)}) collective-permute-start(bf16[272,128]{1,0:T(8,128)(2,1)S(1)} %collective-permute-done.13.refs_2_), channel_id=1, source_target_pairs={{0,1},{1,0},{2,3},{3,2},{4,5},{5,4},{6,7},{7,6},{8,9},{9,8},{10,11... | collective-permute-start | bytes 208904 | tf_op jit(solution)/shard_map/ppermute | solution.py:464
  38.4 6.5 %collective-permute-start.18 = (bf16[272,128]{1,0:T(8,128)(2,1)S(1)}, bf16[272,128]{1,0:T(8,128)(2,1)S(1)}, u32[]{:S(2)}, u32[]{:S(2)}) collective-permute-start(bf16[272,128]{1,0:T(8,128)(2,1)S(1)} %collective-permute-done.14.refs_3_), channel_id=1, source_target_pairs={{0,1},{1,0},{2,3},{3,2},{4,5},{5,4},{6,7},{7,6},{8,9},{9,8},{10,11... | collective-permute-start | bytes 208904 | tf_op jit(solution)/shard_map/ppermute | solution.py:464
  41.4 10.2 %collective-permute-start.2 = (bf16[272,256]{1,0:T(8,128)(2,1)S(1)}, bf16[272,256]{1,0:T(8,128)(2,1)S(1)}, u32[]{:S(2)}, u32[]{:S(2)}) collective-permute-start(bf16[272,256]{1,0:T(8,128)(2,1)S(1)} %get-tuple-element.41), channel_id=1, source_target_pairs={{0,4},{2,6},{4,0},{6,2},{8,12},{10,14},{12,8},{14,10},{16,20},{18,... | collective-permute-start | bytes 417800 | tf_op jit(solution)/shard_map/ppermute | solution.py:461
  43.1 8.5 %collective-permute-start.3 = (bf16[272,256]{1,0:T(8,128)(2,1)S(1)}, bf16[272,256]{1,0:T(8,128)(2,1)S(1)}, u32[]{:S(2)}, u32[]{:S(2)}) collective-permute-start(bf16[272,256]{1,0:T(8,128)(2,1)S(1)} %get-tuple-element.42), channel_id=1, source_target_pairs={{0,8},{2,10},{4,12},{6,14},{8,0},{10,2},{12,4},{14,6},{16,24},{18,... | collective-permute-start | bytes 417800 | tf_op jit(solution)/shard_map/ppermute | solution.py:461
  43.1 8.5 %collective-permute-start.4 = (bf16[272,256]{1,0:T(8,128)(2,1)S(1)}, bf16[272,256]{1,0:T(8,128)(2,1)S(1)}, u32[]{:S(2)}, u32[]{:S(2)}) collective-permute-start(bf16[272,256]{1,0:T(8,128)(2,1)S(1)} %get-tuple-element.43), channel_id=1, source_target_pairs={{0,12},{2,14},{4,8},{6,10},{8,4},{10,6},{12,0},{14,2},{16,28},{18,... | collective-permute-start | bytes 417800 | tf_op jit(solution)/shard_map/ppermute | solution.py:461
  61.2 2.0 %collective-permute-start.27 = (f32[512,256]{1,0:T(8,128)S(1)}, f32[512,256]{1,0:T(8,128)S(1)}, u32[]{:S(2)}, u32[]{:S(2)}) collective-permute-start(f32[512,256]{1,0:T(8,128)S(1)} %get-tuple-element.71), channel_id=1, source_target_pairs={{0,2},{2,0},{4,6},{6,4},{8,10},{10,8},{12,14},{14,12},{16,18},{18,... | collective-permute-start | bytes 1572872 | tf_op jit(solution)/shard_map/ppermute | solution.py:461
  61.3 5.9 %collective-permute-start.5 = (bf16[2,4,64,128]{3,2,1,0:T(8,128)(2,1)S(1)}, bf16[2,4,64,128]{3,2,1,0:T(8,128)(2,1)S(1)}, u32[]{:S(2)}, u32[]{:S(2)}) collective-permute-start(bf16[2,4,64,128]{3,2,1,0:T(8,128)(2,1)S(1)} %get-tuple-element.49), channel_id=1, source_target_pairs={{0,1},{1,0},{2,3},{3,2},{4,5},{5,4},{6,7},{7,6},{8,9},{9,8},{10,11... | collective-permute-start | bytes 393224 | tf_op jit(solution)/shard_map/ppermute | solution.py:464
  63.3 5.6 %collective-permute-start.28 = (bf16[256,256]{1,0:T(8,128)(2,1)S(1)}, bf16[256,256]{1,0:T(8,128)(2,1)S(1)}, u32[]{:S(2)}, u32[]{:S(2)}) collective-permute-start(bf16[256,256]{1,0:T(8,128)(2,1)S(1)} %get-tuple-element.73), channel_id=1, source_target_pairs={{0,4},{2,6},{4,0},{6,2},{8,12},{10,14},{12,8},{14,10},{16,20},{18,... | collective-permute-start | bytes 393224 | tf_op jit(solution)/shard_map/ppermute | solution.py:461
  65.1 4.5 %collective-permute-start.6 = (bf16[2,4,64,128]{3,2,1,0:T(8,128)(2,1)S(1)}, bf16[2,4,64,128]{3,2,1,0:T(8,128)(2,1)S(1)}, u32[]{:S(2)}, u32[]{:S(2)}) collective-permute-start(bf16[2,4,64,128]{3,2,1,0:T(8,128)(2,1)S(1)} %get-tuple-element.50), channel_id=1, source_target_pairs={{0,2},{2,0},{4,6},{6,4},{8,10},{10,8},{12,14},{14,12},{16,18},{18,... | collective-permute-start | bytes 393224 | tf_op jit(solution)/shard_map/ppermute | solution.py:461
  65.1 5.5 %collective-permute-start.7 = (bf16[2,4,64,128]{3,2,1,0:T(8,128)(2,1)S(1)}, bf16[2,4,64,128]{3,2,1,0:T(8,128)(2,1)S(1)}, u32[]{:S(2)}, u32[]{:S(2)}) collective-permute-start(bf16[2,4,64,128]{3,2,1,0:T(8,128)(2,1)S(1)} %get-tuple-element.51), channel_id=1, source_target_pairs={{0,3},{1,2},{2,1},{3,0},{4,7},{5,6},{6,5},{7,4},{8,11},{9,10},{10,... | collective-permute-start | bytes 393224 | tf_op jit(solution)/shard_map/ppermute | solution.py:470
  66.7 12.9 %collective-permute-start.19 = (bf16[2,4,64,128]{3,2,1,0:T(8,128)(2,1)S(1)}, bf16[2,4,64,128]{3,2,1,0:T(8,128)(2,1)S(1)}, u32[]{:S(2)}, u32[]{:S(2)}) collective-permute-start(bf16[2,4,64,128]{3,2,1,0:T(8,128)(2,1)S(1)} %get-tuple-element.61), channel_id=1, source_target_pairs={{0,1},{1,0},{2,3},{3,2},{4,5},{5,4},{6,7},{7,6},{8,9},{9,8},{10,11... | collective-permute-start | bytes 393224 | tf_op jit(solution)/shard_map/ppermute | solution.py:464
  67.2 14.5 %collective-permute-start.20 = (bf16[2,4,64,128]{3,2,1,0:T(8,128)(2,1)S(1)}, bf16[2,4,64,128]{3,2,1,0:T(8,128)(2,1)S(1)}, u32[]{:S(2)}, u32[]{:S(2)}) collective-permute-start(bf16[2,4,64,128]{3,2,1,0:T(8,128)(2,1)S(1)} %get-tuple-element.62), channel_id=1, source_target_pairs={{0,2},{2,0},{4,6},{6,4},{8,10},{10,8},{12,14},{14,12},{16,18},{18,... | collective-permute-start | bytes 393224 | tf_op jit(solution)/shard_map/ppermute | solution.py:461
  68.9 14.8 %collective-permute-start.21 = (bf16[2,4,64,128]{3,2,1,0:T(8,128)(2,1)S(1)}, bf16[2,4,64,128]{3,2,1,0:T(8,128)(2,1)S(1)}, u32[]{:S(2)}, u32[]{:S(2)}) collective-permute-start(bf16[2,4,64,128]{3,2,1,0:T(8,128)(2,1)S(1)} %get-tuple-element.63), channel_id=1, source_target_pairs={{0,3},{1,2},{2,1},{3,0},{4,7},{5,6},{6,5},{7,4},{8,11},{9,10},{10,... | collective-permute-start | bytes 393224 | tf_op jit(solution)/shard_map/ppermute | solution.py:470
  69.6 4.2 %collective-permute-start.29 = (bf16[64,256]{1,0:T(8,128)(2,1)S(1)}, bf16[64,256]{1,0:T(8,128)(2,1)S(1)}, u32[]{:S(2)}, u32[]{:S(2)}) collective-permute-start(bf16[64,256]{1,0:T(8,128)(2,1)S(1)} %get-tuple-element.75), channel_id=1, source_target_pairs={{0,8},{2,10},{4,12},{6,14},{8,0},{10,2},{12,4},{14,6},{16,24},{18,... | collective-permute-start | bytes 98312 | tf_op jit(solution)/shard_map/ppermute | solution.py:461
  70.5 6.8 %collective-permute-start.30 = (bf16[64,256]{1,0:T(8,128)(2,1)S(1)}, bf16[64,256]{1,0:T(8,128)(2,1)S(1)}, u32[]{:S(2)}, u32[]{:S(2)}) collective-permute-start(bf16[64,256]{1,0:T(8,128)(2,1)S(1)} %get-tuple-element.76), channel_id=1, source_target_pairs={{0,16},{2,18},{4,20},{6,22},{8,24},{10,26},{12,28},{14,30},{16,0},... | collective-permute-start | bytes 98312 | tf_op jit(solution)/shard_map/ppermute | solution.py:461
  73.8 5.7 %collective-permute-start.31 = (bf16[64,256]{1,0:T(8,128)(2,1)S(1)}, bf16[64,256]{1,0:T(8,128)(2,1)S(1)}, u32[]{:S(2)}, u32[]{:S(2)}) collective-permute-start(bf16[64,256]{1,0:T(8,128)(2,1)S(1)} %get-tuple-element.77), channel_id=1, source_target_pairs={{0,24},{2,26},{4,28},{6,30},{8,16},{10,18},{12,20},{14,22},{16,8},... | collective-permute-start | bytes 98312 | tf_op jit(solution)/shard_map/ppermute | solution.py:461
  77.4 7.9 %collective-permute-start.8 = (bf16[2,2,64,128]{3,2,1,0:T(8,128)(2,1)S(1)}, bf16[2,2,64,128]{3,2,1,0:T(8,128)(2,1)S(1)}, u32[]{:S(2)}, u32[]{:S(2)}) collective-permute-start(bf16[2,2,64,128]{3,2,1,0:T(8,128)(2,1)S(1)} %get-tuple-element.53), channel_id=1, source_target_pairs={{0,4},{2,6},{4,0},{6,2},{8,12},{10,14},{12,8},{14,10},{16,20},{18,... | collective-permute-start | bytes 196616 | tf_op jit(solution)/shard_map/ppermute | solution.py:461
  79.6 7.2 %collective-permute-start.9 = (bf16[2,2,64,128]{3,2,1,0:T(8,128)(2,1)S(1)}, bf16[2,2,64,128]{3,2,1,0:T(8,128)(2,1)S(1)}, u32[]{:S(2)}, u32[]{:S(2)}) collective-permute-start(bf16[2,2,64,128]{3,2,1,0:T(8,128)(2,1)S(1)} %get-tuple-element.54), channel_id=1, source_target_pairs={{0,8},{2,10},{4,12},{6,14},{8,0},{10,2},{12,4},{14,6},{16,24},{18,... | collective-permute-start | bytes 196616 | tf_op jit(solution)/shard_map/ppermute | solution.py:461
  79.6 9.6 %collective-permute-start.32 = (bf16[64,256]{1,0:T(8,128)(2,1)S(1)}, bf16[64,256]{1,0:T(8,128)(2,1)S(1)}, u32[]{:S(2)}, u32[]{:S(2)}) collective-permute-start(bf16[64,256]{1,0:T(8,128)(2,1)S(1)} %shard_map.98.refs_0_), channel_id=1, source_target_pairs={{0,8},{2,10},{4,12},{6,14},{8,0},{10,2},{12,4},{14,6},{16,24},{18,... | collective-permute-start | bytes 98312 | tf_op jit(solution)/shard_map/ppermute | solution.py:461
  81.7 8.0 %collective-permute-start.33 = (bf16[64,256]{1,0:T(8,128)(2,1)S(1)}, bf16[64,256]{1,0:T(8,128)(2,1)S(1)}, u32[]{:S(2)}, u32[]{:S(2)}) collective-permute-start(bf16[64,256]{1,0:T(8,128)(2,1)S(1)} %shard_map.98.refs_0_), channel_id=1, source_target_pairs={{0,16},{2,18},{4,20},{6,22},{8,24},{10,26},{12,28},{14,30},{16,0},... | collective-permute-start | bytes 98312 | tf_op jit(solution)/shard_map/ppermute | solution.py:461
  83.8 8.8 %collective-permute-start.34 = (bf16[64,256]{1,0:T(8,128)(2,1)S(1)}, bf16[64,256]{1,0:T(8,128)(2,1)S(1)}, u32[]{:S(2)}, u32[]{:S(2)}) collective-permute-start(bf16[64,256]{1,0:T(8,128)(2,1)S(1)} %shard_map.98.refs_0_), channel_id=1, source_target_pairs={{0,24},{2,26},{4,28},{6,30},{8,16},{10,18},{12,20},{14,22},{16,8},... | collective-permute-start | bytes 98312 | tf_op jit(solution)/shard_map/ppermute | solution.py:461
  85.2 9.3 %collective-permute-start.10 = (bf16[2,2,64,128]{3,2,1,0:T(8,128)(2,1)S(1)}, bf16[2,2,64,128]{3,2,1,0:T(8,128)(2,1)S(1)}, u32[]{:S(2)}, u32[]{:S(2)}) collective-permute-start(bf16[2,2,64,128]{3,2,1,0:T(8,128)(2,1)S(1)} %get-tuple-element.55), channel_id=1, source_target_pairs={{0,12},{2,14},{4,8},{6,10},{8,4},{10,6},{12,0},{14,2},{16,28},{18,... | collective-permute-start | bytes 196616 | tf_op jit(solution)/shard_map/ppermute | solution.py:461
  86.8 9.7 %collective-permute-start.22 = (bf16[2,2,64,128]{3,2,1,0:T(8,128)(2,1)S(1)}, bf16[2,2,64,128]{3,2,1,0:T(8,128)(2,1)S(1)}, u32[]{:S(2)}, u32[]{:S(2)}) collective-permute-start(bf16[2,2,64,128]{3,2,1,0:T(8,128)(2,1)S(1)} %get-tuple-element.64), channel_id=1, source_target_pairs={{0,16},{2,18},{4,20},{6,22},{8,24},{10,26},{12,28},{14,30},{16,0},... | collective-permute-start | bytes 196616 | tf_op jit(solution)/shard_map/ppermute | solution.py:461
  89.2 8.9 %collective-permute-start.23 = (bf16[2,2,64,128]{3,2,1,0:T(8,128)(2,1)S(1)}, bf16[2,2,64,128]{3,2,1,0:T(8,128)(2,1)S(1)}, u32[]{:S(2)}, u32[]{:S(2)}) collective-permute-start(bf16[2,2,64,128]{3,2,1,0:T(8,128)(2,1)S(1)} %get-tuple-element.65), channel_id=1, source_target_pairs={{0,20},{2,22},{4,16},{6,18},{8,28},{10,30},{12,24},{14,26},{16,4},... | collective-permute-start | bytes 196616 | tf_op jit(solution)/shard_map/ppermute | solution.py:461
  89.7 8.4 %collective-permute-start.24 = (bf16[2,2,64,128]{3,2,1,0:T(8,128)(2,1)S(1)}, bf16[2,2,64,128]{3,2,1,0:T(8,128)(2,1)S(1)}, u32[]{:S(2)}, u32[]{:S(2)}) collective-permute-start(bf16[2,2,64,128]{3,2,1,0:T(8,128)(2,1)S(1)} %get-tuple-element.66), channel_id=1, source_target_pairs={{0,24},{2,26},{4,28},{6,30},{8,16},{10,18},{12,20},{14,22},{16,8},... | collective-permute-start | bytes 196616 | tf_op jit(solution)/shard_map/ppermute | solution.py:461
  92.6 7.1 %collective-permute-start.25 = (bf16[2,2,64,128]{3,2,1,0:T(8,128)(2,1)S(1)}, bf16[2,2,64,128]{3,2,1,0:T(8,128)(2,1)S(1)}, u32[]{:S(2)}, u32[]{:S(2)}) collective-permute-start(bf16[2,2,64,128]{3,2,1,0:T(8,128)(2,1)S(1)} %get-tuple-element.67), channel_id=1, source_target_pairs={{0,28},{2,30},{4,24},{6,26},{8,20},{10,22},{12,16},{14,18},{16,12}... | collective-permute-start | bytes 196616 | tf_op jit(solution)/shard_map/ppermute | solution.py:461
  94.5 7.8 %collective-permute-start.35 = (bf16[256,256]{1,0:T(8,128)(2,1)S(1)}, bf16[256,256]{1,0:T(8,128)(2,1)S(1)}, u32[]{:S(2)}, u32[]{:S(2)}) collective-permute-start(bf16[256,256]{1,0:T(8,128)(2,1)S(1)} %shard_map.99.refs_0_), channel_id=1, source_target_pairs={{0,4},{2,6},{4,0},{6,2},{8,12},{10,14},{12,8},{14,10},{16,20},{18,... | collective-permute-start | bytes 393224 | tf_op jit(solution)/shard_map/ppermute | solution.py:461
  101.3 6.4 %collective-permute-start.26 = (bf16[1024,128]{1,0:T(8,128)(2,1)S(1)}, bf16[1024,128]{1,0:T(8,128)(2,1)S(1)}, u32[]{:S(2)}, u32[]{:S(2)}) collective-permute-start(bf16[1024,128]{1,0:T(8,128)(2,1)S(1)} %shard_map.93.own_ref), channel_id=1, source_target_pairs={{0,1},{1,0},{2,3},{3,2},{4,5},{5,4},{6,7},{7,6},{8,9},{9,8},{10,11... | collective-permute-start | bytes 786440 | tf_op jit(solution)/shard_map/ppermute | solution.py:464
  102.4 6.5 %collective-permute-start.36 = (bf16[512,256]{1,0:T(8,128)(2,1)S(1)}, bf16[512,256]{1,0:T(8,128)(2,1)S(1)}, u32[]{:S(2)}, u32[]{:S(2)}) collective-permute-start(bf16[512,256]{1,0:T(8,128)(2,1)S(1)} %shard_map.100.refs_0_), channel_id=1, source_target_pairs={{0,2},{2,0},{4,6},{6,4},{8,10},{10,8},{12,14},{14,12},{16,18},{18,... | collective-permute-start | bytes 786440 | tf_op jit(solution)/shard_map/ppermute | solution.py:461

commit v2 on v0

v2 whole, which is shorter than its diff:
```python
import functools
import math

import jax
import jax.numpy as jnp
from jax import lax
from jax.experimental import pallas as pl
from jax.experimental.pallas import tpu as pltpu
from jax.sharding import PartitionSpec as P

log_total = 8.0
f32 = jnp.float32
bf16 = jnp.bfloat16
MIB = 1 << 20


def nt(a, b):
    return lax.dot_general(a, b, (((1,), (1,)), ((), ())), preferred_element_type=f32)


def tn(a, b):
    return lax.dot_general(a, b, (((0,), (0,)), ((), ())), preferred_element_type=f32)


def nn(a, b):
    return jnp.dot(a, b, preferred_element_type=f32)


def iota(shape, dim):
    return lax.broadcasted_iota(jnp.int32, shape, dim)


def ones_where(cond):
    return jnp.where(cond, 1.0, 0.0).astype(bf16)


def split_index(ids, size):
    local = ids & (size - 1)
    return (local >> 5).astype(f32).astype(bf16), (local & 31).astype(f32).astype(bf16)


def kernel_call(body, outs, *args, vmem=32, cost=None, **kw):
    return pl.pallas_call(
        body,
        out_shape=outs,
        compiler_params=pltpu.CompilerParams(vmem_limit_bytes=vmem * MIB),
        cost_estimate=cost,
        **kw,
    )(*args)


def cost(flops, nbytes):
    return pl.CostEstimate(flops=1, bytes_accessed=1, transcendentals=0)


def anywhere(items):
    return [pl.BlockSpec(memory_space=pl.ANY)] * len(items)


def in_vmem(items):
    return [pl.BlockSpec(memory_space=pltpu.VMEM)] * len(items)


class Plan:
    def __init__(self, owners, steps, block, width):
        self.owners = owners
        self.steps = steps
        self.block = block
        self.width = width
        self.chips = owners // 2
        self.groups = self.chips // 4
        self.share = block // owners
        self.pair = 2 * self.share
        self.deep = min(4, self.chips)
        self.wide = self.chips // self.deep
        self.rows = steps * self.pair


def turn(t):
    return ((t & 1) * 2) ^ ((t >> 1) * 3)


def position():
    r = lax.axis_index("row")
    half = lax.axis_index("col") % 2
    return r, half, turn(2 * (r % 2) + half)


def fetch_kernel(p, ids_ref, own_ref, oth_ref, tot_own_ref, tot_oth_ref, *msgs):
    r, half, mine = position()
    lines = p.steps * p.owners * 8
    group = 128 // p.owners
    count = 2 * len(msgs)
    hi, lo = split_index(ids_ref[...].reshape(lines, 128), p.block)
    sub = iota((p.pair, 128), 0)
    lane = iota((p.pair, 128), 1)
    owner = r ^ (sub // p.share)
    inner = sub % p.share
    pick = ones_where((lane % p.owners == owner) & (lane // p.owners == inner % group))
    sub2 = iota((p.pair, lines), 0) % p.share
    lane2 = iota((p.pair, lines), 1)
    keep = lane2 % 8 == sub2 // group
    line = iota((lines, 128), 0)
    slot = iota((lines, 128), 1)
    step_ok = line // (p.owners * 8) == slot // count
    dest = (line // 8) % p.owners
    mask = (4 * ((slot % count) // 2)) ^ mine
    route = ones_where(step_ok & (dest == (r ^ (2 * mask + slot % 2))))

    def column(digit):
        picked = jnp.where(keep, nt(pick, digit), 0.0).astype(bf16)
        return nn(picked, route)

    index = (column(hi) * 32.0 + column(lo)).astype(jnp.int32)
    logs = jnp.zeros((16, count * p.share), f32)
    log_row = iota((16, count * p.share), 0)
    items = iota((p.share, p.block), 1)
    tables = [own_ref, oth_ref]
    totals = [tot_own_ref, tot_oth_ref]
    for jj in range(2):
        table_log = jnp.log(totals[jj][...].astype(f32)).astype(bf16)
        table_log = jnp.broadcast_to(table_log, (16, p.block))
        for s in range(p.steps):
            pieces = []
            for e in range(count):
                n = s * count + e
                col = index[jj * p.share : (jj + 1) * p.share, n : n + 1]
                pieces.append(ones_where(items == col))
            onehot = jnp.concatenate(pieces, axis=0)
            rows = nn(onehot, tables[jj][...]).astype(bf16)
            logs = logs + jnp.where(log_row == s * 2 + jj, nt(table_log, onehot), 0.0)
            for e in range(count):
                at = e % 2 * p.rows + s * p.pair + jj * p.share
                msgs[e // 2][at : at + p.share, :] = rows[e * p.share : (e + 1) * p.share, :]
    for g, msg in enumerate(msgs):
        tile = (2 * g * p.share) // 128 * 128
        msg[2 * p.rows : 2 * p.rows + 16, :128] = logs[:, tile : tile + 128].astype(bf16)
        msg[2 * p.rows : 2 * p.rows + 16, 128:] = jnp.zeros((16, p.width - 128), bf16)


def fetch(p, ids, own, oth, tot_own, tot_oth):
    outs = [jax.ShapeDtypeStruct((2 * p.rows + 16, p.width), bf16)] * p.groups
    return kernel_call(
        functools.partial(fetch_kernel, p), outs, ids, own, oth, tot_own, tot_oth, vmem=12,
        cost=cost(4 * 2 * 256 * 1024 * 256, 4 * MIB),
    )


def columns_kernel(p, ids_ref, emb_ref, tot_ref, row_ids_ref, *refs):
    cols_ref, logs_ref, index_ref = refs[-3:]
    block = emb_ref.shape[0]
    table = emb_ref[...]
    local = (ids_ref[...] & (block - 1)).astype(f32)
    sub8 = iota((8, block), 0)
    stack = jnp.zeros((8, block), f32)
    for s in range(p.steps):
        stack = jnp.where(sub8 == s, jnp.broadcast_to(local[s : s + 1, :], (8, block)), stack)
    index = stack.T.astype(jnp.int32)
    logs = jnp.log(tot_ref[...].astype(f32))
    first = logs.astype(bf16).astype(f32)
    second = (logs - first).astype(bf16).astype(f32)
    third = logs - first - second
    sub16 = iota((16, block), 0)
    digits = jnp.where(sub16 == 0, first, jnp.where(sub16 == 1, second, jnp.where(sub16 == 2, third, 0.0)))
    digits = digits.astype(bf16)
    items = iota((block, block), 1)
    out = jnp.zeros((8, block), f32)
    for s in range(p.steps):
        onehot = ones_where(items == index[:, s : s + 1])
        cols_ref[s] = nn(onehot, table).astype(bf16)
        got = nt(digits, onehot)
        row = got[0:1, :] + got[1:2, :] + got[2:3, :]
        out = jnp.where(sub8 == s, jnp.broadcast_to(row, (8, block)), out)
    logs_ref[...] = out

    r, half, mine = position()
    lines = p.steps * p.owners * 8
    group = 128 // p.owners
    slots = p.groups * 4 * p.steps
    hi, lo = split_index(row_ids_ref[...].reshape(lines, 128), p.block)
    lane = iota((128, p.pair), 0)
    inner = iota((128, p.pair), 1) % p.share
    pick = ones_where((lane % p.owners == r) & (lane // p.owners == inner % group))
    keep = iota((lines, p.pair), 0) % 8 == (iota((lines, p.pair), 1) % p.share) // group
    slot = iota((slots, lines), 0)
    line = iota((slots, lines), 1)
    step_ok = line // (p.owners * 8) == slot % p.steps
    q = (slot // p.steps) % 4
    mask = (4 * (slot // (4 * p.steps))) ^ mine ^ turn(q)
    routes = [
        ones_where(step_ok & ((line // 8) % p.owners == (r ^ (2 * mask + (k ^ (q // 2)))))) for k in range(2)
    ]

    def row_of(digit):
        picked = jnp.where(keep, nn(digit, pick), 0.0).astype(bf16)
        return jnp.where(iota((slots, p.pair), 1) < p.share, nn(routes[0], picked), nn(routes[1], picked))

    index_ref[...] = (row_of(hi) * 32.0 + row_of(lo)).astype(jnp.int32)


def columns(p, ids, emb, tot, row_ids, after):
    block, width = emb.shape
    outs = [
        jax.ShapeDtypeStruct((p.steps, block, width), bf16),
        jax.ShapeDtypeStruct((8, block), f32),
        jax.ShapeDtypeStruct((p.groups * 4 * p.steps, p.pair), jnp.int32),
    ]
    args = (ids, emb, tot, row_ids)
    return kernel_call(
        functools.partial(columns_kernel, p), outs, *args, *after, vmem=12,
        in_specs=in_vmem(args) + anywhere(after),
        cost=cost(2 * 2 * 1024 * 1024 * 256, 2 * MIB),
    )


def factors_kernel(p, scale, step, counts_ref, *refs):
    gain_ref, shift_ref, buf_ref, sems = refs[-4:]
    r, half, mine = position()
    slots = buf_ref.shape[0]
    tiles = counts_ref.shape[2] // 128

    def copy(k):
        src = counts_ref.at[step, :, pl.ds(k * 128, 128)]
        return pltpu.make_async_copy(src, buf_ref.at[k % slots], sems.at[k % slots])

    for k in range(slots - 1):
        copy(k).start()
    for k in range(tiles):
        if k + slots - 1 < tiles:
            copy(k + slots - 1).start()
        copy(k).wait()
        for g in range(p.groups):
            for q in range(4):
                for jj in range(2):
                    owner = r ^ (2 * ((4 * g) ^ turn(q) ^ mine) + (jj ^ (q // 2)))
                    x = buf_ref[k % slots, pl.ds(owner, p.share, stride=p.owners), :].astype(f32)
                    safe = jnp.maximum(x, 1.0)
                    root = safe * lax.rsqrt(safe)
                    at = ((g * 4 + q) * 2 + jj) * p.share
                    gain = jnp.where(x > 0.0, (0.1 * scale) + (0.25 * scale) * root, 0.0)
                    gain_ref[at : at + p.share, k * 128 : k * 128 + 128] = gain
                    shift_ref[at : at + p.share, k * 128 : k * 128 + 128] = jnp.log(safe)


def factors(p, scale, counts, step, after, vmem):
    shape = jax.ShapeDtypeStruct(counts.shape[1:], f32)
    slots = 4
    return kernel_call(
        functools.partial(factors_kernel, p, scale, step), [shape, shape], counts, *after, vmem=vmem,
        in_specs=anywhere((counts, *after)), out_specs=in_vmem((shape, shape)),
        scratch_shapes=[
            pltpu.VMEM((slots, counts.shape[1], 128), jnp.int32),
            pltpu.SemaphoreType.DMA((slots,)),
        ],
        cost=cost(40 * counts.size / 2, 12 * counts.size / 2),
    )


def grads_kernel(p, scale, first, has_acc, *refs):
    msgs = refs[:4]
    cols_ref, col_logs_ref = refs[4:6]
    factor_refs = refs[6 : 6 + 2 * p.steps]
    outs, acc_ref = refs[-4:-1], refs[-1]
    before = refs[6 + 2 * p.steps] if has_acc else None
    targets = [(outs[0], 0), (outs[2], 0), (outs[1], 0), (outs[2], p.rows)]
    group = max(1, 256 // p.pair)
    for s in range(p.steps):
        cols = cols_ref[s]
        col_logs = col_logs_ref[s : s + 1, :] - log_total
        for q0 in range(0, 4, group):
            members = range(q0, min(q0 + group, 4))
            pieces, row_logs = [], []
            for q in members:
                lo = q // 2 * p.rows + s * p.pair
                pieces.append(msgs[q][lo : lo + p.pair, :])
                logs = msgs[q][2 * p.rows : 2 * p.rows + 16, :128].astype(f32).T
                off = ((first // 2 + q // 2) * p.share) % 128
                for jj in range(2):
                    row_logs.append(logs[off : off + p.share, s * 2 + jj : s * 2 + jj + 1])
            x = jnp.concatenate(pieces, axis=0)
            rows = x.shape[0]
            z = nt(x, cols) + (jnp.concatenate(row_logs, axis=0) + col_logs)
            at = (first + q0) * p.pair
            gain = factor_refs[2 * s][at : at + rows, :]
            fitted = gain * (z - factor_refs[2 * s + 1][at : at + rows, :])
            hinge = (0.5 * scale) * jnp.tanh(0.5 * z) + (0.5 * scale)
            weights = jnp.where(gain > 0.0, fitted, hinge).astype(bf16)
            g = nn(weights, cols)
            for k, q in enumerate(members):
                out, lo = targets[q]
                lo += s * p.pair
                out[lo : lo + p.pair, :] = g[k * p.pair : (k + 1) * p.pair].astype(out.dtype)
            c = tn(x, weights)
            if q0 == 0:
                acc_ref[s] = before[s] + c if has_acc else c
            else:
                acc_ref[s] += c


def grads(p, scale, first, msgs, cols, col_logs, factor, acc=None):
    block = cols.shape[1]
    stay = jax.ShapeDtypeStruct((p.rows, p.width), f32)
    outs = [stay, stay, jax.ShapeDtypeStruct((2 * p.rows, p.width), bf16)]
    outs.append(jax.ShapeDtypeStruct((p.steps, p.width, block), f32))
    args = (*msgs, cols, col_logs, *factor) + (() if acc is None else (acc,))
    return kernel_call(
        functools.partial(grads_kernel, p, scale, first, acc is not None), outs, *args, vmem=24,
        cost=cost(3 * 2 * p.steps * 512 * 1024 * 256, 10 * MIB),
    )


def meet_kernel(p, own_ref, pass_ref, got_ref, *refs):
    own_out, pass_out = refs[-2:]
    own_out[...] = (own_ref[...] + got_ref[: p.rows, :].astype(f32)).astype(bf16)
    pass_out[...] = (pass_ref[...] + got_ref[p.rows :, :].astype(f32)).astype(bf16)


def meet(p, own, passed, got, after=()):
    outs = [jax.ShapeDtypeStruct((p.rows, p.width), bf16)] * 2
    args = (own, passed, got)
    return kernel_call(
        functools.partial(meet_kernel, p), outs, *args, *after, vmem=12,
        in_specs=in_vmem(args) + anywhere(after), cost=cost(MIB, 2 * MIB),
    )


def merge_kernel(p, own_ref, core_ref, *refs):
    out = refs[-1]
    for d in range(2):
        for s in range(p.steps):
            src = slice(s * p.pair + d * p.share, s * p.pair + (d + 1) * p.share)
            lo = d * p.rows + s * p.pair
            out[lo : lo + p.share, :] = own_ref[src, :]
            out[lo + p.share : lo + p.pair, :] = core_ref[src, :]


def merge(p, own, core, after=()):
    args = (own, core)
    return kernel_call(
        functools.partial(merge_kernel, p), jax.ShapeDtypeStruct((2 * p.rows, p.width), bf16), *args, *after,
        vmem=12, in_specs=in_vmem(args) + anywhere(after), cost=cost(MIB, 2 * MIB),
    )


def collect_kernel(p, first, has_acc, index_ref, *refs):
    msgs, out_ref = refs[:2], refs[-1]
    items = iota((p.block, p.pair), 0)
    total = refs[2][...] if has_acc else None
    base = first % 4 // 2 * p.rows
    for s in range(p.steps):
        at = [(first + i) * p.steps + s for i in range(2)]
        onehot = jnp.concatenate([ones_where(items == index_ref[k : k + 1, :]) for k in at], axis=1)
        lo = base + s * p.pair
        rows = jnp.concatenate([m[lo : lo + p.pair, :] for m in msgs], axis=0)
        term = nn(onehot, rows)
        total = term if total is None else total + term
    out_ref[...] = total


def collect(p, first, index, msgs, acc=None):
    args = (index, *msgs) + (() if acc is None else (acc,))
    return kernel_call(
        functools.partial(collect_kernel, p, first, acc is not None),
        jax.ShapeDtypeStruct((p.block, p.width), f32), *args, vmem=12,
        cost=cost(2 * 1024 * 512 * 256, 2 * MIB),
    )


def place_kernel(p, ids_ref, sum_ref, mine_ref, other_ref, acc_ref):
    r = lax.axis_index("row")
    block = sum_ref.shape[2]
    local = ids_ref[...] & (block - 1)
    items = iota((block, block), 0)
    for s in range(p.steps):
        total = sum_ref[s]
        top = total.astype(bf16)
        rest = (total - top.astype(f32)).astype(bf16)
        onehot = ones_where(items == local[s : s + 1, :])
        term = nt(onehot, top) + nt(onehot, rest)
        if s == 0:
            acc_ref[...] = term
        else:
            acc_ref[...] += term
    part = block // 2
    mine_ref[...] = acc_ref[pl.ds(pl.multiple_of((r % 2) * part, part), part), :]
    other_ref[...] = acc_ref[pl.ds(pl.multiple_of((1 - r % 2) * part, part), part), :]


def place(p, ids, sums):
    width, block = sums.shape[1:]
    out = jax.ShapeDtypeStruct((block // 2, width), f32)
    return kernel_call(
        functools.partial(place_kernel, p), [out, out], ids, sums, vmem=12,
        scratch_shapes=[pltpu.VMEM((block, width), f32)],
        cost=cost(4 * 2 * 1024 * 1024 * 256, 5 * MIB),
    )


def spread_kernel(parts, stride, count, *refs):
    mine, arrived = refs[0], refs[1 : 1 + count]
    outs, acc_ref = refs[1 + count : -1], refs[-1]
    here = (lax.axis_index("row") // stride) % parts
    total = mine[...]
    for a in arrived:
        total = total + a[...].astype(f32)
    acc_ref[...] = total
    size = outs[0].shape[0]
    for k, out in enumerate(outs):
        at = pl.multiple_of((here ^ k) * size, size)
        out[...] = acc_ref[pl.ds(at, size), :].astype(out.dtype)


def spread(parts, stride, mine, arrived):
    rows, width = mine.shape
    size = rows // parts
    outs = [jax.ShapeDtypeStruct((size, width), bf16 if (parts == 1 or k) else f32) for k in range(parts)]
    return kernel_call(
        functools.partial(spread_kernel, parts, stride, len(arrived)), outs, mine, *arrived, vmem=16,
        scratch_shapes=[pltpu.VMEM((rows, width), f32)],
        cost=cost(MIB, MIB),
    )


def add_kernel(a_ref, b_ref, out_ref):
    out_ref[...] = (a_ref[...].astype(f32) + b_ref[...].astype(f32)).astype(out_ref.dtype)


def add(a, b):
    return kernel_call(add_kernel, jax.ShapeDtypeStruct(a.shape, a.dtype), a, b, vmem=12, cost=cost(MIB, MIB))


def gather_kernel(parts, stride, *refs):
    pieces, out = refs[:-1], refs[-1]
    here = (lax.axis_index("row") // stride) % parts
    size = pieces[0].shape[0]
    for k, piece in enumerate(pieces):
        at = pl.multiple_of((here ^ k) * size, size)
        value = piece[...].astype(out.dtype)
        out[pl.ds(at, size), :] = value


def gather(stride, pieces, dtype=bf16):
    parts = len(pieces)
    rows, width = pieces[0].shape
    return kernel_call(
        functools.partial(gather_kernel, parts, stride),
        jax.ShapeDtypeStruct((parts * rows, width), dtype), *pieces, vmem=16,
        cost=cost(MIB, MIB),
    )


def local(row_emb, col_emb, counts, row_totals, col_totals, row_ids, col_ids):
    owners = lax.axis_size("row")
    cols_n = lax.axis_size("col")
    block, width = row_emb.shape
    block_cols = col_emb.shape[0]
    steps = counts.shape[0]
    p = Plan(owners, steps, block, width)
    scale = (steps * math.sqrt(owners * block * cols_n * block_cols)) ** (-0.5)

    def row_swap(x, mask):
        return lax.ppermute(x, "row", [(i, i ^ mask) for i in range(owners)])

    def col_swap(x, mask=1):
        return lax.ppermute(x, "col", [(i, i ^ mask) for i in range(cols_n)])

    def grid_swap(x, mask_of):
        perm = []
        for i in range(owners):
            for j in range(cols_n):
                row_mask, col_mask = mask_of(2 * (i % 2) + j % 2)
                perm.append((i * cols_n + j, (i ^ row_mask) * cols_n + (j ^ col_mask)))
        return lax.ppermute(x, ("row", "col"), perm)

    def tie(x, *others):
        return lax.optimization_barrier((x, *others))[0]

    def carry(x, group):
        return grid_swap(x, lambda t: (2 * ((4 * group) ^ turn(t)), 0))

    ids = row_ids.reshape(steps, owners * block // 128, 128)
    totals = row_totals.reshape(1, block)
    msgs = fetch(p, ids, row_emb, row_swap(row_emb, 1), totals, row_swap(totals, 1))
    got = [carry(m, g) for g, m in enumerate(msgs)]
    cols, col_logs, index = columns(
        p, col_ids, col_emb, col_totals.reshape(1, block_cols), ids, (msgs[0],)
    )

    factor = []
    last = col_logs
    landed = [None] * p.groups
    for s in range(steps):
        factor += factors(p, scale, counts, s, (last,), 44 if s == 0 else 38)
        last = factor[-1]
        for g in range(p.groups):
            if s == min(g, steps - 1):
                here = tie(got[g], last)
                landed[g] = (here, col_swap(here))

    acc = None
    ready = None
    arrived = None
    rows = None
    end = p.groups - 1
    for g in range(p.groups):
        here, there = landed[g]
        four = (here, there, row_swap(here, 1), row_swap(there, 1))
        own, passed, send, acc = grads(p, scale, 4 * g, four, cols, col_logs, factor, acc)
        own, passed = meet(p, own, passed, col_swap(send), () if ready is None else (ready,))
        ready = merge(p, own, row_swap(passed, 1), () if arrived is None else (arrived,))
        arrived = carry(ready, g)
        if g == end:
            arrived = tie(arrived, there_back) if g else arrived
            far_landed = arrived
        there_back = col_swap(arrived)
        for k, pair in enumerate(((arrived, there_back), (row_swap(arrived, 1), row_swap(there_back, 1)))):
            rows = collect(p, 4 * g + 2 * k, index, pair, rows)

    mine, other = place(p, col_ids, acc)
    mine, *others = spread(p.wide, 2, mine, [row_swap(other, 1)])
    (piece,) = spread(1, 1, mine, [row_swap(o, (k + 1) * 2) for k, o in enumerate(others)])
    stride = 2 * p.wide
    while stride < owners:
        piece = add(piece, row_swap(piece, stride))
        stride *= 2
    piece = tie(piece, far_landed)
    piece = gather(2, [piece] + [row_swap(piece, k * 2) for k in range(1, p.wide)])
    piece = tie(piece, there_back)
    grad_cols = gather(1, [piece, row_swap(piece, 1)], f32)

    if cols_n > 2:
        total = rows
        for mask in range(2, cols_n, 2):
            total = total + col_swap(rows.astype(bf16), mask).astype(f32)
        rows = total
    return rows, grad_cols


def solution(mesh):
    in_specs = (
        P("row", None),
        P("col", None),
        P(None, "row", "col"),
        P("row"),
        P("col"),
        P(),
        P(None, "col"),
    )
    out_specs = (P("row", None), P("col", None))
    return jax.shard_map(local, mesh=mesh, in_specs=in_specs, out_specs=out_specs, check_vma=False)
```

time: 268 us -> 91.2 us (0.34)
  waiting for transfers between devices: 135 us -> 34.6 us
  local copies, waits for them, and re-layouts: 53.9 us -> 7.26 us
  other arithmetic: 28.5 us -> 0 us
  Pallas kernels: 0 us -> 24.3 us
  matrix products: 15.7 us -> 0 us
  between operations: 14.4 us -> 0.88 us
  starting transfers between devices: 20.4 us -> 23.6 us
    psum x2 -> x0, waiting for transfers between devices: 106 us -> none  [the longest x1 63.9 us: local(): grad_cols = lax.psum(col_accum, 'row')]
    gather x9 -> x0, local copies, waits for them, and re-layouts: 41.7 us -> none  [the longest x3 13.9 us: local(): jnp.log(row_totals.astype(jnp.float32)).astype(jnp.bfloat16)[wanted]]
    ppermute x0 -> x28, waiting for transfers between devices: none -> 34.6 us  [the longest x18 16.9 us: row_swap(): return lax.ppermute(x, 'row', [(i, i ^ mask) for i in range(owners)])]
    all_to_all x3 -> x0, waiting for transfers between devices: 28.5 us -> none  [the longest x1 25 us: local(): lax.all_to_all(row_partial, 'row', split_axis=2, concat_axis=2, tiled=True)]
    scatter-add x3 -> x0, other arithmetic: 25.3 us -> none  [the longest x2 12.8 us: local(): col_accum = col_accum.at[col_local[step]].add(col_term)]
    pallas_call x0 -> x21, Pallas kernels: none -> 24.3 us  [kernel_call(): pl.pallas_call(body, out_shape=outs, compiler_params=pltpu.CompilerParams...]
    ppermute x0 -> x28, starting transfers between devices: none -> 23.6 us  [the longest x18 8.99 us: row_swap(): return lax.ppermute(x, 'row', [(i, i ^ mask) for i in range(owners)])]
    all_to_all x3 -> x0, starting transfers between devices: 20.3 us -> none  [the longest x1 7.36 us: local(): lax.all_to_all(log_rows, 'row', split_axis=2, concat_axis=2, tiled=True)]
  transfers between devices with their start and end apart: 5 -> 28, of which waited for: 4 -> 10; matrix products, arithmetic and copies ran while one was open for 23% -> 1% of each run, Pallas kernels for 0% -> 23%
where the time goes in v2:
time: 91.2 us; the launch traced here: 90.6 us
  waiting for transfers between devices  34.6 us (38%)
  Pallas kernels  24.3 us (27%)
  starting transfers between devices  23.6 us (26%)
  local copies, waits for them, and re-layouts  7.26 us (8%)
    pallas_call x21, Pallas kernels, kernel_call(): pl.pallas_call(body, out_shape=outs, compiler_params=pltpu.CompilerParams...  24.3 us
    ppermute x18, waiting for transfers between devices, row_swap(): return lax.ppermute(x, 'row', [(i, i ^ mask) for i in range(owners)])  16.9 us
    ppermute x6, waiting for transfers between devices, col_swap(): return lax.ppermute(x, 'col', [(i, i ^ mask) for i in range(cols_n)])  13.3 us
    ppermute x18, starting transfers between devices, row_swap(): return lax.ppermute(x, 'row', [(i, i ^ mask) for i in range(owners)])  8.99 us
    ppermute x6, starting transfers between devices, col_swap(): return lax.ppermute(x, 'col', [(i, i ^ mask) for i in range(cols_n)])  8.83 us
    unnamed x17, local copies, waits for them, and re-layouts  7.26 us
    ppermute x4, starting transfers between devices, grid_swap(): return lax.ppermute(x, ('row', 'col'), perm)  5.78 us
    ppermute x4, waiting for transfers between devices, grid_swap(): return lax.ppermute(x, ('row', 'col'), perm)  4.45 us
  transfers between devices with their start and end apart: 28, of which 10 were waited for; matrix products, arithmetic and copies ran while one was open for 1% of the time, Pallas kernels for 23%

profile of v2, /device:TPU:0, one launch (start us, length us, event | category | flops | bytes accessed | tf_op | source)
XLA Modules:
  0.0 90.6 jit_solution(11089720338978947986)
XLA Ops:
  0.6 0.5 collective-permute-start
  1.2 0.9 %copy.11 = s32[1,2,128,128]{3,2,1,0:T(8,128)S(1)} copy(s32[1,2,128,128]{3,1,2,0:T(2,128)} %bitcast.11) | data formatting | bytes 262144
  2.1 0.8 collective-permute-done.1.tot_oth_ref
  2.9 1.0 %copy-done.2 = bf16[1024,256]{1,0:T(8,128)(2,1)S(1)} copy-done((bf16[1024,256]{1,0:T(8,128)(2,1)S(1)}, bf16[1024,256]{1,0:T(8,128)(2,1)}, u32[]{:S(2)}) %copy-start.2) | copy-done | bytes 524312
  3.9 0.7 copy-done.6
  4.6 1.7 %shard_map.86 = (bf16[528,256]{1,0:T(8,128)(2,1)S(1)}, bf16[528,256]{1,0:T(8,128)(2,1)S(1)}) custom-call(s32[2,128,128]{2,1,0:T(8,128)S(1)} %bitcast.6, bf16[1024,256]{1,0:T(8,128)(2,1)S(1)} %copy-done.2, bf16[1024,256]{1,0:T(8,128)(2,1)S(1)} %collective-permute-done.oth_ref, s32[1,1024]{1,0:T(1,128)S(1)} %bitcast.9, ...), custom_call_target="tpu_custom_call" | custom-call | flops 1 | bytes 1 | tf_op jit(solution)/shard_map/pallas_call | solution.py:43
  6.4 0.7 collective-permute-start.6
  7.1 4.0 %collective-permute-start.2 = (bf16[528,256]{1,0:T(8,128)(2,1)S(1)}, bf16[528,256]{1,0:T(8,128)(2,1)S(1)}, u32[]{:S(2)}, u32[]{:S(2)}) collective-permute-start(bf16[528,256]{1,0:T(8,128)(2,1)S(1)} %get-tuple-element.34), channel_id=1, source_target_pairs={{0,16},{1,25},{2,30},{3,23},{4,20},{5,29},{6,26},{7,19},{8,24},{9,... | collective-permute-start | bytes 811016 | tf_op jit(solution)/shard_map/ppermute | solution.py:473
  11.1 1.0 %copy-done.3 = bf16[1024,256]{1,0:T(8,128)(2,1)S(1)} copy-done((bf16[1024,256]{1,0:T(8,128)(2,1)S(1)}, bf16[1024,256]{1,0:T(8,128)(2,1)}, u32[]{:S(2)}) %copy-start.3) | copy-done | bytes 524312
  12.1 0.7 copy-done.4
  12.8 0.7 copy-done.7
  13.5 2.9 %shard_map.87 = (bf16[2,1024,256]{2,1,0:T(8,128)(2,1)S(1)}, f32[8,1024]{1,0:T(8,128)S(1)}, s32[16,128]{1,0:T(8,128)S(1)}) custom-call(s32[2,1024]{1,0:T(2,128)S(1)} %copy-done.4, bf16[1024,256]{1,0:T(8,128)(2,1)S(1)} %copy-done.3, s32[1,1024]{1,0:T(1,128)S(1)} %bitcast.10, s32[2,128,128]{2,1,0:T(8,128)S(1)} %bitcast.7, ...), custom_call_target="tpu_custom_call" | custom-call | flops 1 | bytes 1 | tf_op jit(solution)/shard_map/pallas_call | solution.py:43
  16.4 3.7 %shard_map.88 = (f32[1024,1024]{1,0:T(8,128)S(1)}, f32[1024,1024]{1,0:T(8,128)S(1)}) custom-call(s32[2,1024,1024]{2,1,0:T(8,128)} %counts_ref.3, f32[8,1024]{1,0:T(8,128)S(1)} %get-tuple-element.35.refs_0_.refs_5_), custom_call_target="tpu_custom_call" | custom-call | flops 1 | bytes 1 | tf_op jit(solution)/shard_map/pallas_call | solution.py:43
  20.1 4.3 %collective-permute-start.7 = (bf16[528,256]{1,0:T(8,128)(2,1)S(1)}, bf16[528,256]{1,0:T(8,128)(2,1)S(1)}, u32[]{:S(2)}, u32[]{:S(2)}) collective-permute-start(bf16[528,256]{1,0:T(8,128)(2,1)S(1)} %collective-permute-done.6.refs_0_), channel_id=1, source_target_pairs={{0,1},{1,0},{2,3},{3,2},{4,5},{5,4},{6,7},{7,6},{8,9},{9,8},{10,11... | collective-permute-start | bytes 811016 | tf_op jit(solution)/shard_map/ppermute | solution.py:465
  24.4 3.7 %shard_map.89 = (f32[1024,1024]{1,0:T(8,128)S(1)}, f32[1024,1024]{1,0:T(8,128)S(1)}) custom-call(s32[2,1024,1024]{2,1,0:T(8,128)} %counts_ref.3, f32[1024,1024]{1,0:T(8,128)S(1)} %get-tuple-element.36.refs_0_.refs_7_), custom_call_target="tpu_custom_call" | custom-call | flops 1 | bytes 1 | tf_op jit(solution)/shard_map/pallas_call | solution.py:43
  28.2 0.4 collective-permute-start.8
  28.6 3.1 %collective-permute-done.7.refs_1_ = bf16[528,256]{1,0:T(8,128)(2,1)S(1)} collective-permute-done((bf16[528,256]{1,0:T(8,128)(2,1)S(1)}, bf16[528,256]{1,0:T(8,128)(2,1)S(1)}, u32[]{:S(2)}, u32[]{:S(2)}) %collective-permute-start.7) | collective-permute-done | bytes 270368 | tf_op jit(solution)/shard_map/ppermute | solution.py:465
  31.7 0.1 collective-permute-start.9
  31.8 0.4 collective-permute-start.4
  32.2 5.3 %collective-permute-done.3.refs_1_ = bf16[528,256]{1,0:T(8,128)(2,1)S(1)} collective-permute-done((bf16[528,256]{1,0:T(8,128)(2,1)S(1)}, bf16[528,256]{1,0:T(8,128)(2,1)S(1)}, u32[]{:S(2)}, u32[]{:S(2)}) %collective-permute-start.3) | collective-permute-done | bytes 270368 | tf_op jit(solution)/shard_map/ppermute | solution.py:465
  37.6 2.6 %shard_map.90 = (f32[256,256]{1,0:T(8,128)S(1)}, f32[256,256]{1,0:T(8,128)S(1)}, bf16[512,256]{1,0:T(8,128)(2,1)S(1)}, f32[2,256,1024]{2,1,0:T(8,128)S(1)}) custom-call(bf16[528,256]{1,0:T(8,128)(2,1)S(1)} %collective-permute-done.6.refs_0_, bf16[528,256]{1,0:T(8,128)(2,1)S(1)} %collective-permute-done.7.refs_1_, ...), custom_call_target="tpu_custom_call" | custom-call | flops 1 | bytes 1 | tf_op jit(solution)/shard_map/pallas_call | solution.py:43
  40.2 0.7 collective-permute-start.11
  40.9 2.2 %copy-done.1 = f32[1024,1024]{1,0:T(8,128)S(1)} copy-done((f32[1024,1024]{1,0:T(8,128)S(1)}, f32[1024,1024]{1,0:T(8,128)}, u32[]{:S(2)}) %copy-start.1) | copy-done | bytes 4194328
  43.1 2.9 %shard_map.91 = (f32[256,256]{1,0:T(8,128)S(1)}, f32[256,256]{1,0:T(8,128)S(1)}, bf16[512,256]{1,0:T(8,128)(2,1)S(1)}, f32[2,256,1024]{2,1,0:T(8,128)S(1)}) custom-call(bf16[528,256]{1,0:T(8,128)(2,1)S(1)} %collective-permute-done.2.refs_0_, bf16[528,256]{1,0:T(8,128)(2,1)S(1)} %collective-permute-done.3.refs_1_, ...), custom_call_target="tpu_custom_call" | custom-call | flops 1 | bytes 1 | tf_op jit(solution)/shard_map/pallas_call | solution.py:43
  46.0 2.6 %shard_map.100 = (f32[512,256]{1,0:T(8,128)S(1)}, f32[512,256]{1,0:T(8,128)S(1)}) custom-call(s32[2,1024]{1,0:T(2,128)S(1)} %copy-done.5, f32[2,256,1024]{2,1,0:T(8,128)S(1)} %get-tuple-element.55.sum_ref), custom_call_target="tpu_custom_call" | custom-call | flops 1 | bytes 1 | tf_op jit(solution)/shard_map/pallas_call | solution.py:43
  48.6 0.3 collective-permute-start.22
  48.9 1.4 %collective-permute-start.10 = (bf16[512,256]{1,0:T(8,128)(2,1)S(1)}, bf16[512,256]{1,0:T(8,128)(2,1)S(1)}, u32[]{:S(2)}, u32[]{:S(2)}) collective-permute-start(bf16[512,256]{1,0:T(8,128)(2,1)S(1)} %get-tuple-element.46), channel_id=1, source_target_pairs={{0,1},{1,0},{2,3},{3,2},{4,5},{5,4},{6,7},{7,6},{8,9},{9,8},{10,11... | collective-permute-start | bytes 786440 | tf_op jit(solution)/shard_map/ppermute | solution.py:465
  50.4 1.3 %collective-permute-done.12.core_ref = bf16[256,256]{1,0:T(8,128)(2,1)S(1)} collective-permute-done((bf16[256,256]{1,0:T(8,128)(2,1)S(1)}, bf16[256,256]{1,0:T(8,128)(2,1)S(1)}, u32[]{:S(2)}, u32[]{:S(2)}) %collective-permute-start.12) | collective-permute-done | bytes 131104 | tf_op jit(solution)/shard_map/ppermute | solution.py:462
  51.8 0.7 collective-permute-start.14
  52.5 4.9 %collective-permute-done.10.got_ref = bf16[512,256]{1,0:T(8,128)(2,1)S(1)} collective-permute-done((bf16[512,256]{1,0:T(8,128)(2,1)S(1)}, bf16[512,256]{1,0:T(8,128)(2,1)S(1)}, u32[]{:S(2)}, u32[]{:S(2)}) %collective-permute-start.10) | collective-permute-done | bytes 262176 | tf_op jit(solution)/shard_map/ppermute | solution.py:465
  57.6 1.6 %collective-permute-start.23 = (bf16[256,256]{1,0:T(8,128)(2,1)S(1)}, bf16[256,256]{1,0:T(8,128)(2,1)S(1)}, u32[]{:S(2)}, u32[]{:S(2)}) collective-permute-start(bf16[256,256]{1,0:T(8,128)(2,1)S(1)} %get-tuple-element.59), channel_id=1, source_target_pairs={{0,4},{2,6},{4,0},{6,2},{8,12},{10,14},{12,8},{14,10},{16,20},{18,... | collective-permute-start | bytes 393224 | tf_op jit(solution)/shard_map/ppermute | solution.py:462
  59.2 0.4 collective-permute-start.15
  59.6 2.4 %collective-permute-start.16 = (bf16[512,256]{1,0:T(8,128)(2,1)S(1)}, bf16[512,256]{1,0:T(8,128)(2,1)S(1)}, u32[]{:S(2)}, u32[]{:S(2)}) collective-permute-start(bf16[512,256]{1,0:T(8,128)(2,1)S(1)} %collective-permute-done.14.refs_0_), channel_id=1, source_target_pairs={{0,1},{1,0},{2,3},{3,2},{4,5},{5,4},{6,7},{7,6},{8,9},{9,8},{10,11... | collective-permute-start | bytes 786440 | tf_op jit(solution)/shard_map/ppermute | solution.py:465
  62.0 1.6 %collective-permute-done.23.refs_1_ = bf16[256,256]{1,0:T(8,128)(2,1)S(1)} collective-permute-done((bf16[256,256]{1,0:T(8,128)(2,1)S(1)}, bf16[256,256]{1,0:T(8,128)(2,1)S(1)}, u32[]{:S(2)}, u32[]{:S(2)}) %collective-permute-start.23) | collective-permute-done | bytes 131104 | tf_op jit(solution)/shard_map/ppermute | solution.py:462
  63.6 2.5 %collective-permute-start.24 = (bf16[256,256]{1,0:T(8,128)(2,1)S(1)}, bf16[256,256]{1,0:T(8,128)(2,1)S(1)}, u32[]{:S(2)}, u32[]{:S(2)}) collective-permute-start(bf16[256,256]{1,0:T(8,128)(2,1)S(1)} %shard_map.102.a_ref), channel_id=1, source_target_pairs={{0,8},{2,10},{4,12},{6,14},{8,0},{10,2},{12,4},{14,6},{16,24},{18,... | collective-permute-start | bytes 393224 | tf_op jit(solution)/shard_map/ppermute | solution.py:462
  66.1 6.3 %collective-permute-done.24.b_ref = bf16[256,256]{1,0:T(8,128)(2,1)S(1)} collective-permute-done((bf16[256,256]{1,0:T(8,128)(2,1)S(1)}, bf16[256,256]{1,0:T(8,128)(2,1)S(1)}, u32[]{:S(2)}, u32[]{:S(2)}) %collective-permute-start.24) | collective-permute-done | bytes 131104 | tf_op jit(solution)/shard_map/ppermute | solution.py:462
  72.5 0.9 collective-permute-start.25
  73.3 4.4 %collective-permute-done.15.refs_0_ = bf16[512,256]{1,0:T(8,128)(2,1)S(1)} collective-permute-done((bf16[512,256]{1,0:T(8,128)(2,1)S(1)}, bf16[512,256]{1,0:T(8,128)(2,1)S(1)}, u32[]{:S(2)}, u32[]{:S(2)}) %collective-permute-start.15) | collective-permute-done | bytes 262176 | tf_op jit(solution)/shard_map/ppermute | solution.py:473
  77.8 2.8 %collective-permute-done.25.b_ref = bf16[256,256]{1,0:T(8,128)(2,1)S(1)} collective-permute-done((bf16[256,256]{1,0:T(8,128)(2,1)S(1)}, bf16[256,256]{1,0:T(8,128)(2,1)S(1)}, u32[]{:S(2)}, u32[]{:S(2)}) %collective-permute-start.25) | collective-permute-done | bytes 131104 | tf_op jit(solution)/shard_map/ppermute | solution.py:462
  80.6 0.9 collective-permute-start.26
  81.5 0.5 collective-permute-start.21
  82.0 4.1 %collective-permute-done.26.refs_1_ = bf16[256,256]{1,0:T(8,128)(2,1)S(1)} collective-permute-done((bf16[256,256]{1,0:T(8,128)(2,1)S(1)}, bf16[256,256]{1,0:T(8,128)(2,1)S(1)}, u32[]{:S(2)}, u32[]{:S(2)}) %collective-permute-start.26) | collective-permute-done | bytes 131104 | tf_op jit(solution)/shard_map/ppermute | solution.py:462
  86.2 0.5 collective-permute-start.17
  86.8 0.4 shard_map.96.refs_2_
  87.3 0.4 shard_map.97.refs_2_
  87.7 0.4 shard_map.98.refs_2_
  88.2 1.1 %shard_map.106 = f32[1024,256]{1,0:T(8,128)} custom-call(bf16[512,256]{1,0:T(8,128)(2,1)S(1)} %shard_map.105.refs_0_, bf16[512,256]{1,0:T(8,128)(2,1)S(1)} %collective-permute-done.27.refs_1_), custom_call_target="tpu_custom_call" | custom-call | flops 1 | bytes 1 | tf_op jit(solution)/shard_map/pallas_call | solution.py:43
  89.2 1.4 %shard_map.99 = f32[1024,256]{1,0:T(8,128)} custom-call(s32[16,128]{1,0:T(8,128)S(1)} %get-tuple-element.33.index_ref, bf16[512,256]{1,0:T(8,128)(2,1)S(1)} %collective-permute-done.17.refs_0_, bf16[512,256]{1,0:T(8,128)(2,1)S(1)} %collective-permute-done.19.refs_1_, f32[1024,256]{1,0:T(8,128)S(1)} %shard_map.98.refs_2_), custom_call_target="tpu_custom_call" | custom-call | flops 1 | bytes 1 | tf_op jit(solution)/shard_map/pallas_call | solution.py:43
  (46 shorter events, 0.9 us)
Async XLA Ops:
  0.6 2.3 %collective-permute-start = (bf16[1024,256]{1,0:T(8,128)(2,1)}, bf16[1024,256]{1,0:T(8,128)(2,1)S(1)}, u32[]{:S(2)}, u32[]{:S(2)}) collective-permute-start(bf16[1024,256]{1,0:T(8,128)(2,1)} %own_ref.1), channel_id=1, source_target_pairs={{0,2},{2,0},{4,6},{6,4},{8,10},{10,8},{12,14},{14,12},{16,18},{18,... | collective-permute-start | bytes 1572872 | tf_op jit(solution)/shard_map/ppermute | solution.py:462
  1.1 1.8 %collective-permute-start.1 = (s32[1,1024]{1,0:T(1,128)}, s32[1,1024]{1,0:T(1,128)S(1)}, u32[]{:S(2)}, u32[]{:S(2)}) collective-permute-start(s32[1,1024]{1,0:T(1,128)} %bitcast.8), channel_id=1, source_target_pairs={{0,2},{2,0},{4,6},{6,4},{8,10},{10,8},{12,14},{14,12},{16,18},{18,... | collective-permute-start | bytes 12296 | tf_op jit(solution)/shard_map/ppermute | solution.py:462
  2.9 1.0 %copy-start.2 = (bf16[1024,256]{1,0:T(8,128)(2,1)S(1)}, bf16[1024,256]{1,0:T(8,128)(2,1)}, u32[]{:S(2)}) copy-start(bf16[1024,256]{1,0:T(8,128)(2,1)} %own_ref.1) | copy-start | bytes 1572868
  3.9 0.7 copy-start.6
  6.4 13.7 %collective-permute-start.6 = (bf16[528,256]{1,0:T(8,128)(2,1)S(1)}, bf16[528,256]{1,0:T(8,128)(2,1)S(1)}, u32[]{:S(2)}, u32[]{:S(2)}) collective-permute-start(bf16[528,256]{1,0:T(8,128)(2,1)S(1)} %get-tuple-element.32.refs_0_), channel_id=1, source_target_pairs={{0,0},{1,9},{2,14},{3,7},{4,4},{5,13},{6,10},{7,3},{8,8},{9,1},{10... | collective-permute-start | bytes 811016 | tf_op jit(solution)/shard_map/ppermute | solution.py:473
  7.1 21.1 %collective-permute-start.2 = (bf16[528,256]{1,0:T(8,128)(2,1)S(1)}, bf16[528,256]{1,0:T(8,128)(2,1)S(1)}, u32[]{:S(2)}, u32[]{:S(2)}) collective-permute-start(bf16[528,256]{1,0:T(8,128)(2,1)S(1)} %get-tuple-element.34), channel_id=1, source_target_pairs={{0,16},{1,25},{2,30},{3,23},{4,20},{5,29},{6,26},{7,19},{8,24},{9,... | collective-permute-start | bytes 811016 | tf_op jit(solution)/shard_map/ppermute | solution.py:473
  11.1 1.0 %copy-start.3 = (bf16[1024,256]{1,0:T(8,128)(2,1)S(1)}, bf16[1024,256]{1,0:T(8,128)(2,1)}, u32[]{:S(2)}) copy-start(bf16[1024,256]{1,0:T(8,128)(2,1)} %emb_ref.1) | copy-start | bytes 1572868
  12.1 0.7 copy-start.4
  12.8 0.7 copy-start.7
  20.1 11.6 %collective-permute-start.7 = (bf16[528,256]{1,0:T(8,128)(2,1)S(1)}, bf16[528,256]{1,0:T(8,128)(2,1)S(1)}, u32[]{:S(2)}, u32[]{:S(2)}) collective-permute-start(bf16[528,256]{1,0:T(8,128)(2,1)S(1)} %collective-permute-done.6.refs_0_), channel_id=1, source_target_pairs={{0,1},{1,0},{2,3},{3,2},{4,5},{5,4},{6,7},{7,6},{8,9},{9,8},{10,11... | collective-permute-start | bytes 811016 | tf_op jit(solution)/shard_map/ppermute | solution.py:465
  28.1 12.1 %copy-start = (f32[1024,1024]{1,0:T(8,128)}, f32[1024,1024]{1,0:T(8,128)S(1)}, u32[]{:S(2)}) copy-start(f32[1024,1024]{1,0:T(8,128)S(1)} %get-tuple-element.37.refs_9_) | copy-start | bytes 12582916
  28.1 9.4 %collective-permute-start.3 = (bf16[528,256]{1,0:T(8,128)(2,1)S(1)}, bf16[528,256]{1,0:T(8,128)(2,1)S(1)}, u32[]{:S(2)}, u32[]{:S(2)}) collective-permute-start(bf16[528,256]{1,0:T(8,128)(2,1)S(1)} %collective-permute-done.2.refs_0_), channel_id=1, source_target_pairs={{0,1},{1,0},{2,3},{3,2},{4,5},{5,4},{6,7},{7,6},{8,9},{9,8},{10,11... | collective-permute-start | bytes 811016 | tf_op jit(solution)/shard_map/ppermute | solution.py:465
  28.2 9.3 %collective-permute-start.8 = (bf16[528,256]{1,0:T(8,128)(2,1)S(1)}, bf16[528,256]{1,0:T(8,128)(2,1)S(1)}, u32[]{:S(2)}, u32[]{:S(2)}) collective-permute-start(bf16[528,256]{1,0:T(8,128)(2,1)S(1)} %collective-permute-done.6.refs_0_), channel_id=1, source_target_pairs={{0,2},{2,0},{4,6},{6,4},{8,10},{10,8},{12,14},{14,12},{16,18},{18,... | collective-permute-start | bytes 811016 | tf_op jit(solution)/shard_map/ppermute | solution.py:462
  31.7 5.8 %collective-permute-start.9 = (bf16[528,256]{1,0:T(8,128)(2,1)S(1)}, bf16[528,256]{1,0:T(8,128)(2,1)S(1)}, u32[]{:S(2)}, u32[]{:S(2)}) collective-permute-start(bf16[528,256]{1,0:T(8,128)(2,1)S(1)} %collective-permute-done.7.refs_1_), channel_id=1, source_target_pairs={{0,2},{2,0},{4,6},{6,4},{8,10},{10,8},{12,14},{14,12},{16,18},{18,... | collective-permute-start | bytes 811016 | tf_op jit(solution)/shard_map/ppermute | solution.py:462
  31.8 9.0 %collective-permute-start.4 = (bf16[528,256]{1,0:T(8,128)(2,1)S(1)}, bf16[528,256]{1,0:T(8,128)(2,1)S(1)}, u32[]{:S(2)}, u32[]{:S(2)}) collective-permute-start(bf16[528,256]{1,0:T(8,128)(2,1)S(1)} %collective-permute-done.2.refs_0_), channel_id=1, source_target_pairs={{0,2},{2,0},{4,6},{6,4},{8,10},{10,8},{12,14},{14,12},{16,18},{18,... | collective-permute-start | bytes 811016 | tf_op jit(solution)/shard_map/ppermute | solution.py:462
  37.5 3.4 %collective-permute-start.5 = (bf16[528,256]{1,0:T(8,128)(2,1)S(1)}, bf16[528,256]{1,0:T(8,128)(2,1)S(1)}, u32[]{:S(2)}, u32[]{:S(2)}) collective-permute-start(bf16[528,256]{1,0:T(8,128)(2,1)S(1)} %collective-permute-done.3.refs_1_), channel_id=1, source_target_pairs={{0,2},{2,0},{4,6},{6,4},{8,10},{10,8},{12,14},{14,12},{16,18},{18,... | collective-permute-start | bytes 811016 | tf_op jit(solution)/shard_map/ppermute | solution.py:462
  40.2 10.1 %collective-permute-start.11 = (bf16[512,256]{1,0:T(8,128)(2,1)S(1)}, bf16[512,256]{1,0:T(8,128)(2,1)S(1)}, u32[]{:S(2)}, u32[]{:S(2)}) collective-permute-start(bf16[512,256]{1,0:T(8,128)(2,1)S(1)} %get-tuple-element.49), channel_id=1, source_target_pairs={{0,1},{1,0},{2,3},{3,2},{4,5},{5,4},{6,7},{7,6},{8,9},{9,8},{10,11... | collective-permute-start | bytes 786440 | tf_op jit(solution)/shard_map/ppermute | solution.py:465
  40.9 2.2 %copy-start.1 = (f32[1024,1024]{1,0:T(8,128)S(1)}, f32[1024,1024]{1,0:T(8,128)}, u32[]{:S(2)}) copy-start(f32[1024,1024]{1,0:T(8,128)} %copy-done) | copy-start | bytes 12582916
  43.1 2.9 %copy-start.5 = (s32[2,1024]{1,0:T(2,128)S(1)}, s32[2,1024]{1,0:T(2,128)}, u32[]{:S(2)}) copy-start(s32[2,1024]{1,0:T(2,128)} %ids_ref.3) | copy-start | bytes 24580
  48.6 8.9 %collective-permute-start.22 = (f32[512,256]{1,0:T(8,128)S(1)}, f32[512,256]{1,0:T(8,128)S(1)}, u32[]{:S(2)}, u32[]{:S(2)}) collective-permute-start(f32[512,256]{1,0:T(8,128)S(1)} %get-tuple-element.57), channel_id=1, source_target_pairs={{0,2},{2,0},{4,6},{6,4},{8,10},{10,8},{12,14},{14,12},{16,18},{18,... | collective-permute-start | bytes 1572872 | tf_op jit(solution)/shard_map/ppermute | solution.py:462
  48.9 8.5 %collective-permute-start.10 = (bf16[512,256]{1,0:T(8,128)(2,1)S(1)}, bf16[512,256]{1,0:T(8,128)(2,1)S(1)}, u32[]{:S(2)}, u32[]{:S(2)}) collective-permute-start(bf16[512,256]{1,0:T(8,128)(2,1)S(1)} %get-tuple-element.46), channel_id=1, source_target_pairs={{0,1},{1,0},{2,3},{3,2},{4,5},{5,4},{6,7},{7,6},{8,9},{9,8},{10,11... | collective-permute-start | bytes 786440 | tf_op jit(solution)/shard_map/ppermute | solution.py:465
  50.4 1.4 %collective-permute-start.12 = (bf16[256,256]{1,0:T(8,128)(2,1)S(1)}, bf16[256,256]{1,0:T(8,128)(2,1)S(1)}, u32[]{:S(2)}, u32[]{:S(2)}) collective-permute-start(bf16[256,256]{1,0:T(8,128)(2,1)S(1)} %get-tuple-element.51), channel_id=1, source_target_pairs={{0,2},{2,0},{4,6},{6,4},{8,10},{10,8},{12,14},{14,12},{16,18},{18,... | collective-permute-start | bytes 393224 | tf_op jit(solution)/shard_map/ppermute | solution.py:462
  51.8 7.4 %collective-permute-start.14 = (bf16[512,256]{1,0:T(8,128)(2,1)S(1)}, bf16[512,256]{1,0:T(8,128)(2,1)S(1)}, u32[]{:S(2)}, u32[]{:S(2)}) collective-permute-start(bf16[512,256]{1,0:T(8,128)(2,1)S(1)} %shard_map.93.refs_0_), channel_id=1, source_target_pairs={{0,0},{1,9},{2,14},{3,7},{4,4},{5,13},{6,10},{7,3},{8,8},{9,1},{10... | collective-permute-start | bytes 786440 | tf_op jit(solution)/shard_map/ppermute | solution.py:473
  57.4 1.8 %collective-permute-start.13 = (bf16[256,256]{1,0:T(8,128)(2,1)S(1)}, bf16[256,256]{1,0:T(8,128)(2,1)S(1)}, u32[]{:S(2)}, u32[]{:S(2)}) collective-permute-start(bf16[256,256]{1,0:T(8,128)(2,1)S(1)} %get-tuple-element.53), channel_id=1, source_target_pairs={{0,2},{2,0},{4,6},{6,4},{8,10},{10,8},{12,14},{14,12},{16,18},{18,... | collective-permute-start | bytes 393224 | tf_op jit(solution)/shard_map/ppermute | solution.py:462
  57.6 6.0 %collective-permute-start.23 = (bf16[256,256]{1,0:T(8,128)(2,1)S(1)}, bf16[256,256]{1,0:T(8,128)(2,1)S(1)}, u32[]{:S(2)}, u32[]{:S(2)}) collective-permute-start(bf16[256,256]{1,0:T(8,128)(2,1)S(1)} %get-tuple-element.59), channel_id=1, source_target_pairs={{0,4},{2,6},{4,0},{6,2},{8,12},{10,14},{12,8},{14,10},{16,20},{18,... | collective-permute-start | bytes 393224 | tf_op jit(solution)/shard_map/ppermute | solution.py:462
  59.2 18.6 %collective-permute-start.15 = (bf16[512,256]{1,0:T(8,128)(2,1)S(1)}, bf16[512,256]{1,0:T(8,128)(2,1)S(1)}, u32[]{:S(2)}, u32[]{:S(2)}) collective-permute-start(bf16[512,256]{1,0:T(8,128)(2,1)S(1)} %shard_map.95), channel_id=1, source_target_pairs={{0,16},{1,25},{2,30},{3,23},{4,20},{5,29},{6,26},{7,19},{8,24},{9,... | collective-permute-start | bytes 786440 | tf_op jit(solution)/shard_map/ppermute | solution.py:473
  59.6 18.2 %collective-permute-start.16 = (bf16[512,256]{1,0:T(8,128)(2,1)S(1)}, bf16[512,256]{1,0:T(8,128)(2,1)S(1)}, u32[]{:S(2)}, u32[]{:S(2)}) collective-permute-start(bf16[512,256]{1,0:T(8,128)(2,1)S(1)} %collective-permute-done.14.refs_0_), channel_id=1, source_target_pairs={{0,1},{1,0},{2,3},{3,2},{4,5},{5,4},{6,7},{7,6},{8,9},{9,8},{10,11... | collective-permute-start | bytes 786440 | tf_op jit(solution)/shard_map/ppermute | solution.py:465
  63.6 8.8 %collective-permute-start.24 = (bf16[256,256]{1,0:T(8,128)(2,1)S(1)}, bf16[256,256]{1,0:T(8,128)(2,1)S(1)}, u32[]{:S(2)}, u32[]{:S(2)}) collective-permute-start(bf16[256,256]{1,0:T(8,128)(2,1)S(1)} %shard_map.102.a_ref), channel_id=1, source_target_pairs={{0,8},{2,10},{4,12},{6,14},{8,0},{10,2},{12,4},{14,6},{16,24},{18,... | collective-permute-start | bytes 393224 | tf_op jit(solution)/shard_map/ppermute | solution.py:462
  72.5 8.1 %collective-permute-start.25 = (bf16[256,256]{1,0:T(8,128)(2,1)S(1)}, bf16[256,256]{1,0:T(8,128)(2,1)S(1)}, u32[]{:S(2)}, u32[]{:S(2)}) collective-permute-start(bf16[256,256]{1,0:T(8,128)(2,1)S(1)} %shard_map.103.a_ref), channel_id=1, source_target_pairs={{0,16},{2,18},{4,20},{6,22},{8,24},{10,26},{12,28},{14,30},{16,0},... | collective-permute-start | bytes 393224 | tf_op jit(solution)/shard_map/ppermute | solution.py:462
  77.8 8.4 %collective-permute-start.18 = (bf16[512,256]{1,0:T(8,128)(2,1)S(1)}, bf16[512,256]{1,0:T(8,128)(2,1)S(1)}, u32[]{:S(2)}, u32[]{:S(2)}) collective-permute-start(bf16[512,256]{1,0:T(8,128)(2,1)S(1)} %collective-permute-done.15.refs_0_), channel_id=1, source_target_pairs={{0,1},{1,0},{2,3},{3,2},{4,5},{5,4},{6,7},{7,6},{8,9},{9,8},{10,11... | collective-permute-start | bytes 786440 | tf_op jit(solution)/shard_map/ppermute | solution.py:465
  80.6 5.5 %collective-permute-start.26 = (bf16[256,256]{1,0:T(8,128)(2,1)S(1)}, bf16[256,256]{1,0:T(8,128)(2,1)S(1)}, u32[]{:S(2)}, u32[]{:S(2)}) collective-permute-start(bf16[256,256]{1,0:T(8,128)(2,1)S(1)} %shard_map.104.refs_0_), channel_id=1, source_target_pairs={{0,4},{2,6},{4,0},{6,2},{8,12},{10,14},{12,8},{14,10},{16,20},{18,... | collective-permute-start | bytes 393224 | tf_op jit(solution)/shard_map/ppermute | solution.py:462
  81.5 5.8 %collective-permute-start.20 = (bf16[512,256]{1,0:T(8,128)(2,1)S(1)}, bf16[512,256]{1,0:T(8,128)(2,1)S(1)}, u32[]{:S(2)}, u32[]{:S(2)}) collective-permute-start(bf16[512,256]{1,0:T(8,128)(2,1)S(1)} %collective-permute-done.14.refs_0_), channel_id=1, source_target_pairs={{0,2},{2,0},{4,6},{6,4},{8,10},{10,8},{12,14},{14,12},{16,18},{18,... | collective-permute-start | bytes 786440 | tf_op jit(solution)/shard_map/ppermute | solution.py:462
  81.5 5.8 %collective-permute-start.21 = (bf16[512,256]{1,0:T(8,128)(2,1)S(1)}, bf16[512,256]{1,0:T(8,128)(2,1)S(1)}, u32[]{:S(2)}, u32[]{:S(2)}) collective-permute-start(bf16[512,256]{1,0:T(8,128)(2,1)S(1)} %collective-permute-done.16.refs_1_), channel_id=1, source_target_pairs={{0,2},{2,0},{4,6},{6,4},{8,10},{10,8},{12,14},{14,12},{16,18},{18,... | collective-permute-start | bytes 786440 | tf_op jit(solution)/shard_map/ppermute | solution.py:462
  86.2 2.0 %collective-permute-start.27 = (bf16[512,256]{1,0:T(8,128)(2,1)S(1)}, bf16[512,256]{1,0:T(8,128)(2,1)S(1)}, u32[]{:S(2)}, u32[]{:S(2)}) collective-permute-start(bf16[512,256]{1,0:T(8,128)(2,1)S(1)} %shard_map.105.refs_0_), channel_id=1, source_target_pairs={{0,2},{2,0},{4,6},{6,4},{8,10},{10,8},{12,14},{14,12},{16,18},{18,... | collective-permute-start | bytes 786440 | tf_op jit(solution)/shard_map/ppermute | solution.py:462
  86.2 3.0 %collective-permute-start.17 = (bf16[512,256]{1,0:T(8,128)(2,1)S(1)}, bf16[512,256]{1,0:T(8,128)(2,1)S(1)}, u32[]{:S(2)}, u32[]{:S(2)}) collective-permute-start(bf16[512,256]{1,0:T(8,128)(2,1)S(1)} %collective-permute-done.15.refs_0_), channel_id=1, source_target_pairs={{0,2},{2,0},{4,6},{6,4},{8,10},{10,8},{12,14},{14,12},{16,18},{18,... | collective-permute-start | bytes 786440 | tf_op jit(solution)/shard_map/ppermute | solution.py:462
  86.7 2.5 %collective-permute-start.19 = (bf16[512,256]{1,0:T(8,128)(2,1)S(1)}, bf16[512,256]{1,0:T(8,128)(2,1)S(1)}, u32[]{:S(2)}, u32[]{:S(2)}) collective-permute-start(bf16[512,256]{1,0:T(8,128)(2,1)S(1)} %collective-permute-done.18.refs_1_), channel_id=1, source_target_pairs={{0,2},{2,0},{4,6},{6,4},{8,10},{10,8},{12,14},{14,12},{16,18},{18,... | collective-permute-start | bytes 786440 | tf_op jit(solution)/shard_map/ppermute | solution.py:462

commit v3 on v2

--- a/solution.py
+++ b/solution.py
@@ -12,6 +12,7 @@
 f32 = jnp.float32
 bf16 = jnp.bfloat16
 MIB = 1 << 20
+C = dict(meet=0, merge=0, collect=1, place=0, nsend=1, mfar=0, farland=0, ztie=1, ctie=1, nmerge=0, nmeet=0, place1=0, sp2=0, ncol=0, ytime=0, nlate=2, rtie=1, one=1, yfirst=0)
 
 
 def nt(a, b):
@@ -49,8 +50,8 @@
     )(*args)
 
 
-def cost(flops, nbytes):
-    return pl.CostEstimate(flops=1, bytes_accessed=1, transcendentals=0)
+def cost(us):
+    return pl.CostEstimate(flops=int(us * 1.1e9), bytes_accessed=1, transcendentals=0)
 
 
 def anywhere(items):
@@ -73,7 +74,7 @@
         self.pair = 2 * self.share
         self.deep = min(4, self.chips)
         self.wide = self.chips // self.deep
-        self.rows = steps * self.pair
+        self.slots = 2 * self.groups + 2
 
 
 def turn(t):
@@ -86,11 +87,17 @@
     return r, half, turn(2 * (r % 2) + half)
 
 
+def fetched(p, g, q, r, mine):
+    if g:
+        return (4 * g) ^ turn(q) ^ mine, q // 2
+    return q, 0
+
+
 def fetch_kernel(p, ids_ref, own_ref, oth_ref, tot_own_ref, tot_oth_ref, *msgs):
     r, half, mine = position()
     lines = p.steps * p.owners * 8
     group = 128 // p.owners
-    count = 2 * len(msgs)
+    count = p.slots
     hi, lo = split_index(ids_ref[...].reshape(lines, 128), p.block)
     sub = iota((p.pair, 128), 0)
     lane = iota((p.pair, 128), 1)
@@ -104,8 +111,9 @@
     slot = iota((lines, 128), 1)
     step_ok = line // (p.owners * 8) == slot // count
     dest = (line // 8) % p.owners
-    mask = (4 * ((slot % count) // 2)) ^ mine
-    route = ones_where(step_ok & (dest == (r ^ (2 * mask + slot % 2))))
+    e = slot % count
+    far = 2 * ((4 * (e // 2 - 1)) ^ mine) + e % 2
+    route = ones_where(step_ok & (dest == (r ^ jnp.where(e < 4, 2 * e, far))))
 
     def column(digit):
         picked = jnp.where(keep, nt(pick, digit), 0.0).astype(bf16)
@@ -130,19 +138,27 @@
             rows = nn(onehot, tables[jj][...]).astype(bf16)
             logs = logs + jnp.where(log_row == s * 2 + jj, nt(table_log, onehot), 0.0)
             for e in range(count):
-                at = e % 2 * p.rows + s * p.pair + jj * p.share
-                msgs[e // 2][at : at + p.share, :] = rows[e * p.share : (e + 1) * p.share, :]
-    for g, msg in enumerate(msgs):
-        tile = (2 * g * p.share) // 128 * 128
-        msg[2 * p.rows : 2 * p.rows + 16, :128] = logs[:, tile : tile + 128].astype(bf16)
-        msg[2 * p.rows : 2 * p.rows + 16, 128:] = jnp.zeros((16, p.width - 128), bf16)
+                piece = rows[e * p.share : (e + 1) * p.share, :]
+                if e < 4:
+                    msg, at = msgs[e], s * p.pair
+                else:
+                    msg, at = msgs[2 + e // 2], (e % 2 * p.steps + s) * p.pair
+                msg[at + jj * p.share : at + (jj + 1) * p.share, :] = piece
+    for k, msg in enumerate(msgs):
+        e = k if k < 4 else 2 * k - 4
+        tile = (e * p.share) // 128 * 128
+        end = msg.shape[0] - 16
+        wide = min(128, count * p.share - tile)
+        msg[end : end + 16, :] = jnp.zeros((16, p.width), bf16)
+        msg[end : end + 16, :wide] = logs[:, tile : tile + wide].astype(bf16)
 
 
 def fetch(p, ids, own, oth, tot_own, tot_oth):
-    outs = [jax.ShapeDtypeStruct((2 * p.rows + 16, p.width), bf16)] * p.groups
+    n = p.steps * p.pair
+    outs = [jax.ShapeDtypeStruct((k * n + 16, p.width), bf16) for k in [1] * 4 + [2] * (p.groups - 1)]
     return kernel_call(
         functools.partial(fetch_kernel, p), outs, ids, own, oth, tot_own, tot_oth, vmem=12,
-        cost=cost(4 * 2 * 256 * 1024 * 256, 4 * MIB),
+        cost=cost(3),
     )
 
 
@@ -209,7 +225,25 @@
     return kernel_call(
         functools.partial(columns_kernel, p), outs, *args, *after, vmem=12,
         in_specs=in_vmem(args) + anywhere(after),
-        cost=cost(2 * 2 * 1024 * 1024 * 256, 2 * MIB),
+        cost=cost(3),
+    )
+
+
+def pack_kernel(n, a_ref, b_ref, out_ref):
+    out_ref[:n, :] = a_ref[n : 2 * n, :]
+    out_ref[n : 2 * n, :] = b_ref[n : 2 * n, :]
+    if out_ref.shape[0] > 2 * n:
+        out_ref[2 * n : 2 * n + 16, :] = a_ref[2 * n :, :]
+        out_ref[2 * n + 16 :, :] = b_ref[2 * n :, :]
+
+
+def pack(a, b):
+    rows, width = a.shape
+    more = rows % 32
+    n = (rows - more) // 2
+    return kernel_call(
+        functools.partial(pack_kernel, n), jax.ShapeDtypeStruct((2 * n + 2 * more, width), bf16), a, b, vmem=12,
+        cost=cost(0),
     )
 
 
@@ -232,7 +266,8 @@
         for g in range(p.groups):
             for q in range(4):
                 for jj in range(2):
-                    owner = r ^ (2 * ((4 * g) ^ turn(q) ^ mine) + (jj ^ (q // 2)))
+                    mask, swapped = fetched(p, g, q, r, mine)
+                    owner = r ^ (2 * mask + (jj ^ swapped))
                     x = buf_ref[k % slots, pl.ds(owner, p.share, stride=p.owners), :].astype(f32)
                     safe = jnp.maximum(x, 1.0)
                     root = safe * lax.rsqrt(safe)
@@ -252,84 +287,108 @@
             pltpu.VMEM((slots, counts.shape[1], 128), jnp.int32),
             pltpu.SemaphoreType.DMA((slots,)),
         ],
-        cost=cost(40 * counts.size / 2, 12 * counts.size / 2),
-    )
-
-
-def grads_kernel(p, scale, first, has_acc, *refs):
-    msgs = refs[:4]
-    cols_ref, col_logs_ref = refs[4:6]
-    factor_refs = refs[6 : 6 + 2 * p.steps]
-    outs, acc_ref = refs[-4:-1], refs[-1]
-    before = refs[6 + 2 * p.steps] if has_acc else None
-    targets = [(outs[0], 0), (outs[2], 0), (outs[1], 0), (outs[2], p.rows)]
+        cost=cost(0),
+    )
+
+
+def grads_kernel(p, scale, g, steps, *refs):
+    n = len(steps)
+    m = 3 if g else 4
+    msgs, refs = refs[:m], refs[m:]
+    size = n * p.pair
+    if g:
+        here, there, crossed = msgs
+        sources = [(here, 0, 2 * size), (there, 0, 2 * size), (crossed, 0, 2 * size), (crossed, size, 2 * size + 16)]
+    else:
+        sources = [(msg, 0, size) for msg in msgs]
+    cols_ref, col_logs_ref = refs[:2]
+    factor_refs = refs[2 : 2 + 2 * n]
+    outs, acc_refs, rows_ref = refs[-4 - n : -1 - n], refs[-1 - n : -1], refs[-1]
+    befores = refs[2 + 2 * n : 2 + 3 * n] if g else None
+    r, half, mine = position()
+    targets = [(outs[0], 0), (outs[2], 0), (outs[1], 0), (outs[2], n * p.pair)]
     group = max(1, 256 // p.pair)
-    for s in range(p.steps):
+    for i, s in enumerate(steps):
         cols = cols_ref[s]
         col_logs = col_logs_ref[s : s + 1, :] - log_total
         for q0 in range(0, 4, group):
             members = range(q0, min(q0 + group, 4))
             pieces, row_logs = [], []
             for q in members:
-                lo = q // 2 * p.rows + s * p.pair
-                pieces.append(msgs[q][lo : lo + p.pair, :])
-                logs = msgs[q][2 * p.rows : 2 * p.rows + 16, :128].astype(f32).T
-                off = ((first // 2 + q // 2) * p.share) % 128
+                msg, lo, end = sources[q]
+                lo += i * p.pair
+                pieces.append(msg[lo : lo + p.pair, :])
+                logs = msg[end : end + 16, :128].astype(f32).T
+                e = 2 * (g + 1) + q // 2 if g else q
+                off = (e * p.share) % 128
                 for jj in range(2):
                     row_logs.append(logs[off : off + p.share, s * 2 + jj : s * 2 + jj + 1])
             x = jnp.concatenate(pieces, axis=0)
             rows = x.shape[0]
             z = nt(x, cols) + (jnp.concatenate(row_logs, axis=0) + col_logs)
-            at = (first + q0) * p.pair
-            gain = factor_refs[2 * s][at : at + rows, :]
-            fitted = gain * (z - factor_refs[2 * s + 1][at : at + rows, :])
+            at = (4 * g + q0) * p.pair
+            gain = factor_refs[2 * i][at : at + rows, :]
+            fitted = gain * (z - factor_refs[2 * i + 1][at : at + rows, :])
             hinge = (0.5 * scale) * jnp.tanh(0.5 * z) + (0.5 * scale)
             weights = jnp.where(gain > 0.0, fitted, hinge).astype(bf16)
-            g = nn(weights, cols)
-            for k, q in enumerate(members):
-                out, lo = targets[q]
-                lo += s * p.pair
-                out[lo : lo + p.pair, :] = g[k * p.pair : (k + 1) * p.pair].astype(out.dtype)
+            got = nn(weights, cols)
+            if g:
+                for k, q in enumerate(members):
+                    out, lo = targets[q]
+                    lo += i * p.pair
+                    out[lo : lo + p.pair, :] = got[k * p.pair : (k + 1) * p.pair].astype(out.dtype)
+            else:
+                rows_ref[q0 * p.pair : q0 * p.pair + rows, :] = got
             c = tn(x, weights)
             if q0 == 0:
-                acc_ref[s] = before[s] + c if has_acc else c
+                acc_refs[i][...] = befores[i][...] + c if g else c
             else:
-                acc_ref[s] += c
-
-
-def grads(p, scale, first, msgs, cols, col_logs, factor, acc=None):
+                acc_refs[i][...] += c
+        if not g:
+            for q, (out, lo) in enumerate(targets):
+                mask = mine ^ turn(q)
+                for k in range(2):
+                    at = pl.multiple_of(mask * p.pair + (k ^ (q // 2)) * p.share, p.share)
+                    to = lo + i * p.pair + k * p.share
+                    out[to : to + p.share, :] = rows_ref[pl.ds(at, p.share), :].astype(out.dtype)
+
+
+def grads(p, scale, g, steps, msgs, cols, col_logs, factor, acc=()):
     block = cols.shape[1]
-    stay = jax.ShapeDtypeStruct((p.rows, p.width), f32)
-    outs = [stay, stay, jax.ShapeDtypeStruct((2 * p.rows, p.width), bf16)]
-    outs.append(jax.ShapeDtypeStruct((p.steps, p.width, block), f32))
-    args = (*msgs, cols, col_logs, *factor) + (() if acc is None else (acc,))
-    return kernel_call(
-        functools.partial(grads_kernel, p, scale, first, acc is not None), outs, *args, vmem=24,
-        cost=cost(3 * 2 * p.steps * 512 * 1024 * 256, 10 * MIB),
-    )
-
-
-def meet_kernel(p, own_ref, pass_ref, got_ref, *refs):
+    n = len(steps) * p.pair
+    stay = jax.ShapeDtypeStruct((n, p.width), f32)
+    outs = [stay, stay, jax.ShapeDtypeStruct((2 * n, p.width), bf16)]
+    outs += [jax.ShapeDtypeStruct((p.width, block), f32)] * len(steps)
+    args = (*msgs, cols, col_logs, *factor, *acc)
+    return kernel_call(
+        functools.partial(grads_kernel, p, scale, g, steps), outs, *args, vmem=14,
+        scratch_shapes=[pltpu.VMEM((4 * p.pair, p.width), f32)],
+        cost=cost(0),
+    )
+
+
+def meet_kernel(own_ref, pass_ref, got_ref, *refs):
     own_out, pass_out = refs[-2:]
-    own_out[...] = (own_ref[...] + got_ref[: p.rows, :].astype(f32)).astype(bf16)
-    pass_out[...] = (pass_ref[...] + got_ref[p.rows :, :].astype(f32)).astype(bf16)
-
-
-def meet(p, own, passed, got, after=()):
-    outs = [jax.ShapeDtypeStruct((p.rows, p.width), bf16)] * 2
+    n = own_ref.shape[0]
+    own_out[...] = (own_ref[...] + got_ref[:n, :].astype(f32)).astype(bf16)
+    pass_out[...] = (pass_ref[...] + got_ref[n:, :].astype(f32)).astype(bf16)
+
+
+def meet(own, passed, got, after=()):
+    outs = [jax.ShapeDtypeStruct(own.shape, bf16)] * 2
     args = (own, passed, got)
     return kernel_call(
-        functools.partial(meet_kernel, p), outs, *args, *after, vmem=12,
-        in_specs=in_vmem(args) + anywhere(after), cost=cost(MIB, 2 * MIB),
+        meet_kernel, outs, *args, *after, vmem=12, in_specs=in_vmem(args) + anywhere(after), cost=cost(C['meet'])
     )
 
 
 def merge_kernel(p, own_ref, core_ref, *refs):
     out = refs[-1]
+    n = own_ref.shape[0]
     for d in range(2):
-        for s in range(p.steps):
-            src = slice(s * p.pair + d * p.share, s * p.pair + (d + 1) * p.share)
-            lo = d * p.rows + s * p.pair
+        for at in range(0, n, p.pair):
+            src = slice(at + d * p.share, at + (d + 1) * p.share)
+            lo = d * n + at
             out[lo : lo + p.share, :] = own_ref[src, :]
             out[lo + p.share : lo + p.pair, :] = core_ref[src, :]
 
@@ -337,68 +396,98 @@
 def merge(p, own, core, after=()):
     args = (own, core)
     return kernel_call(
-        functools.partial(merge_kernel, p), jax.ShapeDtypeStruct((2 * p.rows, p.width), bf16), *args, *after,
-        vmem=12, in_specs=in_vmem(args) + anywhere(after), cost=cost(MIB, 2 * MIB),
-    )
-
-
-def collect_kernel(p, first, has_acc, index_ref, *refs):
+        functools.partial(merge_kernel, p),
+        jax.ShapeDtypeStruct((2 * own.shape[0], p.width), bf16), *args, *after,
+        vmem=12, in_specs=in_vmem(args) + anywhere(after), cost=cost(C['merge']),
+    )
+
+
+def collect_kernel(p, first, steps, has_acc, index_ref, *refs):
     msgs, out_ref = refs[:2], refs[-1]
+    bases = (0, first % 4 // 2)
     items = iota((p.block, p.pair), 0)
     total = refs[2][...] if has_acc else None
-    base = first % 4 // 2 * p.rows
-    for s in range(p.steps):
-        at = [(first + i) * p.steps + s for i in range(2)]
+    for i, s in enumerate(steps):
+        at = [(first + k) * p.steps + s for k in range(2)]
         onehot = jnp.concatenate([ones_where(items == index_ref[k : k + 1, :]) for k in at], axis=1)
-        lo = base + s * p.pair
-        rows = jnp.concatenate([m[lo : lo + p.pair, :] for m in msgs], axis=0)
+        lo = [(base * len(steps) + i) * p.pair for base in bases]
+        rows = jnp.concatenate([m[k : k + p.pair, :] for m, k in zip(msgs, lo)], axis=0)
         term = nn(onehot, rows)
         total = term if total is None else total + term
     out_ref[...] = total
 
 
-def collect(p, first, index, msgs, acc=None):
+def collect(p, first, steps, index, msgs, acc=None):
     args = (index, *msgs) + (() if acc is None else (acc,))
     return kernel_call(
-        functools.partial(collect_kernel, p, first, acc is not None),
+        functools.partial(collect_kernel, p, first, steps, acc is not None),
         jax.ShapeDtypeStruct((p.block, p.width), f32), *args, vmem=12,
-        cost=cost(2 * 1024 * 512 * 256, 2 * MIB),
-    )
-
-
-def place_kernel(p, ids_ref, sum_ref, mine_ref, other_ref, acc_ref):
+        cost=cost(C['collect']),
+    )
+
+
+def finish_kernel(p, first, steps, index_ref, a_ref, b_ref, acc_ref, mine_ref, other_ref, rows_ref, cols_ref):
+    half = mine_ref.shape[0]
+    core = lax.axis_index("row") % 2
+    cols_ref[pl.ds(pl.multiple_of(core * half, half), half), :] = mine_ref[...].astype(f32)
+    cols_ref[pl.ds(pl.multiple_of((1 - core) * half, half), half), :] = other_ref[...].astype(f32)
+    collect_kernel(p, first, steps, True, index_ref, a_ref, b_ref, acc_ref, rows_ref)
+
+
+def finish(p, first, steps, index, msgs, acc, mine, other):
+    outs = [
+        jax.ShapeDtypeStruct((p.block, p.width), f32),
+        jax.ShapeDtypeStruct((2 * mine.shape[0], p.width), f32),
+    ]
+    return kernel_call(
+        functools.partial(finish_kernel, p, first, steps), outs, index, *msgs, acc, mine, other, vmem=16,
+        cost=cost(0),
+    )
+
+
+def place_kernel(step, final, ids_ref, sum_ref, *refs):
     r = lax.axis_index("row")
-    block = sum_ref.shape[2]
+    block = sum_ref.shape[1]
     local = ids_ref[...] & (block - 1)
     items = iota((block, block), 0)
-    for s in range(p.steps):
-        total = sum_ref[s]
-        top = total.astype(bf16)
-        rest = (total - top.astype(f32)).astype(bf16)
-        onehot = ones_where(items == local[s : s + 1, :])
-        term = nt(onehot, top) + nt(onehot, rest)
-        if s == 0:
-            acc_ref[...] = term
-        else:
-            acc_ref[...] += term
+    total = sum_ref[...]
+    top = total.astype(bf16)
+    rest = (total - top.astype(f32)).astype(bf16)
+    onehot = ones_where(items == local[step : step + 1, :])
+    term = nt(onehot, top) + nt(onehot, rest)
+    if step:
+        term = term + refs[0][...]
+    if not final:
+        refs[-1][...] = term
+        return
+    mine_ref, top_ref, rest_ref, acc_ref = refs[-4:]
+    acc_ref[...] = term
     part = block // 2
     mine_ref[...] = acc_ref[pl.ds(pl.multiple_of((r % 2) * part, part), part), :]
-    other_ref[...] = acc_ref[pl.ds(pl.multiple_of((1 - r % 2) * part, part), part), :]
-
-
-def place(p, ids, sums):
-    width, block = sums.shape[1:]
-    out = jax.ShapeDtypeStruct((block // 2, width), f32)
-    return kernel_call(
-        functools.partial(place_kernel, p), [out, out], ids, sums, vmem=12,
-        scratch_shapes=[pltpu.VMEM((block, width), f32)],
-        cost=cost(4 * 2 * 1024 * 1024 * 256, 5 * MIB),
-    )
-
-
-def spread_kernel(parts, stride, count, *refs):
+    other = acc_ref[pl.ds(pl.multiple_of((1 - r % 2) * part, part), part), :]
+    top_ref[...] = other.astype(bf16)
+    rest_ref[...] = (other - other.astype(bf16).astype(f32)).astype(bf16)
+
+
+def place(step, final, ids, sums, acc=(), after=()):
+    width, block = sums.shape
+    if final:
+        outs = [jax.ShapeDtypeStruct((block // 2, width), kind) for kind in (f32, bf16, bf16)]
+        scratch = [pltpu.VMEM((block, width), f32)]
+    else:
+        outs = [jax.ShapeDtypeStruct((block, width), f32)]
+        scratch = []
+    return kernel_call(
+        functools.partial(place_kernel, step, final), outs, ids, sums, *acc, *after, vmem=12,
+        in_specs=in_vmem((ids, sums, *acc)) + anywhere(after),
+        scratch_shapes=scratch,
+        cost=cost(C['place']),
+    )
+
+
+def spread_kernel(parts, stride, count, after, *refs):
     mine, arrived = refs[0], refs[1 : 1 + count]
-    outs, acc_ref = refs[1 + count : -1], refs[-1]
+    outs, acc_ref = refs[1 + count + after : -1], refs[-1]
     here = (lax.axis_index("row") // stride) % parts
     total = mine[...]
     for a in arrived:
@@ -410,14 +499,15 @@
         out[...] = acc_ref[pl.ds(at, size), :].astype(out.dtype)
 
 
-def spread(parts, stride, mine, arrived):
+def spread(parts, stride, mine, arrived, after=()):
     rows, width = mine.shape
     size = rows // parts
     outs = [jax.ShapeDtypeStruct((size, width), bf16 if (parts == 1 or k) else f32) for k in range(parts)]
     return kernel_call(
-        functools.partial(spread_kernel, parts, stride, len(arrived)), outs, mine, *arrived, vmem=16,
+        functools.partial(spread_kernel, parts, stride, len(arrived), len(after)), outs, mine, *arrived, *after,
+        vmem=16, in_specs=in_vmem((mine, *arrived)) + anywhere(after),
         scratch_shapes=[pltpu.VMEM((rows, width), f32)],
-        cost=cost(MIB, MIB),
+        cost=cost(0),
     )
 
 
@@ -426,7 +516,7 @@
 
 
 def add(a, b):
-    return kernel_call(add_kernel, jax.ShapeDtypeStruct(a.shape, a.dtype), a, b, vmem=12, cost=cost(MIB, MIB))
+    return kernel_call(add_kernel, jax.ShapeDtypeStruct(a.shape, a.dtype), a, b, vmem=12, cost=cost(0))
 
 
 def gather_kernel(parts, stride, *refs):
@@ -445,7 +535,7 @@
     return kernel_call(
         functools.partial(gather_kernel, parts, stride),
         jax.ShapeDtypeStruct((parts * rows, width), dtype), *pieces, vmem=16,
-        cost=cost(MIB, MIB),
+        cost=cost(0),
     )
 
 
@@ -481,52 +571,96 @@
     ids = row_ids.reshape(steps, owners * block // 128, 128)
     totals = row_totals.reshape(1, block)
     msgs = fetch(p, ids, row_emb, row_swap(row_emb, 1), totals, row_swap(totals, 1))
-    got = [carry(m, g) for g, m in enumerate(msgs)]
+    far = [carry(msgs[3 + g], g) for g in range(1, p.groups)]
+    near = [msgs[0]] + [row_swap(msgs[k], 2 * k) for k in range(1, 4)]
     cols, col_logs, index = columns(
         p, col_ids, col_emb, col_totals.reshape(1, block_cols), ids, (msgs[0],)
     )
 
+    every = tuple(range(steps))
     factor = []
-    last = col_logs
-    landed = [None] * p.groups
-    for s in range(steps):
-        factor += factors(p, scale, counts, s, (last,), 44 if s == 0 else 38)
-        last = factor[-1]
-        for g in range(p.groups):
-            if s == min(g, steps - 1):
-                here = tie(got[g], last)
-                landed[g] = (here, col_swap(here))
-
-    acc = None
-    ready = None
-    arrived = None
+    last = (col_logs,)
+    for s in every:
+        factor += factors(p, scale, counts, s, last, 44 if s == 0 else 38)
+        last = (factor[-1],)
+        if s == C['ytime']:
+            far = [tie(x, factor[-1], *near[1:]) for x in far]
+            last = (*last, *far)
+    near[1] = tie(near[1], *last)
+
+    *term, acc0, acc1 = grads(p, scale, 0, every, near, cols, col_logs, factor)
+    terms = [term]
+    sums = [acc0, acc1]
+    crossed = []
+    for g in range(1, p.groups):
+        here = far[g - 1]
+        there = tie(col_swap(here), acc0)
+        crossed.append(there)
+        four = (here, there, row_swap(pack(here, there), 1))
+        *term, acc0, acc1 = grads(p, scale, g, every, four, cols, col_logs, factor, sums)
+        sums = [acc0, acc1]
+        terms.append(term)
+
+    def pick(flag, *xs):
+        return xs if flag else ()
+
+    met = [col_swap(t[2] if g or not C['nsend'] else tie(t[2], *crossed)) for g, t in enumerate(terms)]
+    placed = ()
+    for s in every:
+        final = s + 1 == steps
+        placed = place(
+            s, final, col_ids, sums[s], placed,
+            pick(final and C['place1'] & 1, met[0]) + pick(final and C['place1'] & 2, met[-1]),
+        )
+    mine, *rest = placed
+    mine, *others = spread(p.wide, 2, mine, [row_swap(x, 1) for x in rest])
+
+    end = p.groups - 1
+    both = [None] * p.groups
+    for g in (range(end, -1, -1) if C['nmeet'] else range(p.groups)):
+        own, passed, _ = terms[g]
+        both[g] = meet(
+            own, passed, met[g], pick(g and C['mfar'] == 1, mine) + pick(not g and C['nmeet'], both[-1] and both[-1][0]) + pick(not g and C['nlate'] == 1, sums[0]) + pick(not g and C['nlate'] == 2, placed[0])
+        )
+    parcels = [None] * p.groups
+    for g in (range(end, -1, -1) if C['nmerge'] else range(p.groups)):
+        own, passed = both[g]
+        parcels[g] = merge(
+            p, own, row_swap(passed, 1), pick(g and C['mfar'] == 2, mine) + pick(not g and C['nmerge'], parcels[-1])
+        )
+    (piece,) = spread(
+        1, 1, mine, [row_swap(o, (k + 1) * 2) for k, o in enumerate(others)], pick(C['sp2'], parcels[-1])
+    )
+
     rows = None
-    end = p.groups - 1
+    there = None
     for g in range(p.groups):
-        here, there = landed[g]
-        four = (here, there, row_swap(here, 1), row_swap(there, 1))
-        own, passed, send, acc = grads(p, scale, 4 * g, four, cols, col_logs, factor, acc)
-        own, passed = meet(p, own, passed, col_swap(send), () if ready is None else (ready,))
-        ready = merge(p, own, row_swap(passed, 1), () if arrived is None else (arrived,))
-        arrived = carry(ready, g)
-        if g == end:
-            arrived = tie(arrived, there_back) if g else arrived
-            far_landed = arrived
-        there_back = col_swap(arrived)
-        for k, pair in enumerate(((arrived, there_back), (row_swap(arrived, 1), row_swap(there_back, 1)))):
-            rows = collect(p, 4 * g + 2 * k, index, pair, rows)
-
-    mine, other = place(p, col_ids, acc)
-    mine, *others = spread(p.wide, 2, mine, [row_swap(other, 1)])
-    (piece,) = spread(1, 1, mine, [row_swap(o, (k + 1) * 2) for k, o in enumerate(others)])
+        here = carry(parcels[g], g)
+        if g and C['farland']:
+            here = tie(here, there, *pick(C['ncol'], rows))
+        there = col_swap(here)
+        rows = collect(p, 4 * g, every, index, (here, there), rows)
+        other = pack(here, there)
+        if C['rtie'] and g == end:
+            other = tie(other, early)
+        other = row_swap(other, 1)
+        early = rows
+        if g < end or not C['one']:
+            rows = early = collect(p, 4 * g + 2, every, index, (other, other), rows)
+
     stride = 2 * p.wide
     while stride < owners:
         piece = add(piece, row_swap(piece, stride))
         stride *= 2
-    piece = tie(piece, far_landed)
+    if C['ztie']:
+        piece = tie(piece, here)
     piece = gather(2, [piece] + [row_swap(piece, k * 2) for k in range(1, p.wide)])
-    piece = tie(piece, there_back)
-    grad_cols = gather(1, [piece, row_swap(piece, 1)], f32)
+    if C['ctie']:
+        piece = tie(piece, there)
+    if C['one']:
+        rows, grad_cols = finish(p, 4 * end + 2, every, index, (other, other), rows, piece, row_swap(piece, 1))
+    else:
+        grad_cols = gather(1, [piece, row_swap(piece, 1)], f32)
 
     if cols_n > 2:
         total = rows

time: 91.2 us -> 83.9 us (0.920)
  waiting for transfers between devices: 34.6 us -> 28.8 us
  local copies, waits for them, and re-layouts: 7.26 us -> 2.65 us
  starting transfers between devices: 23.6 us -> 26.2 us
    ppermute x6 -> x5, waiting for transfers between devices: 13.3 us -> 3.22 us  [col_swap(): return lax.ppermute(x, 'col', [(i, i ^ mask) for i in range(cols_n)])]
    ppermute x18 -> x17, starting transfers between devices: 8.99 us -> 14.1 us  [row_swap(): return lax.ppermute(x, 'row', [(i, i ^ mask) for i in range(owners)])]
    unnamed x17 -> x11, local copies, waits for them, and re-layouts: 7.26 us -> 2.65 us
    ppermute x6 -> x5, starting transfers between devices: 8.83 us -> 5.22 us  [col_swap(): return lax.ppermute(x, 'col', [(i, i ^ mask) for i in range(cols_n)])]
    ppermute x18 -> x17, waiting for transfers between devices: 16.9 us -> 19.4 us  [row_swap(): return lax.ppermute(x, 'row', [(i, i ^ mask) for i in range(owners)])]
    ppermute x4 -> x3, waiting for transfers between devices: 4.45 us -> 6.2 us  [grid_swap(): return lax.ppermute(x, ('row', 'col'), perm)]
    ppermute x4 -> x3, starting transfers between devices: 5.78 us -> 6.85 us  [grid_swap(): return lax.ppermute(x, ('row', 'col'), perm)]
    pallas_call x21 -> x24, Pallas kernels: 24.3 us -> 25.1 us  [kernel_call(): pl.pallas_call(body, out_shape=outs, compiler_params=pltpu.CompilerParams...]
  transfers between devices with their start and end apart: 28 -> 25, of which waited for: 10 -> 10; matrix products, arithmetic and copies ran while one was open for 1% -> 1% of each run, Pallas kernels for 23% -> 25%
where the time goes in v3:
time: 83.9 us; the launch traced here: 83.6 us
  waiting for transfers between devices  28.8 us (34%)
  starting transfers between devices  26.2 us (31%)
  Pallas kernels  25.1 us (30%)
  local copies, waits for them, and re-layouts  2.65 us (3%)
  between operations  0.86 us (1%)
    pallas_call x24, Pallas kernels, kernel_call(): pl.pallas_call(body, out_shape=outs, compiler_params=pltpu.CompilerParams...  25.1 us
    ppermute x17, waiting for transfers between devices, row_swap(): return lax.ppermute(x, 'row', [(i, i ^ mask) for i in range(owners)])  19.4 us
    ppermute x17, starting transfers between devices, row_swap(): return lax.ppermute(x, 'row', [(i, i ^ mask) for i in range(owners)])  14.1 us
    ppermute x3, starting transfers between devices, grid_swap(): return lax.ppermute(x, ('row', 'col'), perm)  6.85 us
    ppermute x3, waiting for transfers between devices, grid_swap(): return lax.ppermute(x, ('row', 'col'), perm)  6.2 us
    ppermute x5, starting transfers between devices, col_swap(): return lax.ppermute(x, 'col', [(i, i ^ mask) for i in range(cols_n)])  5.22 us
    ppermute x5, waiting for transfers between devices, col_swap(): return lax.ppermute(x, 'col', [(i, i ^ mask) for i in range(cols_n)])  3.22 us
    unnamed x11, local copies, waits for them, and re-layouts  2.65 us
  transfers between devices with their start and end apart: 25, of which 10 were waited for; matrix products, arithmetic and copies ran while one was open for 1% of the time, Pallas kernels for 25%

profile of v3, /device:TPU:0, one launch (start us, length us, event | category | flops | bytes accessed | tf_op | source)
XLA Modules:
  0.0 83.6 jit_solution(14799251650547382954)
XLA Ops:
  0.6 0.5 collective-permute-start
  1.1 0.1 collective-permute-start.1
  1.2 0.9 %copy.11 = s32[1,2,128,128]{3,2,1,0:T(8,128)S(1)} copy(s32[1,2,128,128]{3,1,2,0:T(2,128)} %bitcast.11) | data formatting | bytes 262144
  2.1 0.8 collective-permute-done.1.tot_oth_ref
  2.9 1.0 %copy-done.1 = bf16[1024,256]{1,0:T(8,128)(2,1)S(1)} copy-done((bf16[1024,256]{1,0:T(8,128)(2,1)S(1)}, bf16[1024,256]{1,0:T(8,128)(2,1)}, u32[]{:S(2)}) %copy-start.1) | copy-done | bytes 524312
  3.9 0.7 copy-done.3
  4.6 2.3 %shard_map.86 = (bf16[272,256]{1,0:T(8,128)(2,1)S(1)}, bf16[272,256]{1,0:T(8,128)(2,1)S(1)}, bf16[272,256]{1,0:T(8,128)(2,1)S(1)}, bf16[272,256]{1,0:T(8,128)(2,1)S(1)}, bf16[528,256]{1,0:T(8,128)(2,1)S(1)}) custom-call(s32[2,128,128]{2,1,0:T(8,128)S(1)} %bitcast.6, bf16[1024,256]{1,0:T(8,128)(2,1)S(1)} %copy-done.1, ...), custom_call_target="tpu_custom_call" | custom-call | flops 3300000000 | bytes 1 | tf_op jit(solution)/shard_map/pallas_call | solution.py:44
  6.9 2.9 %collective-permute-start.3 = (bf16[272,256]{1,0:T(8,128)(2,1)S(1)}, bf16[272,256]{1,0:T(8,128)(2,1)S(1)}, u32[]{:S(2)}, u32[]{:S(2)}) collective-permute-start(bf16[272,256]{1,0:T(8,128)(2,1)S(1)} %get-tuple-element.45), channel_id=1, source_target_pairs={{0,4},{2,6},{4,0},{6,2},{8,12},{10,14},{12,8},{14,10},{16,20},{18,... | collective-permute-start | bytes 417800 | tf_op jit(solution)/shard_map/ppermute | solution.py:552
  9.8 1.6 %collective-permute-start.4 = (bf16[272,256]{1,0:T(8,128)(2,1)S(1)}, bf16[272,256]{1,0:T(8,128)(2,1)S(1)}, u32[]{:S(2)}, u32[]{:S(2)}) collective-permute-start(bf16[272,256]{1,0:T(8,128)(2,1)S(1)} %get-tuple-element.46), channel_id=1, source_target_pairs={{0,8},{2,10},{4,12},{6,14},{8,0},{10,2},{12,4},{14,6},{16,24},{18,... | collective-permute-start | bytes 417800 | tf_op jit(solution)/shard_map/ppermute | solution.py:552
  11.4 3.0 %collective-permute-start.2 = (bf16[528,256]{1,0:T(8,128)(2,1)S(1)}, bf16[528,256]{1,0:T(8,128)(2,1)S(1)}, u32[]{:S(2)}, u32[]{:S(2)}) collective-permute-start(bf16[528,256]{1,0:T(8,128)(2,1)S(1)} %get-tuple-element.42), channel_id=1, source_target_pairs={{0,16},{1,25},{2,30},{3,23},{4,20},{5,29},{6,26},{7,19},{8,24},{9,... | collective-permute-start | bytes 811016 | tf_op jit(solution)/shard_map/ppermute | solution.py:563
  14.4 2.9 %shard_map.87 = (bf16[2,1024,256]{2,1,0:T(8,128)(2,1)S(1)}, f32[8,1024]{1,0:T(8,128)S(1)}, s32[16,128]{1,0:T(8,128)S(1)}) custom-call(s32[2,1024]{1,0:T(2,128)S(1)} %copy-done, bf16[1024,256]{1,0:T(8,128)(2,1)S(1)} %copy-done.2, s32[1,1024]{1,0:T(1,128)S(1)} %bitcast.10, s32[2,128,128]{2,1,0:T(8,128)S(1)} %bitcast.7, ...), custom_call_target="tpu_custom_call" | custom-call | flops 3300000000 | bytes 1 | tf_op jit(solution)/shard_map/pallas_call | solution.py:44
  17.3 3.7 %shard_map.88 = (f32[1024,1024]{1,0:T(8,128)S(1)}, f32[1024,1024]{1,0:T(8,128)S(1)}) custom-call(s32[2,1024,1024]{2,1,0:T(8,128)} %counts_ref.3, f32[8,1024]{1,0:T(8,128)S(1)} %get-tuple-element.43.refs_0_.refs_5_.refs_4_), custom_call_target="tpu_custom_call" | custom-call | bytes 1 | tf_op jit(solution)/shard_map/pallas_call | solution.py:44
  21.1 6.2 %collective-permute-done.2.refs_1_.a_ref.refs_0_ = bf16[528,256]{1,0:T(8,128)(2,1)S(1)} collective-permute-done((bf16[528,256]{1,0:T(8,128)(2,1)S(1)}, bf16[528,256]{1,0:T(8,128)(2,1)S(1)}, u32[]{:S(2)}, u32[]{:S(2)}) %collective-permute-start.2) | collective-permute-done | bytes 270368 | tf_op jit(solution)/shard_map/ppermute | solution.py:563
  27.3 0.4 collective-permute-start.6
  27.7 3.7 %shard_map.89 = (f32[1024,1024]{1,0:T(8,128)S(1)}, f32[1024,1024]{1,0:T(8,128)S(1)}) custom-call(s32[2,1024,1024]{2,1,0:T(8,128)} %counts_ref.3, f32[1024,1024]{1,0:T(8,128)S(1)} %get-tuple-element.44.refs_0_.refs_7_.refs_6_, bf16[528,256]{1,0:T(8,128)(2,1)S(1)} %collective-permute-done.2.refs_1_.a_ref.refs_0_), custom_call_target="tpu_custom_call" | custom-call | bytes 1 | tf_op jit(solution)/shard_map/pallas_call | solution.py:44
  31.4 3.2 %shard_map.90 = (f32[256,256]{1,0:T(8,128)S(1)}, f32[256,256]{1,0:T(8,128)S(1)}, bf16[512,256]{1,0:T(8,128)(2,1)S(1)}, f32[256,1024]{1,0:T(8,128)S(1)}, f32[256,1024]{1,0:T(8,128)S(1)}) custom-call(bf16[272,256]{1,0:T(8,128)(2,1)S(1)} %get-tuple-element.40.refs_0_, bf16[272,256]{1,0:T(8,128)(2,1)S(1)} %collective-permute-done.3.refs_1_, ...), custom_call_target="tpu_custom_call" | custom-call | bytes 1 | tf_op jit(solution)/shard_map/pallas_call | solution.py:44
  34.7 0.1 collective-permute-start.7
  34.8 1.6 %collective-permute-start.12 = (bf16[512,256]{1,0:T(8,128)(2,1)S(1)}, bf16[512,256]{1,0:T(8,128)(2,1)S(1)}, u32[]{:S(2)}, u32[]{:S(2)}) collective-permute-start(bf16[512,256]{1,0:T(8,128)(2,1)S(1)} %get-tuple-element.65), channel_id=1, source_target_pairs={{0,1},{1,0},{2,3},{3,2},{4,5},{5,4},{6,7},{7,6},{8,9},{9,8},{10,11... | collective-permute-start | bytes 786440 | tf_op jit(solution)/shard_map/ppermute | solution.py:555
  36.4 3.0 %shard_map.92 = (f32[256,256]{1,0:T(8,128)S(1)}, f32[256,256]{1,0:T(8,128)S(1)}, bf16[512,256]{1,0:T(8,128)(2,1)S(1)}, f32[256,1024]{1,0:T(8,128)S(1)}, f32[256,1024]{1,0:T(8,128)S(1)}) custom-call(bf16[528,256]{1,0:T(8,128)(2,1)S(1)} %collective-permute-done.2.refs_1_.a_ref.refs_0_, bf16[528,256]{1,0:T(8,128)(2,1)S(1)} %collective-permute-done.6.b_ref.refs_1_, ...), custom_call_target="tpu_custom_call" | custom-call | bytes 1 | tf_op jit(solution)/shard_map/pallas_call | solution.py:44
  39.4 1.5 %collective-permute-start.8 = (bf16[512,256]{1,0:T(8,128)(2,1)S(1)}, bf16[512,256]{1,0:T(8,128)(2,1)S(1)}, u32[]{:S(2)}, u32[]{:S(2)}) collective-permute-start(bf16[512,256]{1,0:T(8,128)(2,1)S(1)} %get-tuple-element.59), channel_id=1, source_target_pairs={{0,1},{1,0},{2,3},{3,2},{4,5},{5,4},{6,7},{7,6},{8,9},{9,8},{10,11... | collective-permute-start | bytes 786440 | tf_op jit(solution)/shard_map/ppermute | solution.py:555
  40.9 1.3 %shard_map.96.refs_0_ = f32[1024,256]{1,0:T(8,128)S(1)} custom-call(s32[2,1024]{1,0:T(2,128)S(1)} %copy-done, f32[256,1024]{1,0:T(8,128)S(1)} %get-tuple-element.67.sum_ref), custom_call_target="tpu_custom_call" | custom-call | bytes 1 | tf_op jit(solution)/shard_map/pallas_call | solution.py:44
  42.2 1.5 %shard_map.97 = (f32[512,256]{1,0:T(8,128)S(1)}, bf16[512,256]{1,0:T(8,128)(2,1)S(1)}, bf16[512,256]{1,0:T(8,128)(2,1)S(1)}) custom-call(s32[2,1024]{1,0:T(2,128)S(1)} %copy-done, f32[256,1024]{1,0:T(8,128)S(1)} %get-tuple-element.66.sum_ref, f32[1024,256]{1,0:T(8,128)S(1)} %shard_map.96.refs_0_), custom_call_target="tpu_custom_call" | custom-call | bytes 1 | tf_op jit(solution)/shard_map/pallas_call | solution.py:44
  43.7 0.2 collective-permute-done.12.got_ref
  44.1 0.5 collective-permute-start.18
  44.6 0.1 collective-permute-start.19
  44.6 0.8 collective-permute-done.13.core_ref
  45.4 0.7 collective-permute-start.14
  46.1 3.0 %collective-permute-done.8.got_ref = bf16[512,256]{1,0:T(8,128)(2,1)S(1)} collective-permute-done((bf16[512,256]{1,0:T(8,128)(2,1)S(1)}, bf16[512,256]{1,0:T(8,128)(2,1)S(1)}, u32[]{:S(2)}, u32[]{:S(2)}) %collective-permute-start.8) | collective-permute-done | bytes 262176 | tf_op jit(solution)/shard_map/ppermute | solution.py:555
  49.1 0.1 collective-permute-start.9
  49.3 0.2 shard_map.104
  49.5 1.1 %collective-permute-start.20 = (bf16[256,256]{1,0:T(8,128)(2,1)S(1)}, bf16[256,256]{1,0:T(8,128)(2,1)S(1)}, u32[]{:S(2)}, u32[]{:S(2)}) collective-permute-start(bf16[256,256]{1,0:T(8,128)(2,1)S(1)} %get-tuple-element.75), channel_id=1, source_target_pairs={{0,4},{2,6},{4,0},{6,2},{8,12},{10,14},{12,8},{14,10},{16,20},{18,... | collective-permute-start | bytes 393224 | tf_op jit(solution)/shard_map/ppermute | solution.py:552
  50.6 3.2 %collective-permute-start.10 = (bf16[512,256]{1,0:T(8,128)(2,1)S(1)}, bf16[512,256]{1,0:T(8,128)(2,1)S(1)}, u32[]{:S(2)}, u32[]{:S(2)}) collective-permute-start(bf16[512,256]{1,0:T(8,128)(2,1)S(1)} %shard_map.94), channel_id=1, source_target_pairs={{0,16},{1,25},{2,30},{3,23},{4,20},{5,29},{6,26},{7,19},{8,24},{9,... | collective-permute-start | bytes 786440 | tf_op jit(solution)/shard_map/ppermute | solution.py:563
  53.8 1.5 %collective-permute-start.15 = (bf16[512,256]{1,0:T(8,128)(2,1)S(1)}, bf16[512,256]{1,0:T(8,128)(2,1)S(1)}, u32[]{:S(2)}, u32[]{:S(2)}) collective-permute-start(bf16[512,256]{1,0:T(8,128)(2,1)S(1)} %collective-permute-done.14.a_ref.refs_0_), channel_id=1, source_target_pairs={{0,1},{1,0},{2,3},{3,2},{4,5},{5,4},{6,7},{7,6},{8,9},{9,8},{10,11... | collective-permute-start | bytes 786440 | tf_op jit(solution)/shard_map/ppermute | solution.py:555
  55.2 1.9 %collective-permute-done.20.refs_1_ = bf16[256,256]{1,0:T(8,128)(2,1)S(1)} collective-permute-done((bf16[256,256]{1,0:T(8,128)(2,1)S(1)}, bf16[256,256]{1,0:T(8,128)(2,1)S(1)}, u32[]{:S(2)}, u32[]{:S(2)}) %collective-permute-start.20) | collective-permute-done | bytes 131104 | tf_op jit(solution)/shard_map/ppermute | solution.py:552
  57.2 1.9 %collective-permute-start.21 = (bf16[256,256]{1,0:T(8,128)(2,1)S(1)}, bf16[256,256]{1,0:T(8,128)(2,1)S(1)}, u32[]{:S(2)}, u32[]{:S(2)}) collective-permute-start(bf16[256,256]{1,0:T(8,128)(2,1)S(1)} %shard_map.105.a_ref), channel_id=1, source_target_pairs={{0,8},{2,10},{4,12},{6,14},{8,0},{10,2},{12,4},{14,6},{16,24},{18,... | collective-permute-start | bytes 393224 | tf_op jit(solution)/shard_map/ppermute | solution.py:552
  59.1 6.0 %collective-permute-done.21.b_ref = bf16[256,256]{1,0:T(8,128)(2,1)S(1)} collective-permute-done((bf16[256,256]{1,0:T(8,128)(2,1)S(1)}, bf16[256,256]{1,0:T(8,128)(2,1)S(1)}, u32[]{:S(2)}, u32[]{:S(2)}) %collective-permute-start.21) | collective-permute-done | bytes 131104 | tf_op jit(solution)/shard_map/ppermute | solution.py:552
  65.1 3.2 %collective-permute-start.22 = (bf16[256,256]{1,0:T(8,128)(2,1)S(1)}, bf16[256,256]{1,0:T(8,128)(2,1)S(1)}, u32[]{:S(2)}, u32[]{:S(2)}) collective-permute-start(bf16[256,256]{1,0:T(8,128)(2,1)S(1)} %shard_map.106.a_ref), channel_id=1, source_target_pairs={{0,16},{2,18},{4,20},{6,22},{8,24},{10,26},{12,28},{14,30},{16,0},... | collective-permute-start | bytes 393224 | tf_op jit(solution)/shard_map/ppermute | solution.py:552
  68.3 0.1 collective-permute-start.11
  68.6 5.9 %collective-permute-done.22.b_ref = bf16[256,256]{1,0:T(8,128)(2,1)S(1)} collective-permute-done((bf16[256,256]{1,0:T(8,128)(2,1)S(1)}, bf16[256,256]{1,0:T(8,128)(2,1)S(1)}, u32[]{:S(2)}, u32[]{:S(2)}) %collective-permute-start.22) | collective-permute-done | bytes 131104 | tf_op jit(solution)/shard_map/ppermute | solution.py:552
  74.5 1.2 %collective-permute-start.23 = (bf16[256,256]{1,0:T(8,128)(2,1)S(1)}, bf16[256,256]{1,0:T(8,128)(2,1)S(1)}, u32[]{:S(2)}, u32[]{:S(2)}) collective-permute-start(bf16[256,256]{1,0:T(8,128)(2,1)S(1)} %shard_map.107.refs_0_), channel_id=1, source_target_pairs={{0,4},{2,6},{4,0},{6,2},{8,12},{10,14},{12,8},{14,10},{16,20},{18,... | collective-permute-start | bytes 393224 | tf_op jit(solution)/shard_map/ppermute | solution.py:552
  75.7 0.4 shard_map.101.refs_2_
  76.2 3.4 %collective-permute-done.23.refs_1_ = bf16[256,256]{1,0:T(8,128)(2,1)S(1)} collective-permute-done((bf16[256,256]{1,0:T(8,128)(2,1)S(1)}, bf16[256,256]{1,0:T(8,128)(2,1)S(1)}, u32[]{:S(2)}, u32[]{:S(2)}) %collective-permute-start.23) | collective-permute-done | bytes 131104 | tf_op jit(solution)/shard_map/ppermute | solution.py:552
  79.6 0.1 collective-permute-start.24
  79.7 0.4 shard_map.102.refs_2_
  80.1 0.6 collective-permute-start.17
  80.7 0.4 shard_map.103.acc_ref
  81.2 0.7 collective-permute-done.17.a_ref.b_ref
  81.8 1.8 %shard_map.109 = (f32[1024,256]{1,0:T(8,128)}, f32[1024,256]{1,0:T(8,128)}) custom-call(s32[16,128]{1,0:T(8,128)S(1)} %get-tuple-element.41.index_ref, bf16[512,256]{1,0:T(8,128)(2,1)S(1)} %collective-permute-done.17.a_ref.b_ref, bf16[512,256]{1,0:T(8,128)(2,1)S(1)} %collective-permute-done.17.a_ref.b_ref, f32[1024,256]{1,0:T(8,128)S(1)} %shard_map.103.acc_ref, ...), custom_call_target="tpu_custom_call" | custom-call | bytes 1 | tf_op jit(solution)/shard_map/pallas_call | solution.py:44
  (37 shorter events, 0.6 us)
Async XLA Ops:
  0.6 2.3 %collective-permute-start = (bf16[1024,256]{1,0:T(8,128)(2,1)}, bf16[1024,256]{1,0:T(8,128)(2,1)S(1)}, u32[]{:S(2)}, u32[]{:S(2)}) collective-permute-start(bf16[1024,256]{1,0:T(8,128)(2,1)} %own_ref.1), channel_id=1, source_target_pairs={{0,2},{2,0},{4,6},{6,4},{8,10},{10,8},{12,14},{14,12},{16,18},{18,... | collective-permute-start | bytes 1572872 | tf_op jit(solution)/shard_map/ppermute | solution.py:552
  1.1 1.8 %collective-permute-start.1 = (s32[1,1024]{1,0:T(1,128)}, s32[1,1024]{1,0:T(1,128)S(1)}, u32[]{:S(2)}, u32[]{:S(2)}) collective-permute-start(s32[1,1024]{1,0:T(1,128)} %bitcast.8), channel_id=1, source_target_pairs={{0,2},{2,0},{4,6},{6,4},{8,10},{10,8},{12,14},{14,12},{16,18},{18,... | collective-permute-start | bytes 12296 | tf_op jit(solution)/shard_map/ppermute | solution.py:552
  2.9 1.0 %copy-start.1 = (bf16[1024,256]{1,0:T(8,128)(2,1)S(1)}, bf16[1024,256]{1,0:T(8,128)(2,1)}, u32[]{:S(2)}) copy-start(bf16[1024,256]{1,0:T(8,128)(2,1)} %own_ref.1) | copy-start | bytes 1572868
  3.9 0.7 copy-start.3
  4.6 9.8 %copy-start = (s32[2,1024]{1,0:T(2,128)S(1)}, s32[2,1024]{1,0:T(2,128)}, u32[]{:S(2)}) copy-start(s32[2,1024]{1,0:T(2,128)} %ids_ref.5) | copy-start | bytes 24580
  4.6 9.8 %copy-start.2 = (bf16[1024,256]{1,0:T(8,128)(2,1)S(1)}, bf16[1024,256]{1,0:T(8,128)(2,1)}, u32[]{:S(2)}) copy-start(bf16[1024,256]{1,0:T(8,128)(2,1)} %emb_ref.1) | copy-start | bytes 1572868
  4.6 9.8 %copy-start.4 = (s32[1024]{0:T(1024)S(1)}, s32[1024]{0:T(1024)}, u32[]{:S(2)}) copy-start(s32[1024]{0:T(1024)} %param.11) | copy-start | bytes 12292
  6.9 14.1 %collective-permute-start.3 = (bf16[272,256]{1,0:T(8,128)(2,1)S(1)}, bf16[272,256]{1,0:T(8,128)(2,1)S(1)}, u32[]{:S(2)}, u32[]{:S(2)}) collective-permute-start(bf16[272,256]{1,0:T(8,128)(2,1)S(1)} %get-tuple-element.45), channel_id=1, source_target_pairs={{0,4},{2,6},{4,0},{6,2},{8,12},{10,14},{12,8},{14,10},{16,20},{18,... | collective-permute-start | bytes 417800 | tf_op jit(solution)/shard_map/ppermute | solution.py:552
  9.8 11.2 %collective-permute-start.4 = (bf16[272,256]{1,0:T(8,128)(2,1)S(1)}, bf16[272,256]{1,0:T(8,128)(2,1)S(1)}, u32[]{:S(2)}, u32[]{:S(2)}) collective-permute-start(bf16[272,256]{1,0:T(8,128)(2,1)S(1)} %get-tuple-element.46), channel_id=1, source_target_pairs={{0,8},{2,10},{4,12},{6,14},{8,0},{10,2},{12,4},{14,6},{16,24},{18,... | collective-permute-start | bytes 417800 | tf_op jit(solution)/shard_map/ppermute | solution.py:552
  11.4 9.6 %collective-permute-start.5 = (bf16[272,256]{1,0:T(8,128)(2,1)S(1)}, bf16[272,256]{1,0:T(8,128)(2,1)S(1)}, u32[]{:S(2)}, u32[]{:S(2)}) collective-permute-start(bf16[272,256]{1,0:T(8,128)(2,1)S(1)} %get-tuple-element.47), channel_id=1, source_target_pairs={{0,12},{2,14},{4,8},{6,10},{8,4},{10,6},{12,0},{14,2},{16,28},{18,... | collective-permute-start | bytes 417800 | tf_op jit(solution)/shard_map/ppermute | solution.py:552
  11.4 15.8 %collective-permute-start.2 = (bf16[528,256]{1,0:T(8,128)(2,1)S(1)}, bf16[528,256]{1,0:T(8,128)(2,1)S(1)}, u32[]{:S(2)}, u32[]{:S(2)}) collective-permute-start(bf16[528,256]{1,0:T(8,128)(2,1)S(1)} %get-tuple-element.42), channel_id=1, source_target_pairs={{0,16},{1,25},{2,30},{3,23},{4,20},{5,29},{6,26},{7,19},{8,24},{9,... | collective-permute-start | bytes 811016 | tf_op jit(solution)/shard_map/ppermute | solution.py:563
  27.3 7.4 %collective-permute-start.6 = (bf16[528,256]{1,0:T(8,128)(2,1)S(1)}, bf16[528,256]{1,0:T(8,128)(2,1)S(1)}, u32[]{:S(2)}, u32[]{:S(2)}) collective-permute-start(bf16[528,256]{1,0:T(8,128)(2,1)S(1)} %collective-permute-done.2.refs_1_.a_ref.refs_0_), channel_id=1, source_target_pairs={{0,1},{1,0},{2,3},{3,2},{4,5},{5,4},{6,7},{7,6},{8,9},{9,8},{10,11... | collective-permute-start | bytes 811016 | tf_op jit(solution)/shard_map/ppermute | solution.py:555
  34.7 1.7 %collective-permute-start.7 = (bf16[544,256]{1,0:T(8,128)(2,1)S(1)}, bf16[544,256]{1,0:T(8,128)(2,1)S(1)}, u32[]{:S(2)}, u32[]{:S(2)}) collective-permute-start(bf16[544,256]{1,0:T(8,128)(2,1)S(1)} %shard_map.91), channel_id=1, source_target_pairs={{0,2},{2,0},{4,6},{6,4},{8,10},{10,8},{12,14},{14,12},{16,18},{18,... | collective-permute-start | bytes 835592 | tf_op jit(solution)/shard_map/ppermute | solution.py:552
  34.8 9.2 %collective-permute-start.12 = (bf16[512,256]{1,0:T(8,128)(2,1)S(1)}, bf16[512,256]{1,0:T(8,128)(2,1)S(1)}, u32[]{:S(2)}, u32[]{:S(2)}) collective-permute-start(bf16[512,256]{1,0:T(8,128)(2,1)S(1)} %get-tuple-element.65), channel_id=1, source_target_pairs={{0,1},{1,0},{2,3},{3,2},{4,5},{5,4},{6,7},{7,6},{8,9},{9,8},{10,11... | collective-permute-start | bytes 786440 | tf_op jit(solution)/shard_map/ppermute | solution.py:555
  39.4 9.7 %collective-permute-start.8 = (bf16[512,256]{1,0:T(8,128)(2,1)S(1)}, bf16[512,256]{1,0:T(8,128)(2,1)S(1)}, u32[]{:S(2)}, u32[]{:S(2)}) collective-permute-start(bf16[512,256]{1,0:T(8,128)(2,1)S(1)} %get-tuple-element.59), channel_id=1, source_target_pairs={{0,1},{1,0},{2,3},{3,2},{4,5},{5,4},{6,7},{7,6},{8,9},{9,8},{10,11... | collective-permute-start | bytes 786440 | tf_op jit(solution)/shard_map/ppermute | solution.py:555
  44.0 1.4 %collective-permute-start.13 = (bf16[256,256]{1,0:T(8,128)(2,1)S(1)}, bf16[256,256]{1,0:T(8,128)(2,1)S(1)}, u32[]{:S(2)}, u32[]{:S(2)}) collective-permute-start(bf16[256,256]{1,0:T(8,128)(2,1)S(1)} %get-tuple-element.70), channel_id=1, source_target_pairs={{0,2},{2,0},{4,6},{6,4},{8,10},{10,8},{12,14},{14,12},{16,18},{18,... | collective-permute-start | bytes 393224 | tf_op jit(solution)/shard_map/ppermute | solution.py:552
  44.1 5.2 %collective-permute-start.18 = (bf16[512,256]{1,0:T(8,128)(2,1)S(1)}, bf16[512,256]{1,0:T(8,128)(2,1)S(1)}, u32[]{:S(2)}, u32[]{:S(2)}) collective-permute-start(bf16[512,256]{1,0:T(8,128)(2,1)S(1)} %get-tuple-element.72), channel_id=1, source_target_pairs={{0,2},{2,0},{4,6},{6,4},{8,10},{10,8},{12,14},{14,12},{16,18},{18,... | collective-permute-start | bytes 786440 | tf_op jit(solution)/shard_map/ppermute | solution.py:552
  44.6 4.7 %collective-permute-start.19 = (bf16[512,256]{1,0:T(8,128)(2,1)S(1)}, bf16[512,256]{1,0:T(8,128)(2,1)S(1)}, u32[]{:S(2)}, u32[]{:S(2)}) collective-permute-start(bf16[512,256]{1,0:T(8,128)(2,1)S(1)} %get-tuple-element.73), channel_id=1, source_target_pairs={{0,2},{2,0},{4,6},{6,4},{8,10},{10,8},{12,14},{14,12},{16,18},{18,... | collective-permute-start | bytes 786440 | tf_op jit(solution)/shard_map/ppermute | solution.py:552
  45.4 8.3 %collective-permute-start.14 = (bf16[512,256]{1,0:T(8,128)(2,1)S(1)}, bf16[512,256]{1,0:T(8,128)(2,1)S(1)}, u32[]{:S(2)}, u32[]{:S(2)}) collective-permute-start(bf16[512,256]{1,0:T(8,128)(2,1)S(1)} %shard_map.99), channel_id=1, source_target_pairs={{0,0},{1,9},{2,14},{3,7},{4,4},{5,13},{6,10},{7,3},{8,8},{9,1},{10... | collective-permute-start | bytes 786440 | tf_op jit(solution)/shard_map/ppermute | solution.py:563
  49.1 1.4 %collective-permute-start.9 = (bf16[256,256]{1,0:T(8,128)(2,1)S(1)}, bf16[256,256]{1,0:T(8,128)(2,1)S(1)}, u32[]{:S(2)}, u32[]{:S(2)}) collective-permute-start(bf16[256,256]{1,0:T(8,128)(2,1)S(1)} %get-tuple-element.61), channel_id=1, source_target_pairs={{0,2},{2,0},{4,6},{6,4},{8,10},{10,8},{12,14},{14,12},{16,18},{18,... | collective-permute-start | bytes 393224 | tf_op jit(solution)/shard_map/ppermute | solution.py:552
  49.5 7.7 %collective-permute-start.20 = (bf16[256,256]{1,0:T(8,128)(2,1)S(1)}, bf16[256,256]{1,0:T(8,128)(2,1)S(1)}, u32[]{:S(2)}, u32[]{:S(2)}) collective-permute-start(bf16[256,256]{1,0:T(8,128)(2,1)S(1)} %get-tuple-element.75), channel_id=1, source_target_pairs={{0,4},{2,6},{4,0},{6,2},{8,12},{10,14},{12,8},{14,10},{16,20},{18,... | collective-permute-start | bytes 393224 | tf_op jit(solution)/shard_map/ppermute | solution.py:552
  50.6 17.8 %collective-permute-start.10 = (bf16[512,256]{1,0:T(8,128)(2,1)S(1)}, bf16[512,256]{1,0:T(8,128)(2,1)S(1)}, u32[]{:S(2)}, u32[]{:S(2)}) collective-permute-start(bf16[512,256]{1,0:T(8,128)(2,1)S(1)} %shard_map.94), channel_id=1, source_target_pairs={{0,16},{1,25},{2,30},{3,23},{4,20},{5,29},{6,26},{7,19},{8,24},{9,... | collective-permute-start | bytes 786440 | tf_op jit(solution)/shard_map/ppermute | solution.py:563
  53.8 14.7 %collective-permute-start.15 = (bf16[512,256]{1,0:T(8,128)(2,1)S(1)}, bf16[512,256]{1,0:T(8,128)(2,1)S(1)}, u32[]{:S(2)}, u32[]{:S(2)}) collective-permute-start(bf16[512,256]{1,0:T(8,128)(2,1)S(1)} %collective-permute-done.14.a_ref.refs_0_), channel_id=1, source_target_pairs={{0,1},{1,0},{2,3},{3,2},{4,5},{5,4},{6,7},{7,6},{8,9},{9,8},{10,11... | collective-permute-start | bytes 786440 | tf_op jit(solution)/shard_map/ppermute | solution.py:555
  57.2 7.9 %collective-permute-start.21 = (bf16[256,256]{1,0:T(8,128)(2,1)S(1)}, bf16[256,256]{1,0:T(8,128)(2,1)S(1)}, u32[]{:S(2)}, u32[]{:S(2)}) collective-permute-start(bf16[256,256]{1,0:T(8,128)(2,1)S(1)} %shard_map.105.a_ref), channel_id=1, source_target_pairs={{0,8},{2,10},{4,12},{6,14},{8,0},{10,2},{12,4},{14,6},{16,24},{18,... | collective-permute-start | bytes 393224 | tf_op jit(solution)/shard_map/ppermute | solution.py:552
  65.1 9.3 %collective-permute-start.22 = (bf16[256,256]{1,0:T(8,128)(2,1)S(1)}, bf16[256,256]{1,0:T(8,128)(2,1)S(1)}, u32[]{:S(2)}, u32[]{:S(2)}) collective-permute-start(bf16[256,256]{1,0:T(8,128)(2,1)S(1)} %shard_map.106.a_ref), channel_id=1, source_target_pairs={{0,16},{2,18},{4,20},{6,22},{8,24},{10,26},{12,28},{14,30},{16,0},... | collective-permute-start | bytes 393224 | tf_op jit(solution)/shard_map/ppermute | solution.py:552
  68.3 11.2 %collective-permute-start.11 = (bf16[512,256]{1,0:T(8,128)(2,1)S(1)}, bf16[512,256]{1,0:T(8,128)(2,1)S(1)}, u32[]{:S(2)}, u32[]{:S(2)}) collective-permute-start(bf16[512,256]{1,0:T(8,128)(2,1)S(1)} %collective-permute-done.10.a_ref.refs_0_), channel_id=1, source_target_pairs={{0,1},{1,0},{2,3},{3,2},{4,5},{5,4},{6,7},{7,6},{8,9},{9,8},{10,11... | collective-permute-start | bytes 786440 | tf_op jit(solution)/shard_map/ppermute | solution.py:555
  68.5 11.2 %collective-permute-start.16 = (bf16[512,256]{1,0:T(8,128)(2,1)S(1)}, bf16[512,256]{1,0:T(8,128)(2,1)S(1)}, u32[]{:S(2)}, u32[]{:S(2)}) collective-permute-start(bf16[512,256]{1,0:T(8,128)(2,1)S(1)} %shard_map.100), channel_id=1, source_target_pairs={{0,2},{2,0},{4,6},{6,4},{8,10},{10,8},{12,14},{14,12},{16,18},{18,... | collective-permute-start | bytes 786440 | tf_op jit(solution)/shard_map/ppermute | solution.py:552
  74.5 5.0 %collective-permute-start.23 = (bf16[256,256]{1,0:T(8,128)(2,1)S(1)}, bf16[256,256]{1,0:T(8,128)(2,1)S(1)}, u32[]{:S(2)}, u32[]{:S(2)}) collective-permute-start(bf16[256,256]{1,0:T(8,128)(2,1)S(1)} %shard_map.107.refs_0_), channel_id=1, source_target_pairs={{0,4},{2,6},{4,0},{6,2},{8,12},{10,14},{12,8},{14,10},{16,20},{18,... | collective-permute-start | bytes 393224 | tf_op jit(solution)/shard_map/ppermute | solution.py:552
  79.6 1.6 %collective-permute-start.24 = (bf16[512,256]{1,0:T(8,128)(2,1)S(1)}, bf16[512,256]{1,0:T(8,128)(2,1)S(1)}, u32[]{:S(2)}, u32[]{:S(2)}) collective-permute-start(bf16[512,256]{1,0:T(8,128)(2,1)S(1)} %shard_map.108.mine_ref), channel_id=1, source_target_pairs={{0,2},{2,0},{4,6},{6,4},{8,10},{10,8},{12,14},{14,12},{16,18},{18,... | collective-permute-start | bytes 786440 | tf_op jit(solution)/shard_map/ppermute | solution.py:552
  80.1 1.7 %collective-permute-start.17 = (bf16[512,256]{1,0:T(8,128)(2,1)S(1)}, bf16[512,256]{1,0:T(8,128)(2,1)S(1)}, u32[]{:S(2)}, u32[]{:S(2)}) collective-permute-start(bf16[512,256]{1,0:T(8,128)(2,1)S(1)} %shard_map.95), channel_id=1, source_target_pairs={{0,2},{2,0},{4,6},{6,4},{8,10},{10,8},{12,14},{14,12},{16,18},{18,... | collective-permute-start | bytes 786440 | tf_op jit(solution)/shard_map/ppermute | solution.py:552

commit v4 on v3

--- a/solution.py
+++ b/solution.py
@@ -12,7 +12,6 @@
 f32 = jnp.float32
 bf16 = jnp.bfloat16
 MIB = 1 << 20
-C = dict(meet=0, merge=0, collect=1, place=0, nsend=1, mfar=0, farland=0, ztie=1, ctie=1, nmerge=0, nmeet=0, place1=0, sp2=0, ncol=0, ytime=0, nlate=2, rtie=1, one=1, yfirst=0)
 
 
 def nt(a, b):
@@ -255,7 +254,7 @@
 
     def copy(k):
         src = counts_ref.at[step, :, pl.ds(k * 128, 128)]
-        return pltpu.make_async_copy(src, buf_ref.at[k % slots], sems.at[k % slots])
+        return pltpu.make_async_copy(src, buf_ref.at[k % slots, : p.block], sems.at[k % slots])
 
     for k in range(slots - 1):
         copy(k).start()
@@ -284,18 +283,18 @@
         functools.partial(factors_kernel, p, scale, step), [shape, shape], counts, *after, vmem=vmem,
         in_specs=anywhere((counts, *after)), out_specs=in_vmem((shape, shape)),
         scratch_shapes=[
-            pltpu.VMEM((slots, counts.shape[1], 128), jnp.int32),
+            pltpu.VMEM((slots, p.block + p.owners, 128), jnp.int32),
             pltpu.SemaphoreType.DMA((slots,)),
         ],
         cost=cost(0),
     )
 
 
-def grads_kernel(p, scale, g, steps, *refs):
+def grads_kernel(p, scale, g, steps, done, has_acc, *refs):
     n = len(steps)
+    size = p.steps * p.pair
     m = 3 if g else 4
     msgs, refs = refs[:m], refs[m:]
-    size = n * p.pair
     if g:
         here, there, crossed = msgs
         sources = [(here, 0, 2 * size), (there, 0, 2 * size), (crossed, 0, 2 * size), (crossed, size, 2 * size + 16)]
@@ -304,9 +303,17 @@
     cols_ref, col_logs_ref = refs[:2]
     factor_refs = refs[2 : 2 + 2 * n]
     outs, acc_refs, rows_ref = refs[-4 - n : -1 - n], refs[-1 - n : -1], refs[-1]
-    befores = refs[2 + 2 * n : 2 + 3 * n] if g else None
+    befores = refs[2 + 2 * n : 2 + 3 * n]
+    total = (done + n) * p.pair
+    if done:
+        old = done * p.pair
+        prior = refs[2 + (3 if has_acc else 2) * n :][:3]
+        outs[0][:old, :] = prior[0][...]
+        outs[1][:old, :] = prior[1][...]
+        outs[2][:old, :] = prior[2][:old, :]
+        outs[2][total : total + old, :] = prior[2][old:, :]
     r, half, mine = position()
-    targets = [(outs[0], 0), (outs[2], 0), (outs[1], 0), (outs[2], n * p.pair)]
+    targets = [(outs[0], 0), (outs[2], 0), (outs[1], 0), (outs[2], total)]
     group = max(1, 256 // p.pair)
     for i, s in enumerate(steps):
         cols = cols_ref[s]
@@ -316,7 +323,7 @@
             pieces, row_logs = [], []
             for q in members:
                 msg, lo, end = sources[q]
-                lo += i * p.pair
+                lo += s * p.pair
                 pieces.append(msg[lo : lo + p.pair, :])
                 logs = msg[end : end + 16, :128].astype(f32).T
                 e = 2 * (g + 1) + q // 2 if g else q
@@ -335,13 +342,13 @@
             if g:
                 for k, q in enumerate(members):
                     out, lo = targets[q]
-                    lo += i * p.pair
+                    lo += (done + i) * p.pair
                     out[lo : lo + p.pair, :] = got[k * p.pair : (k + 1) * p.pair].astype(out.dtype)
             else:
                 rows_ref[q0 * p.pair : q0 * p.pair + rows, :] = got
             c = tn(x, weights)
             if q0 == 0:
-                acc_refs[i][...] = befores[i][...] + c if g else c
+                acc_refs[i][...] = befores[i][...] + c if has_acc else c
             else:
                 acc_refs[i][...] += c
         if not g:
@@ -349,19 +356,20 @@
                 mask = mine ^ turn(q)
                 for k in range(2):
                     at = pl.multiple_of(mask * p.pair + (k ^ (q // 2)) * p.share, p.share)
-                    to = lo + i * p.pair + k * p.share
+                    to = lo + (done + i) * p.pair + k * p.share
                     out[to : to + p.share, :] = rows_ref[pl.ds(at, p.share), :].astype(out.dtype)
 
 
-def grads(p, scale, g, steps, msgs, cols, col_logs, factor, acc=()):
+def grads(p, scale, g, steps, msgs, cols, col_logs, factor, acc=(), prior=()):
     block = cols.shape[1]
-    n = len(steps) * p.pair
+    done = prior[0].shape[0] // p.pair if prior else 0
+    n = (done + len(steps)) * p.pair
     stay = jax.ShapeDtypeStruct((n, p.width), f32)
     outs = [stay, stay, jax.ShapeDtypeStruct((2 * n, p.width), bf16)]
     outs += [jax.ShapeDtypeStruct((p.width, block), f32)] * len(steps)
-    args = (*msgs, cols, col_logs, *factor, *acc)
-    return kernel_call(
-        functools.partial(grads_kernel, p, scale, g, steps), outs, *args, vmem=14,
+    args = (*msgs, cols, col_logs, *factor, *acc, *prior)
+    return kernel_call(
+        functools.partial(grads_kernel, p, scale, g, steps, done, bool(acc)), outs, *args, vmem=14,
         scratch_shapes=[pltpu.VMEM((4 * p.pair, p.width), f32)],
         cost=cost(0),
     )
@@ -374,11 +382,11 @@
     pass_out[...] = (pass_ref[...] + got_ref[n:, :].astype(f32)).astype(bf16)
 
 
-def meet(own, passed, got, after=()):
+def meet(own, passed, got, after):
     outs = [jax.ShapeDtypeStruct(own.shape, bf16)] * 2
     args = (own, passed, got)
     return kernel_call(
-        meet_kernel, outs, *args, *after, vmem=12, in_specs=in_vmem(args) + anywhere(after), cost=cost(C['meet'])
+        meet_kernel, outs, *args, *after, vmem=12, in_specs=in_vmem(args) + anywhere(after), cost=cost(0)
     )
 
 
@@ -398,7 +406,7 @@
     return kernel_call(
         functools.partial(merge_kernel, p),
         jax.ShapeDtypeStruct((2 * own.shape[0], p.width), bf16), *args, *after,
-        vmem=12, in_specs=in_vmem(args) + anywhere(after), cost=cost(C['merge']),
+        vmem=12, in_specs=in_vmem(args) + anywhere(after), cost=cost(0),
     )
 
 
@@ -422,7 +430,7 @@
     return kernel_call(
         functools.partial(collect_kernel, p, first, steps, acc is not None),
         jax.ShapeDtypeStruct((p.block, p.width), f32), *args, vmem=12,
-        cost=cost(C['collect']),
+        cost=cost(1),
     )
 
 
@@ -481,7 +489,7 @@
         functools.partial(place_kernel, step, final), outs, ids, sums, *acc, *after, vmem=12,
         in_specs=in_vmem((ids, sums, *acc)) + anywhere(after),
         scratch_shapes=scratch,
-        cost=cost(C['place']),
+        cost=cost(0),
     )
 
 
@@ -580,87 +588,61 @@
     every = tuple(range(steps))
     factor = []
     last = (col_logs,)
+    term = ()
+    sums = []
     for s in every:
         factor += factors(p, scale, counts, s, last, 44 if s == 0 else 38)
+        if s == 0:
+            *term, total = grads(p, scale, 0, (s,), near, cols, col_logs, factor)
+            sums.append(total)
         last = (factor[-1],)
-        if s == C['ytime']:
-            far = [tie(x, factor[-1], *near[1:]) for x in far]
+        if s == 0:
+            far = [tie(x, *(sums or last), *near[1:]) for x in far]
             last = (*last, *far)
     near[1] = tie(near[1], *last)
-
-    *term, acc0, acc1 = grads(p, scale, 0, every, near, cols, col_logs, factor)
-    terms = [term]
-    sums = [acc0, acc1]
+    rest = every[len(sums) :]
+    term = grads(p, scale, 0, rest, near, cols, col_logs, factor[2 * len(sums) :], (), tuple(term))
+    sums += term[3:]
+    terms = [term[:3]]
+    acc0 = sums[-1]
     crossed = []
     for g in range(1, p.groups):
         here = far[g - 1]
         there = tie(col_swap(here), acc0)
         crossed.append(there)
         four = (here, there, row_swap(pack(here, there), 1))
-        *term, acc0, acc1 = grads(p, scale, g, every, four, cols, col_logs, factor, sums)
-        sums = [acc0, acc1]
-        terms.append(term)
-
-    def pick(flag, *xs):
-        return xs if flag else ()
-
-    met = [col_swap(t[2] if g or not C['nsend'] else tie(t[2], *crossed)) for g, t in enumerate(terms)]
+        made = grads(p, scale, g, every, four, cols, col_logs, factor, tuple(sums))
+        terms.append(made[:3])
+        sums = made[3:]
+
+    met = [col_swap(t[2] if g else tie(t[2], *crossed)) for g, t in enumerate(terms)]
     placed = ()
     for s in every:
-        final = s + 1 == steps
-        placed = place(
-            s, final, col_ids, sums[s], placed,
-            pick(final and C['place1'] & 1, met[0]) + pick(final and C['place1'] & 2, met[-1]),
-        )
-    mine, *rest = placed
-    mine, *others = spread(p.wide, 2, mine, [row_swap(x, 1) for x in rest])
-
-    end = p.groups - 1
-    both = [None] * p.groups
-    for g in (range(end, -1, -1) if C['nmeet'] else range(p.groups)):
-        own, passed, _ = terms[g]
-        both[g] = meet(
-            own, passed, met[g], pick(g and C['mfar'] == 1, mine) + pick(not g and C['nmeet'], both[-1] and both[-1][0]) + pick(not g and C['nlate'] == 1, sums[0]) + pick(not g and C['nlate'] == 2, placed[0])
-        )
-    parcels = [None] * p.groups
-    for g in (range(end, -1, -1) if C['nmerge'] else range(p.groups)):
-        own, passed = both[g]
-        parcels[g] = merge(
-            p, own, row_swap(passed, 1), pick(g and C['mfar'] == 2, mine) + pick(not g and C['nmerge'], parcels[-1])
-        )
-    (piece,) = spread(
-        1, 1, mine, [row_swap(o, (k + 1) * 2) for k, o in enumerate(others)], pick(C['sp2'], parcels[-1])
-    )
-
-    rows = None
-    there = None
-    for g in range(p.groups):
-        here = carry(parcels[g], g)
-        if g and C['farland']:
-            here = tie(here, there, *pick(C['ncol'], rows))
-        there = col_swap(here)
-        rows = collect(p, 4 * g, every, index, (here, there), rows)
-        other = pack(here, there)
-        if C['rtie'] and g == end:
-            other = tie(other, early)
-        other = row_swap(other, 1)
-        early = rows
-        if g < end or not C['one']:
-            rows = early = collect(p, 4 * g + 2, every, index, (other, other), rows)
+        placed = place(s, s + 1 == steps, col_ids, sums[s], placed)
+    mine, *parts = placed
+    mine, *others = spread(p.wide, 2, mine, [row_swap(x, 1) for x in parts])
+    parcels = []
+    for g, (own, passed, _) in enumerate(terms):
+        own, passed = meet(own, passed, met[g], () if g else placed[:1])
+        parcels.append(merge(p, own, row_swap(passed, 1)))
+    (piece,) = spread(1, 1, mine, [row_swap(x, (k + 1) * 2) for k, x in enumerate(others)])
+    heres = [carry(x, g) for g, x in enumerate(parcels)]
+    theres = [col_swap(x) for x in heres]
 
     stride = 2 * p.wide
     while stride < owners:
         piece = add(piece, row_swap(piece, stride))
         stride *= 2
-    if C['ztie']:
-        piece = tie(piece, here)
     piece = gather(2, [piece] + [row_swap(piece, k * 2) for k in range(1, p.wide)])
-    if C['ctie']:
-        piece = tie(piece, there)
-    if C['one']:
-        rows, grad_cols = finish(p, 4 * end + 2, every, index, (other, other), rows, piece, row_swap(piece, 1))
-    else:
-        grad_cols = gather(1, [piece, row_swap(piece, 1)], f32)
+
+    rows = None
+    for g, (here, there) in enumerate(zip(heres, theres)):
+        rows = collect(p, 4 * g, every, index, (here, there), rows)
+        other = row_swap(pack(here, there), 1)
+        if g + 1 < p.groups:
+            rows = collect(p, 4 * g + 2, every, index, (other, other), rows)
+    last = 4 * p.groups - 2
+    rows, grad_cols = finish(p, last, every, index, (other, other), rows, piece, row_swap(piece, 1))
 
     if cols_n > 2:
         total = rows

time: 83.9 us -> 83.4 us (level)
  starting transfers between devices: 26.2 us -> 23.8 us
  waiting for transfers between devices: 28.8 us -> 30.4 us
    ppermute x5, waiting for transfers between devices: 3.22 us -> 5.58 us  [col_swap(): return lax.ppermute(x, 'col', [(i, i ^ mask) for i in range(cols_n)])]
    ppermute x5, starting transfers between devices: 5.22 us -> 3.08 us  [col_swap(): return lax.ppermute(x, 'col', [(i, i ^ mask) for i in range(cols_n)])]
    ppermute x3, waiting for transfers between devices: 6.2 us -> 4.55 us  [grid_swap(): return lax.ppermute(x, ('row', 'col'), perm)]
    ppermute x17, waiting for transfers between devices: 19.4 us -> 20.3 us  [row_swap(): return lax.ppermute(x, 'row', [(i, i ^ mask) for i in range(owners)])]
    pallas_call x24 -> x25, Pallas kernels: 25.1 us -> 25.4 us  [kernel_call(): pl.pallas_call(body, out_shape=outs, compiler_params=pltpu.CompilerParams...]
  transfers between devices with their start and end apart: 25 -> 25, of which waited for: 10 -> 11; matrix products, arithmetic and copies ran while one was open for 1% -> 1% of each run, Pallas kernels for 25% -> 26%
where the time goes in v4:
time: 83.4 us; the launch traced here: 83.1 us
  waiting for transfers between devices  30.4 us (36%)
  Pallas kernels  25.4 us (30%)
  starting transfers between devices  23.8 us (29%)
  local copies, waits for them, and re-layouts  2.65 us (3%)
  between operations  0.88 us (1%)
    pallas_call x25, Pallas kernels, kernel_call(): pl.pallas_call(body, out_shape=outs, compiler_params=pltpu.CompilerParams...  25.4 us
    ppermute x17, waiting for transfers between devices, row_swap(): return lax.ppermute(x, 'row', [(i, i ^ mask) for i in range(owners)])  20.3 us
    ppermute x17, starting transfers between devices, row_swap(): return lax.ppermute(x, 'row', [(i, i ^ mask) for i in range(owners)])  14 us
    ppermute x3, starting transfers between devices, grid_swap(): return lax.ppermute(x, ('row', 'col'), perm)  6.76 us
    ppermute x5, waiting for transfers between devices, col_swap(): return lax.ppermute(x, 'col', [(i, i ^ mask) for i in range(cols_n)])  5.58 us
    ppermute x3, waiting for transfers between devices, grid_swap(): return lax.ppermute(x, ('row', 'col'), perm)  4.55 us
    ppermute x5, starting transfers between devices, col_swap(): return lax.ppermute(x, 'col', [(i, i ^ mask) for i in range(cols_n)])  3.08 us
    unnamed x11, local copies, waits for them, and re-layouts  2.65 us
  transfers between devices with their start and end apart: 25, of which 11 were waited for; matrix products, arithmetic and copies ran while one was open for 1% of the time, Pallas kernels for 26%

profile of v4, /device:TPU:0, one launch (start us, length us, event | category | flops | bytes accessed | tf_op | source)
XLA Modules:
  0.0 83.1 jit_solution(17344144879531113395)
XLA Ops:
  0.6 0.5 collective-permute-start
  1.1 0.1 collective-permute-start.1
  1.2 0.9 %copy.11 = s32[1,2,128,128]{3,2,1,0:T(8,128)S(1)} copy(s32[1,2,128,128]{3,1,2,0:T(2,128)} %bitcast.11) | data formatting | bytes 262144
  2.1 0.8 collective-permute-done.1.tot_oth_ref
  2.9 1.0 %copy-done.1 = bf16[1024,256]{1,0:T(8,128)(2,1)S(1)} copy-done((bf16[1024,256]{1,0:T(8,128)(2,1)S(1)}, bf16[1024,256]{1,0:T(8,128)(2,1)}, u32[]{:S(2)}) %copy-start.1) | copy-done | bytes 524312
  3.9 0.7 copy-done.3
  4.6 2.3 %shard_map.86 = (bf16[272,256]{1,0:T(8,128)(2,1)S(1)}, bf16[272,256]{1,0:T(8,128)(2,1)S(1)}, bf16[272,256]{1,0:T(8,128)(2,1)S(1)}, bf16[272,256]{1,0:T(8,128)(2,1)S(1)}, bf16[528,256]{1,0:T(8,128)(2,1)S(1)}) custom-call(s32[2,128,128]{2,1,0:T(8,128)S(1)} %bitcast.6, bf16[1024,256]{1,0:T(8,128)(2,1)S(1)} %copy-done.1, ...), custom_call_target="tpu_custom_call" | custom-call | flops 3300000000 | bytes 1 | tf_op jit(solution)/shard_map/pallas_call | solution.py:43
  6.9 2.9 %collective-permute-start.3 = (bf16[272,256]{1,0:T(8,128)(2,1)S(1)}, bf16[272,256]{1,0:T(8,128)(2,1)S(1)}, u32[]{:S(2)}, u32[]{:S(2)}) collective-permute-start(bf16[272,256]{1,0:T(8,128)(2,1)S(1)} %get-tuple-element.43), channel_id=1, source_target_pairs={{0,4},{2,6},{4,0},{6,2},{8,12},{10,14},{12,8},{14,10},{16,20},{18,... | collective-permute-start | bytes 417800 | tf_op jit(solution)/shard_map/ppermute | solution.py:560
  9.8 1.6 %collective-permute-start.4 = (bf16[272,256]{1,0:T(8,128)(2,1)S(1)}, bf16[272,256]{1,0:T(8,128)(2,1)S(1)}, u32[]{:S(2)}, u32[]{:S(2)}) collective-permute-start(bf16[272,256]{1,0:T(8,128)(2,1)S(1)} %get-tuple-element.44), channel_id=1, source_target_pairs={{0,8},{2,10},{4,12},{6,14},{8,0},{10,2},{12,4},{14,6},{16,24},{18,... | collective-permute-start | bytes 417800 | tf_op jit(solution)/shard_map/ppermute | solution.py:560
  11.4 3.0 %collective-permute-start.2 = (bf16[528,256]{1,0:T(8,128)(2,1)S(1)}, bf16[528,256]{1,0:T(8,128)(2,1)S(1)}, u32[]{:S(2)}, u32[]{:S(2)}) collective-permute-start(bf16[528,256]{1,0:T(8,128)(2,1)S(1)} %get-tuple-element.42), channel_id=1, source_target_pairs={{0,16},{1,25},{2,30},{3,23},{4,20},{5,29},{6,26},{7,19},{8,24},{9,... | collective-permute-start | bytes 811016 | tf_op jit(solution)/shard_map/ppermute | solution.py:571
  14.4 2.9 %shard_map.87 = (bf16[2,1024,256]{2,1,0:T(8,128)(2,1)S(1)}, f32[8,1024]{1,0:T(8,128)S(1)}, s32[16,128]{1,0:T(8,128)S(1)}) custom-call(s32[2,1024]{1,0:T(2,128)S(1)} %copy-done, bf16[1024,256]{1,0:T(8,128)(2,1)S(1)} %copy-done.2, s32[1,1024]{1,0:T(1,128)S(1)} %bitcast.10, s32[2,128,128]{2,1,0:T(8,128)S(1)} %bitcast.7, ...), custom_call_target="tpu_custom_call" | custom-call | flops 3300000000 | bytes 1 | tf_op jit(solution)/shard_map/pallas_call | solution.py:43
  17.3 3.7 %shard_map.88 = (f32[1024,1024]{1,0:T(8,128)S(1)}, f32[1024,1024]{1,0:T(8,128)S(1)}) custom-call(s32[2,1024,1024]{2,1,0:T(8,128)} %counts_ref.3, f32[8,1024]{1,0:T(8,128)S(1)} %get-tuple-element.47.refs_0_.refs_5_.refs_4_), custom_call_target="tpu_custom_call" | custom-call | bytes 1 | tf_op jit(solution)/shard_map/pallas_call | solution.py:43
  21.1 1.6 %shard_map.89 = (f32[128,256]{1,0:T(8,128)S(1)}, f32[128,256]{1,0:T(8,128)S(1)}, bf16[256,256]{1,0:T(8,128)(2,1)S(1)}, f32[256,1024]{1,0:T(8,128)S(1)}) custom-call(bf16[272,256]{1,0:T(8,128)(2,1)S(1)} %get-tuple-element.40.refs_0_, bf16[272,256]{1,0:T(8,128)(2,1)S(1)} %collective-permute-done.3.refs_1_, ...), custom_call_target="tpu_custom_call" | custom-call | bytes 1 | tf_op jit(solution)/shard_map/pallas_call | solution.py:43
  22.7 4.5 %collective-permute-done.2.refs_1_.a_ref.refs_0_ = bf16[528,256]{1,0:T(8,128)(2,1)S(1)} collective-permute-done((bf16[528,256]{1,0:T(8,128)(2,1)S(1)}, bf16[528,256]{1,0:T(8,128)(2,1)S(1)}, u32[]{:S(2)}, u32[]{:S(2)}) %collective-permute-start.2) | collective-permute-done | bytes 270368 | tf_op jit(solution)/shard_map/ppermute | solution.py:571
  27.3 0.4 collective-permute-start.6
  27.7 3.7 %shard_map.90 = (f32[1024,1024]{1,0:T(8,128)S(1)}, f32[1024,1024]{1,0:T(8,128)S(1)}) custom-call(s32[2,1024,1024]{2,1,0:T(8,128)} %counts_ref.3, f32[1024,1024]{1,0:T(8,128)S(1)} %get-tuple-element.49.refs_7_.refs_0_.refs_6_, bf16[528,256]{1,0:T(8,128)(2,1)S(1)} %collective-permute-done.2.refs_1_.a_ref.refs_0_), custom_call_target="tpu_custom_call" | custom-call | bytes 1 | tf_op jit(solution)/shard_map/pallas_call | solution.py:43
  31.4 1.8 %shard_map.91 = (f32[256,256]{1,0:T(8,128)S(1)}, f32[256,256]{1,0:T(8,128)S(1)}, bf16[512,256]{1,0:T(8,128)(2,1)S(1)}, f32[256,1024]{1,0:T(8,128)S(1)}) custom-call(bf16[272,256]{1,0:T(8,128)(2,1)S(1)} %get-tuple-element.40.refs_0_, bf16[272,256]{1,0:T(8,128)(2,1)S(1)} %collective-permute-done.3.refs_1_, ...), custom_call_target="tpu_custom_call" | custom-call | bytes 1 | tf_op jit(solution)/shard_map/pallas_call | solution.py:43
  33.2 1.4 %collective-permute-done.6.b_ref.refs_1_ = bf16[528,256]{1,0:T(8,128)(2,1)S(1)} collective-permute-done((bf16[528,256]{1,0:T(8,128)(2,1)S(1)}, bf16[528,256]{1,0:T(8,128)(2,1)S(1)}, u32[]{:S(2)}, u32[]{:S(2)}) %collective-permute-start.6) | collective-permute-done | bytes 270368 | tf_op jit(solution)/shard_map/ppermute | solution.py:563
  34.8 0.3 collective-permute-start.13
  35.1 1.2 %collective-permute-done.7.refs_2_ = bf16[544,256]{1,0:T(8,128)(2,1)S(1)} collective-permute-done((bf16[544,256]{1,0:T(8,128)(2,1)S(1)}, bf16[544,256]{1,0:T(8,128)(2,1)S(1)}, u32[]{:S(2)}, u32[]{:S(2)}) %collective-permute-start.7) | collective-permute-done | bytes 278560 | tf_op jit(solution)/shard_map/ppermute | solution.py:560
  36.3 3.0 %shard_map.93 = (f32[256,256]{1,0:T(8,128)S(1)}, f32[256,256]{1,0:T(8,128)S(1)}, bf16[512,256]{1,0:T(8,128)(2,1)S(1)}, f32[256,1024]{1,0:T(8,128)S(1)}, f32[256,1024]{1,0:T(8,128)S(1)}) custom-call(bf16[528,256]{1,0:T(8,128)(2,1)S(1)} %collective-permute-done.2.refs_1_.a_ref.refs_0_, bf16[528,256]{1,0:T(8,128)(2,1)S(1)} %collective-permute-done.6.b_ref.refs_1_, ...), custom_call_target="tpu_custom_call" | custom-call | bytes 1 | tf_op jit(solution)/shard_map/pallas_call | solution.py:43
  39.3 0.6 collective-permute-start.8
  40.0 1.3 %shard_map.97.refs_0_ = f32[1024,256]{1,0:T(8,128)S(1)} custom-call(s32[2,1024]{1,0:T(2,128)S(1)} %copy-done, f32[256,1024]{1,0:T(8,128)S(1)} %get-tuple-element.70.sum_ref), custom_call_target="tpu_custom_call" | custom-call | bytes 1 | tf_op jit(solution)/shard_map/pallas_call | solution.py:43
  41.2 1.5 %shard_map.98 = (f32[512,256]{1,0:T(8,128)S(1)}, bf16[512,256]{1,0:T(8,128)(2,1)S(1)}, bf16[512,256]{1,0:T(8,128)(2,1)S(1)}) custom-call(s32[2,1024]{1,0:T(2,128)S(1)} %copy-done, f32[256,1024]{1,0:T(8,128)S(1)} %get-tuple-element.69.sum_ref, f32[1024,256]{1,0:T(8,128)S(1)} %shard_map.97.refs_0_), custom_call_target="tpu_custom_call" | custom-call | bytes 1 | tf_op jit(solution)/shard_map/pallas_call | solution.py:43
  42.8 1.2 %collective-permute-done.13.got_ref = bf16[512,256]{1,0:T(8,128)(2,1)S(1)} collective-permute-done((bf16[512,256]{1,0:T(8,128)(2,1)S(1)}, bf16[512,256]{1,0:T(8,128)(2,1)S(1)}, u32[]{:S(2)}, u32[]{:S(2)}) %collective-permute-start.13) | collective-permute-done | bytes 262176 | tf_op jit(solution)/shard_map/ppermute | solution.py:563
  44.1 0.5 collective-permute-start.18
  44.6 0.1 collective-permute-start.19
  44.6 0.8 collective-permute-done.14.core_ref
  45.4 0.7 collective-permute-start.15
  46.1 3.0 %collective-permute-done.8.got_ref = bf16[512,256]{1,0:T(8,128)(2,1)S(1)} collective-permute-done((bf16[512,256]{1,0:T(8,128)(2,1)S(1)}, bf16[512,256]{1,0:T(8,128)(2,1)S(1)}, u32[]{:S(2)}, u32[]{:S(2)}) %collective-permute-start.8) | collective-permute-done | bytes 262176 | tf_op jit(solution)/shard_map/ppermute | solution.py:563
  49.1 0.1 collective-permute-start.9
  49.3 0.2 shard_map.105
  49.5 1.1 %collective-permute-start.20 = (bf16[256,256]{1,0:T(8,128)(2,1)S(1)}, bf16[256,256]{1,0:T(8,128)(2,1)S(1)}, u32[]{:S(2)}, u32[]{:S(2)}) collective-permute-start(bf16[256,256]{1,0:T(8,128)(2,1)S(1)} %get-tuple-element.77), channel_id=1, source_target_pairs={{0,4},{2,6},{4,0},{6,2},{8,12},{10,14},{12,8},{14,10},{16,20},{18,... | collective-permute-start | bytes 393224 | tf_op jit(solution)/shard_map/ppermute | solution.py:560
  50.6 3.1 %collective-permute-start.10 = (bf16[512,256]{1,0:T(8,128)(2,1)S(1)}, bf16[512,256]{1,0:T(8,128)(2,1)S(1)}, u32[]{:S(2)}, u32[]{:S(2)}) collective-permute-start(bf16[512,256]{1,0:T(8,128)(2,1)S(1)} %shard_map.95), channel_id=1, source_target_pairs={{0,16},{1,25},{2,30},{3,23},{4,20},{5,29},{6,26},{7,19},{8,24},{9,... | collective-permute-start | bytes 786440 | tf_op jit(solution)/shard_map/ppermute | solution.py:571
  53.7 1.4 %collective-permute-start.16 = (bf16[512,256]{1,0:T(8,128)(2,1)S(1)}, bf16[512,256]{1,0:T(8,128)(2,1)S(1)}, u32[]{:S(2)}, u32[]{:S(2)}) collective-permute-start(bf16[512,256]{1,0:T(8,128)(2,1)S(1)} %collective-permute-done.15.a_ref.refs_0_), channel_id=1, source_target_pairs={{0,1},{1,0},{2,3},{3,2},{4,5},{5,4},{6,7},{7,6},{8,9},{9,8},{10,11... | collective-permute-start | bytes 786440 | tf_op jit(solution)/shard_map/ppermute | solution.py:563
  55.1 2.0 %collective-permute-done.20.refs_1_ = bf16[256,256]{1,0:T(8,128)(2,1)S(1)} collective-permute-done((bf16[256,256]{1,0:T(8,128)(2,1)S(1)}, bf16[256,256]{1,0:T(8,128)(2,1)S(1)}, u32[]{:S(2)}, u32[]{:S(2)}) %collective-permute-start.20) | collective-permute-done | bytes 131104 | tf_op jit(solution)/shard_map/ppermute | solution.py:560
  57.2 1.7 %collective-permute-start.21 = (bf16[256,256]{1,0:T(8,128)(2,1)S(1)}, bf16[256,256]{1,0:T(8,128)(2,1)S(1)}, u32[]{:S(2)}, u32[]{:S(2)}) collective-permute-start(bf16[256,256]{1,0:T(8,128)(2,1)S(1)} %shard_map.106.a_ref), channel_id=1, source_target_pairs={{0,8},{2,10},{4,12},{6,14},{8,0},{10,2},{12,4},{14,6},{16,24},{18,... | collective-permute-start | bytes 393224 | tf_op jit(solution)/shard_map/ppermute | solution.py:560
  58.9 6.1 %collective-permute-done.21.b_ref = bf16[256,256]{1,0:T(8,128)(2,1)S(1)} collective-permute-done((bf16[256,256]{1,0:T(8,128)(2,1)S(1)}, bf16[256,256]{1,0:T(8,128)(2,1)S(1)}, u32[]{:S(2)}, u32[]{:S(2)}) %collective-permute-start.21) | collective-permute-done | bytes 131104 | tf_op jit(solution)/shard_map/ppermute | solution.py:560
  65.1 3.0 %collective-permute-start.22 = (bf16[256,256]{1,0:T(8,128)(2,1)S(1)}, bf16[256,256]{1,0:T(8,128)(2,1)S(1)}, u32[]{:S(2)}, u32[]{:S(2)}) collective-permute-start(bf16[256,256]{1,0:T(8,128)(2,1)S(1)} %shard_map.107.a_ref), channel_id=1, source_target_pairs={{0,16},{2,18},{4,20},{6,22},{8,24},{10,26},{12,28},{14,30},{16,0},... | collective-permute-start | bytes 393224 | tf_op jit(solution)/shard_map/ppermute | solution.py:560
  68.1 0.2 collective-permute-start.11
  68.4 5.8 %collective-permute-done.22.b_ref = bf16[256,256]{1,0:T(8,128)(2,1)S(1)} collective-permute-done((bf16[256,256]{1,0:T(8,128)(2,1)S(1)}, bf16[256,256]{1,0:T(8,128)(2,1)S(1)}, u32[]{:S(2)}, u32[]{:S(2)}) %collective-permute-start.22) | collective-permute-done | bytes 131104 | tf_op jit(solution)/shard_map/ppermute | solution.py:560
  74.2 1.5 %collective-permute-start.23 = (bf16[256,256]{1,0:T(8,128)(2,1)S(1)}, bf16[256,256]{1,0:T(8,128)(2,1)S(1)}, u32[]{:S(2)}, u32[]{:S(2)}) collective-permute-start(bf16[256,256]{1,0:T(8,128)(2,1)S(1)} %shard_map.108.refs_0_), channel_id=1, source_target_pairs={{0,4},{2,6},{4,0},{6,2},{8,12},{10,14},{12,8},{14,10},{16,20},{18,... | collective-permute-start | bytes 393224 | tf_op jit(solution)/shard_map/ppermute | solution.py:560
  75.7 3.6 %collective-permute-done.23.refs_1_ = bf16[256,256]{1,0:T(8,128)(2,1)S(1)} collective-permute-done((bf16[256,256]{1,0:T(8,128)(2,1)S(1)}, bf16[256,256]{1,0:T(8,128)(2,1)S(1)}, u32[]{:S(2)}, u32[]{:S(2)}) %collective-permute-start.23) | collective-permute-done | bytes 131104 | tf_op jit(solution)/shard_map/ppermute | solution.py:560
  79.4 0.5 collective-permute-start.12
  80.0 0.4 shard_map.102.refs_2_
  80.4 0.4 shard_map.103.refs_2_
  80.9 0.4 shard_map.104.acc_ref
  81.3 1.8 %shard_map.110 = (f32[1024,256]{1,0:T(8,128)}, f32[1024,256]{1,0:T(8,128)}) custom-call(s32[16,128]{1,0:T(8,128)S(1)} %get-tuple-element.41.index_ref, bf16[512,256]{1,0:T(8,128)(2,1)S(1)} %collective-permute-done.12.a_ref.b_ref, bf16[512,256]{1,0:T(8,128)(2,1)S(1)} %collective-permute-done.12.a_ref.b_ref, f32[1024,256]{1,0:T(8,128)S(1)} %shard_map.104.acc_ref, ...), custom_call_target="tpu_custom_call" | custom-call | bytes 1 | tf_op jit(solution)/shard_map/pallas_call | solution.py:43
  (38 shorter events, 0.6 us)
Async XLA Ops:
  0.6 2.3 %collective-permute-start = (bf16[1024,256]{1,0:T(8,128)(2,1)}, bf16[1024,256]{1,0:T(8,128)(2,1)S(1)}, u32[]{:S(2)}, u32[]{:S(2)}) collective-permute-start(bf16[1024,256]{1,0:T(8,128)(2,1)} %own_ref.1), channel_id=1, source_target_pairs={{0,2},{2,0},{4,6},{6,4},{8,10},{10,8},{12,14},{14,12},{16,18},{18,... | collective-permute-start | bytes 1572872 | tf_op jit(solution)/shard_map/ppermute | solution.py:560
  1.1 1.8 %collective-permute-start.1 = (s32[1,1024]{1,0:T(1,128)}, s32[1,1024]{1,0:T(1,128)S(1)}, u32[]{:S(2)}, u32[]{:S(2)}) collective-permute-start(s32[1,1024]{1,0:T(1,128)} %bitcast.8), channel_id=1, source_target_pairs={{0,2},{2,0},{4,6},{6,4},{8,10},{10,8},{12,14},{14,12},{16,18},{18,... | collective-permute-start | bytes 12296 | tf_op jit(solution)/shard_map/ppermute | solution.py:560
  2.9 1.0 %copy-start.1 = (bf16[1024,256]{1,0:T(8,128)(2,1)S(1)}, bf16[1024,256]{1,0:T(8,128)(2,1)}, u32[]{:S(2)}) copy-start(bf16[1024,256]{1,0:T(8,128)(2,1)} %own_ref.1) | copy-start | bytes 1572868
  3.9 0.7 copy-start.3
  4.6 9.8 %copy-start = (s32[2,1024]{1,0:T(2,128)S(1)}, s32[2,1024]{1,0:T(2,128)}, u32[]{:S(2)}) copy-start(s32[2,1024]{1,0:T(2,128)} %ids_ref.5) | copy-start | bytes 24580
  4.6 9.8 %copy-start.2 = (bf16[1024,256]{1,0:T(8,128)(2,1)S(1)}, bf16[1024,256]{1,0:T(8,128)(2,1)}, u32[]{:S(2)}) copy-start(bf16[1024,256]{1,0:T(8,128)(2,1)} %emb_ref.1) | copy-start | bytes 1572868
  4.6 9.8 %copy-start.4 = (s32[1024]{0:T(1024)S(1)}, s32[1024]{0:T(1024)}, u32[]{:S(2)}) copy-start(s32[1024]{0:T(1024)} %param.11) | copy-start | bytes 12292
  6.9 14.1 %collective-permute-start.3 = (bf16[272,256]{1,0:T(8,128)(2,1)S(1)}, bf16[272,256]{1,0:T(8,128)(2,1)S(1)}, u32[]{:S(2)}, u32[]{:S(2)}) collective-permute-start(bf16[272,256]{1,0:T(8,128)(2,1)S(1)} %get-tuple-element.43), channel_id=1, source_target_pairs={{0,4},{2,6},{4,0},{6,2},{8,12},{10,14},{12,8},{14,10},{16,20},{18,... | collective-permute-start | bytes 417800 | tf_op jit(solution)/shard_map/ppermute | solution.py:560
  9.8 11.2 %collective-permute-start.4 = (bf16[272,256]{1,0:T(8,128)(2,1)S(1)}, bf16[272,256]{1,0:T(8,128)(2,1)S(1)}, u32[]{:S(2)}, u32[]{:S(2)}) collective-permute-start(bf16[272,256]{1,0:T(8,128)(2,1)S(1)} %get-tuple-element.44), channel_id=1, source_target_pairs={{0,8},{2,10},{4,12},{6,14},{8,0},{10,2},{12,4},{14,6},{16,24},{18,... | collective-permute-start | bytes 417800 | tf_op jit(solution)/shard_map/ppermute | solution.py:560
  11.4 9.6 %collective-permute-start.5 = (bf16[272,256]{1,0:T(8,128)(2,1)S(1)}, bf16[272,256]{1,0:T(8,128)(2,1)S(1)}, u32[]{:S(2)}, u32[]{:S(2)}) collective-permute-start(bf16[272,256]{1,0:T(8,128)(2,1)S(1)} %get-tuple-element.45), channel_id=1, source_target_pairs={{0,12},{2,14},{4,8},{6,10},{8,4},{10,6},{12,0},{14,2},{16,28},{18,... | collective-permute-start | bytes 417800 | tf_op jit(solution)/shard_map/ppermute | solution.py:560
  11.4 15.8 %collective-permute-start.2 = (bf16[528,256]{1,0:T(8,128)(2,1)S(1)}, bf16[528,256]{1,0:T(8,128)(2,1)S(1)}, u32[]{:S(2)}, u32[]{:S(2)}) collective-permute-start(bf16[528,256]{1,0:T(8,128)(2,1)S(1)} %get-tuple-element.42), channel_id=1, source_target_pairs={{0,16},{1,25},{2,30},{3,23},{4,20},{5,29},{6,26},{7,19},{8,24},{9,... | collective-permute-start | bytes 811016 | tf_op jit(solution)/shard_map/ppermute | solution.py:571
  27.3 7.4 %collective-permute-start.6 = (bf16[528,256]{1,0:T(8,128)(2,1)S(1)}, bf16[528,256]{1,0:T(8,128)(2,1)S(1)}, u32[]{:S(2)}, u32[]{:S(2)}) collective-permute-start(bf16[528,256]{1,0:T(8,128)(2,1)S(1)} %collective-permute-done.2.refs_1_.a_ref.refs_0_), channel_id=1, source_target_pairs={{0,1},{1,0},{2,3},{3,2},{4,5},{5,4},{6,7},{7,6},{8,9},{9,8},{10,11... | collective-permute-start | bytes 811016 | tf_op jit(solution)/shard_map/ppermute | solution.py:563
  34.7 1.6 %collective-permute-start.7 = (bf16[544,256]{1,0:T(8,128)(2,1)S(1)}, bf16[544,256]{1,0:T(8,128)(2,1)S(1)}, u32[]{:S(2)}, u32[]{:S(2)}) collective-permute-start(bf16[544,256]{1,0:T(8,128)(2,1)S(1)} %shard_map.92), channel_id=1, source_target_pairs={{0,2},{2,0},{4,6},{6,4},{8,10},{10,8},{12,14},{14,12},{16,18},{18,... | collective-permute-start | bytes 835592 | tf_op jit(solution)/shard_map/ppermute | solution.py:560
  34.8 9.2 %collective-permute-start.13 = (bf16[512,256]{1,0:T(8,128)(2,1)S(1)}, bf16[512,256]{1,0:T(8,128)(2,1)S(1)}, u32[]{:S(2)}, u32[]{:S(2)}) collective-permute-start(bf16[512,256]{1,0:T(8,128)(2,1)S(1)} %get-tuple-element.68), channel_id=1, source_target_pairs={{0,1},{1,0},{2,3},{3,2},{4,5},{5,4},{6,7},{7,6},{8,9},{9,8},{10,11... | collective-permute-start | bytes 786440 | tf_op jit(solution)/shard_map/ppermute | solution.py:563
  39.3 9.8 %collective-permute-start.8 = (bf16[512,256]{1,0:T(8,128)(2,1)S(1)}, bf16[512,256]{1,0:T(8,128)(2,1)S(1)}, u32[]{:S(2)}, u32[]{:S(2)}) collective-permute-start(bf16[512,256]{1,0:T(8,128)(2,1)S(1)} %get-tuple-element.62), channel_id=1, source_target_pairs={{0,1},{1,0},{2,3},{3,2},{4,5},{5,4},{6,7},{7,6},{8,9},{9,8},{10,11... | collective-permute-start | bytes 786440 | tf_op jit(solution)/shard_map/ppermute | solution.py:563
  44.0 1.4 %collective-permute-start.14 = (bf16[256,256]{1,0:T(8,128)(2,1)S(1)}, bf16[256,256]{1,0:T(8,128)(2,1)S(1)}, u32[]{:S(2)}, u32[]{:S(2)}) collective-permute-start(bf16[256,256]{1,0:T(8,128)(2,1)S(1)} %get-tuple-element.73), channel_id=1, source_target_pairs={{0,2},{2,0},{4,6},{6,4},{8,10},{10,8},{12,14},{14,12},{16,18},{18,... | collective-permute-start | bytes 393224 | tf_op jit(solution)/shard_map/ppermute | solution.py:560
  44.1 5.2 %collective-permute-start.18 = (bf16[512,256]{1,0:T(8,128)(2,1)S(1)}, bf16[512,256]{1,0:T(8,128)(2,1)S(1)}, u32[]{:S(2)}, u32[]{:S(2)}) collective-permute-start(bf16[512,256]{1,0:T(8,128)(2,1)S(1)} %get-tuple-element.74), channel_id=1, source_target_pairs={{0,2},{2,0},{4,6},{6,4},{8,10},{10,8},{12,14},{14,12},{16,18},{18,... | collective-permute-start | bytes 786440 | tf_op jit(solution)/shard_map/ppermute | solution.py:560
  44.6 4.7 %collective-permute-start.19 = (bf16[512,256]{1,0:T(8,128)(2,1)S(1)}, bf16[512,256]{1,0:T(8,128)(2,1)S(1)}, u32[]{:S(2)}, u32[]{:S(2)}) collective-permute-start(bf16[512,256]{1,0:T(8,128)(2,1)S(1)} %get-tuple-element.75), channel_id=1, source_target_pairs={{0,2},{2,0},{4,6},{6,4},{8,10},{10,8},{12,14},{14,12},{16,18},{18,... | collective-permute-start | bytes 786440 | tf_op jit(solution)/shard_map/ppermute | solution.py:560
  45.4 8.3 %collective-permute-start.15 = (bf16[512,256]{1,0:T(8,128)(2,1)S(1)}, bf16[512,256]{1,0:T(8,128)(2,1)S(1)}, u32[]{:S(2)}, u32[]{:S(2)}) collective-permute-start(bf16[512,256]{1,0:T(8,128)(2,1)S(1)} %shard_map.100), channel_id=1, source_target_pairs={{0,0},{1,9},{2,14},{3,7},{4,4},{5,13},{6,10},{7,3},{8,8},{9,1},{10... | collective-permute-start | bytes 786440 | tf_op jit(solution)/shard_map/ppermute | solution.py:571
  49.1 1.4 %collective-permute-start.9 = (bf16[256,256]{1,0:T(8,128)(2,1)S(1)}, bf16[256,256]{1,0:T(8,128)(2,1)S(1)}, u32[]{:S(2)}, u32[]{:S(2)}) collective-permute-start(bf16[256,256]{1,0:T(8,128)(2,1)S(1)} %get-tuple-element.64), channel_id=1, source_target_pairs={{0,2},{2,0},{4,6},{6,4},{8,10},{10,8},{12,14},{14,12},{16,18},{18,... | collective-permute-start | bytes 393224 | tf_op jit(solution)/shard_map/ppermute | solution.py:560
  49.5 7.7 %collective-permute-start.20 = (bf16[256,256]{1,0:T(8,128)(2,1)S(1)}, bf16[256,256]{1,0:T(8,128)(2,1)S(1)}, u32[]{:S(2)}, u32[]{:S(2)}) collective-permute-start(bf16[256,256]{1,0:T(8,128)(2,1)S(1)} %get-tuple-element.77), channel_id=1, source_target_pairs={{0,4},{2,6},{4,0},{6,2},{8,12},{10,14},{12,8},{14,10},{16,20},{18,... | collective-permute-start | bytes 393224 | tf_op jit(solution)/shard_map/ppermute | solution.py:560
  50.6 17.5 %collective-permute-start.10 = (bf16[512,256]{1,0:T(8,128)(2,1)S(1)}, bf16[512,256]{1,0:T(8,128)(2,1)S(1)}, u32[]{:S(2)}, u32[]{:S(2)}) collective-permute-start(bf16[512,256]{1,0:T(8,128)(2,1)S(1)} %shard_map.95), channel_id=1, source_target_pairs={{0,16},{1,25},{2,30},{3,23},{4,20},{5,29},{6,26},{7,19},{8,24},{9,... | collective-permute-start | bytes 786440 | tf_op jit(solution)/shard_map/ppermute | solution.py:571
  53.7 14.7 %collective-permute-start.16 = (bf16[512,256]{1,0:T(8,128)(2,1)S(1)}, bf16[512,256]{1,0:T(8,128)(2,1)S(1)}, u32[]{:S(2)}, u32[]{:S(2)}) collective-permute-start(bf16[512,256]{1,0:T(8,128)(2,1)S(1)} %collective-permute-done.15.a_ref.refs_0_), channel_id=1, source_target_pairs={{0,1},{1,0},{2,3},{3,2},{4,5},{5,4},{6,7},{7,6},{8,9},{9,8},{10,11... | collective-permute-start | bytes 786440 | tf_op jit(solution)/shard_map/ppermute | solution.py:563
  57.2 7.9 %collective-permute-start.21 = (bf16[256,256]{1,0:T(8,128)(2,1)S(1)}, bf16[256,256]{1,0:T(8,128)(2,1)S(1)}, u32[]{:S(2)}, u32[]{:S(2)}) collective-permute-start(bf16[256,256]{1,0:T(8,128)(2,1)S(1)} %shard_map.106.a_ref), channel_id=1, source_target_pairs={{0,8},{2,10},{4,12},{6,14},{8,0},{10,2},{12,4},{14,6},{16,24},{18,... | collective-permute-start | bytes 393224 | tf_op jit(solution)/shard_map/ppermute | solution.py:560
  65.1 9.1 %collective-permute-start.22 = (bf16[256,256]{1,0:T(8,128)(2,1)S(1)}, bf16[256,256]{1,0:T(8,128)(2,1)S(1)}, u32[]{:S(2)}, u32[]{:S(2)}) collective-permute-start(bf16[256,256]{1,0:T(8,128)(2,1)S(1)} %shard_map.107.a_ref), channel_id=1, source_target_pairs={{0,16},{2,18},{4,20},{6,22},{8,24},{10,26},{12,28},{14,30},{16,0},... | collective-permute-start | bytes 393224 | tf_op jit(solution)/shard_map/ppermute | solution.py:560
  68.1 11.3 %collective-permute-start.11 = (bf16[512,256]{1,0:T(8,128)(2,1)S(1)}, bf16[512,256]{1,0:T(8,128)(2,1)S(1)}, u32[]{:S(2)}, u32[]{:S(2)}) collective-permute-start(bf16[512,256]{1,0:T(8,128)(2,1)S(1)} %collective-permute-done.10.a_ref.refs_0_), channel_id=1, source_target_pairs={{0,1},{1,0},{2,3},{3,2},{4,5},{5,4},{6,7},{7,6},{8,9},{9,8},{10,11... | collective-permute-start | bytes 786440 | tf_op jit(solution)/shard_map/ppermute | solution.py:563
  68.4 12.1 %collective-permute-start.17 = (bf16[512,256]{1,0:T(8,128)(2,1)S(1)}, bf16[512,256]{1,0:T(8,128)(2,1)S(1)}, u32[]{:S(2)}, u32[]{:S(2)}) collective-permute-start(bf16[512,256]{1,0:T(8,128)(2,1)S(1)} %shard_map.101), channel_id=1, source_target_pairs={{0,2},{2,0},{4,6},{6,4},{8,10},{10,8},{12,14},{14,12},{16,18},{18,... | collective-permute-start | bytes 786440 | tf_op jit(solution)/shard_map/ppermute | solution.py:560
  74.2 5.0 %collective-permute-start.23 = (bf16[256,256]{1,0:T(8,128)(2,1)S(1)}, bf16[256,256]{1,0:T(8,128)(2,1)S(1)}, u32[]{:S(2)}, u32[]{:S(2)}) collective-permute-start(bf16[256,256]{1,0:T(8,128)(2,1)S(1)} %shard_map.108.refs_0_), channel_id=1, source_target_pairs={{0,4},{2,6},{4,0},{6,2},{8,12},{10,14},{12,8},{14,10},{16,20},{18,... | collective-permute-start | bytes 393224 | tf_op jit(solution)/shard_map/ppermute | solution.py:560
  79.3 2.0 %collective-permute-start.24 = (bf16[512,256]{1,0:T(8,128)(2,1)S(1)}, bf16[512,256]{1,0:T(8,128)(2,1)S(1)}, u32[]{:S(2)}, u32[]{:S(2)}) collective-permute-start(bf16[512,256]{1,0:T(8,128)(2,1)S(1)} %shard_map.109.mine_ref), channel_id=1, source_target_pairs={{0,2},{2,0},{4,6},{6,4},{8,10},{10,8},{12,14},{14,12},{16,18},{18,... | collective-permute-start | bytes 786440 | tf_op jit(solution)/shard_map/ppermute | solution.py:560
  79.4 1.9 %collective-permute-start.12 = (bf16[512,256]{1,0:T(8,128)(2,1)S(1)}, bf16[512,256]{1,0:T(8,128)(2,1)S(1)}, u32[]{:S(2)}, u32[]{:S(2)}) collective-permute-start(bf16[512,256]{1,0:T(8,128)(2,1)S(1)} %shard_map.96), channel_id=1, source_target_pairs={{0,2},{2,0},{4,6},{6,4},{8,10},{10,8},{12,14},{14,12},{16,18},{18,... | collective-permute-start | bytes 786440 | tf_op jit(solution)/shard_map/ppermute | solution.py:560

commit v5 on v4

--- a/solution.py
+++ b/solution.py
@@ -468,19 +468,18 @@
     if not final:
         refs[-1][...] = term
         return
-    mine_ref, top_ref, rest_ref, acc_ref = refs[-4:]
+    mine_ref, other_ref, acc_ref = refs[-3:]
     acc_ref[...] = term
     part = block // 2
     mine_ref[...] = acc_ref[pl.ds(pl.multiple_of((r % 2) * part, part), part), :]
     other = acc_ref[pl.ds(pl.multiple_of((1 - r % 2) * part, part), part), :]
-    top_ref[...] = other.astype(bf16)
-    rest_ref[...] = (other - other.astype(bf16).astype(f32)).astype(bf16)
+    other_ref[...] = other.astype(bf16)
 
 
 def place(step, final, ids, sums, acc=(), after=()):
     width, block = sums.shape
     if final:
-        outs = [jax.ShapeDtypeStruct((block // 2, width), kind) for kind in (f32, bf16, bf16)]
+        outs = [jax.ShapeDtypeStruct((block // 2, width), kind) for kind in (f32, bf16)]
         scratch = [pltpu.VMEM((block, width), f32)]
     else:
         outs = [jax.ShapeDtypeStruct((block, width), f32)]

time: 83.4 us -> 83.4 us (level)
    ppermute x17 -> x16, waiting for transfers between devices: 20.3 us -> 20.4 us  [row_swap(): return lax.ppermute(x, 'row', [(i, i ^ mask) for i in range(owners)])]
    ppermute x17 -> x16, starting transfers between devices: 14 us -> 13.8 us  [row_swap(): return lax.ppermute(x, 'row', [(i, i ^ mask) for i in range(owners)])]
  transfers between devices with their start and end apart: 25 -> 24, of which waited for: 11 -> 12; matrix products, arithmetic and copies ran while one was open for 1% -> 1% of each run, Pallas kernels for 26% -> 26%
where the time goes in v5:
time: 83.4 us; the launch traced here: 83.1 us
  waiting for transfers between devices  30.6 us (37%)
  Pallas kernels  25.3 us (30%)
  starting transfers between devices  23.7 us (28%)
  local copies, waits for them, and re-layouts  2.65 us (3%)
  between operations  0.88 us (1%)
    pallas_call x25, Pallas kernels, kernel_call(): pl.pallas_call(body, out_shape=outs, compiler_params=pltpu.CompilerParams...  25.3 us
    ppermute x16, waiting for transfers between devices, row_swap(): return lax.ppermute(x, 'row', [(i, i ^ mask) for i in range(owners)])  20.4 us
    ppermute x16, starting transfers between devices, row_swap(): return lax.ppermute(x, 'row', [(i, i ^ mask) for i in range(owners)])  13.8 us
    ppermute x3, starting transfers between devices, grid_swap(): return lax.ppermute(x, ('row', 'col'), perm)  6.78 us
    ppermute x5, waiting for transfers between devices, col_swap(): return lax.ppermute(x, 'col', [(i, i ^ mask) for i in range(cols_n)])  5.62 us
    ppermute x3, waiting for transfers between devices, grid_swap(): return lax.ppermute(x, ('row', 'col'), perm)  4.55 us
    ppermute x5, starting transfers between devices, col_swap(): return lax.ppermute(x, 'col', [(i, i ^ mask) for i in range(cols_n)])  3.04 us
    unnamed x11, local copies, waits for them, and re-layouts  2.65 us
  transfers between devices with their start and end apart: 24, of which 12 were waited for; matrix products, arithmetic and copies ran while one was open for 1% of the time, Pallas kernels for 26%

profile of v5, /device:TPU:0, one launch (start us, length us, event | category | flops | bytes accessed | tf_op | source)
XLA Modules:
  0.0 83.1 jit_solution(1564095502820356661)
XLA Ops:
  0.6 0.5 collective-permute-start
  1.1 0.1 collective-permute-start.1
  1.2 0.9 %copy.11 = s32[1,2,128,128]{3,2,1,0:T(8,128)S(1)} copy(s32[1,2,128,128]{3,1,2,0:T(2,128)} %bitcast.11) | data formatting | bytes 262144
  2.1 0.8 collective-permute-done.1.tot_oth_ref
  2.9 1.0 %copy-done.1 = bf16[1024,256]{1,0:T(8,128)(2,1)S(1)} copy-done((bf16[1024,256]{1,0:T(8,128)(2,1)S(1)}, bf16[1024,256]{1,0:T(8,128)(2,1)}, u32[]{:S(2)}) %copy-start.1) | copy-done | bytes 524312
  3.9 0.7 copy-done.3
  4.6 2.3 %shard_map.86 = (bf16[272,256]{1,0:T(8,128)(2,1)S(1)}, bf16[272,256]{1,0:T(8,128)(2,1)S(1)}, bf16[272,256]{1,0:T(8,128)(2,1)S(1)}, bf16[272,256]{1,0:T(8,128)(2,1)S(1)}, bf16[528,256]{1,0:T(8,128)(2,1)S(1)}) custom-call(s32[2,128,128]{2,1,0:T(8,128)S(1)} %bitcast.6, bf16[1024,256]{1,0:T(8,128)(2,1)S(1)} %copy-done.1, ...), custom_call_target="tpu_custom_call" | custom-call | flops 3300000000 | bytes 1 | tf_op jit(solution)/shard_map/pallas_call | solution.py:43
  6.9 2.9 %collective-permute-start.3 = (bf16[272,256]{1,0:T(8,128)(2,1)S(1)}, bf16[272,256]{1,0:T(8,128)(2,1)S(1)}, u32[]{:S(2)}, u32[]{:S(2)}) collective-permute-start(bf16[272,256]{1,0:T(8,128)(2,1)S(1)} %get-tuple-element.42), channel_id=1, source_target_pairs={{0,4},{2,6},{4,0},{6,2},{8,12},{10,14},{12,8},{14,10},{16,20},{18,... | collective-permute-start | bytes 417800 | tf_op jit(solution)/shard_map/ppermute | solution.py:559
  9.8 1.6 %collective-permute-start.4 = (bf16[272,256]{1,0:T(8,128)(2,1)S(1)}, bf16[272,256]{1,0:T(8,128)(2,1)S(1)}, u32[]{:S(2)}, u32[]{:S(2)}) collective-permute-start(bf16[272,256]{1,0:T(8,128)(2,1)S(1)} %get-tuple-element.43), channel_id=1, source_target_pairs={{0,8},{2,10},{4,12},{6,14},{8,0},{10,2},{12,4},{14,6},{16,24},{18,... | collective-permute-start | bytes 417800 | tf_op jit(solution)/shard_map/ppermute | solution.py:559
  11.4 3.0 %collective-permute-start.2 = (bf16[528,256]{1,0:T(8,128)(2,1)S(1)}, bf16[528,256]{1,0:T(8,128)(2,1)S(1)}, u32[]{:S(2)}, u32[]{:S(2)}) collective-permute-start(bf16[528,256]{1,0:T(8,128)(2,1)S(1)} %get-tuple-element.41), channel_id=1, source_target_pairs={{0,16},{1,25},{2,30},{3,23},{4,20},{5,29},{6,26},{7,19},{8,24},{9,... | collective-permute-start | bytes 811016 | tf_op jit(solution)/shard_map/ppermute | solution.py:570
  14.4 2.9 %shard_map.87 = (bf16[2,1024,256]{2,1,0:T(8,128)(2,1)S(1)}, f32[8,1024]{1,0:T(8,128)S(1)}, s32[16,128]{1,0:T(8,128)S(1)}) custom-call(s32[2,1024]{1,0:T(2,128)S(1)} %copy-done, bf16[1024,256]{1,0:T(8,128)(2,1)S(1)} %copy-done.2, s32[1,1024]{1,0:T(1,128)S(1)} %bitcast.10, s32[2,128,128]{2,1,0:T(8,128)S(1)} %bitcast.7, ...), custom_call_target="tpu_custom_call" | custom-call | flops 3300000000 | bytes 1 | tf_op jit(solution)/shard_map/pallas_call | solution.py:43
  17.3 3.7 %shard_map.88 = (f32[1024,1024]{1,0:T(8,128)S(1)}, f32[1024,1024]{1,0:T(8,128)S(1)}) custom-call(s32[2,1024,1024]{2,1,0:T(8,128)} %counts_ref.3, f32[8,1024]{1,0:T(8,128)S(1)} %get-tuple-element.46.refs_0_.refs_5_.refs_4_), custom_call_target="tpu_custom_call" | custom-call | bytes 1 | tf_op jit(solution)/shard_map/pallas_call | solution.py:43
  21.1 1.6 %shard_map.89 = (f32[128,256]{1,0:T(8,128)S(1)}, f32[128,256]{1,0:T(8,128)S(1)}, bf16[256,256]{1,0:T(8,128)(2,1)S(1)}, f32[256,1024]{1,0:T(8,128)S(1)}) custom-call(bf16[272,256]{1,0:T(8,128)(2,1)S(1)} %get-tuple-element.39.refs_0_, bf16[272,256]{1,0:T(8,128)(2,1)S(1)} %collective-permute-done.3.refs_1_, ...), custom_call_target="tpu_custom_call" | custom-call | bytes 1 | tf_op jit(solution)/shard_map/pallas_call | solution.py:43
  22.7 4.5 %collective-permute-done.2.refs_1_.a_ref.refs_0_ = bf16[528,256]{1,0:T(8,128)(2,1)S(1)} collective-permute-done((bf16[528,256]{1,0:T(8,128)(2,1)S(1)}, bf16[528,256]{1,0:T(8,128)(2,1)S(1)}, u32[]{:S(2)}, u32[]{:S(2)}) %collective-permute-start.2) | collective-permute-done | bytes 270368 | tf_op jit(solution)/shard_map/ppermute | solution.py:570
  27.3 0.4 collective-permute-start.6
  27.7 3.7 %shard_map.90 = (f32[1024,1024]{1,0:T(8,128)S(1)}, f32[1024,1024]{1,0:T(8,128)S(1)}) custom-call(s32[2,1024,1024]{2,1,0:T(8,128)} %counts_ref.3, f32[1024,1024]{1,0:T(8,128)S(1)} %get-tuple-element.48.refs_7_.refs_0_.refs_6_, bf16[528,256]{1,0:T(8,128)(2,1)S(1)} %collective-permute-done.2.refs_1_.a_ref.refs_0_), custom_call_target="tpu_custom_call" | custom-call | bytes 1 | tf_op jit(solution)/shard_map/pallas_call | solution.py:43
  31.4 1.8 %shard_map.91 = (f32[256,256]{1,0:T(8,128)S(1)}, f32[256,256]{1,0:T(8,128)S(1)}, bf16[512,256]{1,0:T(8,128)(2,1)S(1)}, f32[256,1024]{1,0:T(8,128)S(1)}) custom-call(bf16[272,256]{1,0:T(8,128)(2,1)S(1)} %get-tuple-element.39.refs_0_, bf16[272,256]{1,0:T(8,128)(2,1)S(1)} %collective-permute-done.3.refs_1_, ...), custom_call_target="tpu_custom_call" | custom-call | bytes 1 | tf_op jit(solution)/shard_map/pallas_call | solution.py:43
  33.2 1.4 %collective-permute-done.6.b_ref.refs_1_ = bf16[528,256]{1,0:T(8,128)(2,1)S(1)} collective-permute-done((bf16[528,256]{1,0:T(8,128)(2,1)S(1)}, bf16[528,256]{1,0:T(8,128)(2,1)S(1)}, u32[]{:S(2)}, u32[]{:S(2)}) %collective-permute-start.6) | collective-permute-done | bytes 270368 | tf_op jit(solution)/shard_map/ppermute | solution.py:562
  34.7 0.1 collective-permute-start.7
  34.8 0.3 collective-permute-start.13
  35.1 1.2 %collective-permute-done.7.refs_2_ = bf16[544,256]{1,0:T(8,128)(2,1)S(1)} collective-permute-done((bf16[544,256]{1,0:T(8,128)(2,1)S(1)}, bf16[544,256]{1,0:T(8,128)(2,1)S(1)}, u32[]{:S(2)}, u32[]{:S(2)}) %collective-permute-start.7) | collective-permute-done | bytes 278560 | tf_op jit(solution)/shard_map/ppermute | solution.py:559
  36.3 3.0 %shard_map.93 = (f32[256,256]{1,0:T(8,128)S(1)}, f32[256,256]{1,0:T(8,128)S(1)}, bf16[512,256]{1,0:T(8,128)(2,1)S(1)}, f32[256,1024]{1,0:T(8,128)S(1)}, f32[256,1024]{1,0:T(8,128)S(1)}) custom-call(bf16[528,256]{1,0:T(8,128)(2,1)S(1)} %collective-permute-done.2.refs_1_.a_ref.refs_0_, bf16[528,256]{1,0:T(8,128)(2,1)S(1)} %collective-permute-done.6.b_ref.refs_1_, ...), custom_call_target="tpu_custom_call" | custom-call | bytes 1 | tf_op jit(solution)/shard_map/pallas_call | solution.py:43
  39.3 0.6 collective-permute-start.8
  40.0 1.3 %shard_map.97.refs_0_ = f32[1024,256]{1,0:T(8,128)S(1)} custom-call(s32[2,1024]{1,0:T(2,128)S(1)} %copy-done, f32[256,1024]{1,0:T(8,128)S(1)} %get-tuple-element.69.sum_ref), custom_call_target="tpu_custom_call" | custom-call | bytes 1 | tf_op jit(solution)/shard_map/pallas_call | solution.py:43
  41.2 1.5 %shard_map.98 = (f32[512,256]{1,0:T(8,128)S(1)}, bf16[512,256]{1,0:T(8,128)(2,1)S(1)}) custom-call(s32[2,1024]{1,0:T(2,128)S(1)} %copy-done, f32[256,1024]{1,0:T(8,128)S(1)} %get-tuple-element.68.sum_ref, f32[1024,256]{1,0:T(8,128)S(1)} %shard_map.97.refs_0_), custom_call_target="tpu_custom_call" | custom-call | bytes 1 | tf_op jit(solution)/shard_map/pallas_call | solution.py:43
  42.7 1.2 %collective-permute-done.13.got_ref = bf16[512,256]{1,0:T(8,128)(2,1)S(1)} collective-permute-done((bf16[512,256]{1,0:T(8,128)(2,1)S(1)}, bf16[512,256]{1,0:T(8,128)(2,1)S(1)}, u32[]{:S(2)}, u32[]{:S(2)}) %collective-permute-start.13) | collective-permute-done | bytes 262176 | tf_op jit(solution)/shard_map/ppermute | solution.py:562
  44.1 0.5 collective-permute-start.18
  44.6 0.8 %collective-permute-done.14.core_ref = bf16[256,256]{1,0:T(8,128)(2,1)S(1)} collective-permute-done((bf16[256,256]{1,0:T(8,128)(2,1)S(1)}, bf16[256,256]{1,0:T(8,128)(2,1)S(1)}, u32[]{:S(2)}, u32[]{:S(2)}) %collective-permute-start.14) | collective-permute-done | bytes 131104 | tf_op jit(solution)/shard_map/ppermute | solution.py:559
  45.4 0.7 collective-permute-start.15
  46.1 3.0 %collective-permute-done.8.got_ref = bf16[512,256]{1,0:T(8,128)(2,1)S(1)} collective-permute-done((bf16[512,256]{1,0:T(8,128)(2,1)S(1)}, bf16[512,256]{1,0:T(8,128)(2,1)S(1)}, u32[]{:S(2)}, u32[]{:S(2)}) %collective-permute-start.8) | collective-permute-done | bytes 262176 | tf_op jit(solution)/shard_map/ppermute | solution.py:562
  49.2 0.2 collective-permute-start.9
  49.3 0.1 shard_map.105
  49.4 1.1 %collective-permute-start.19 = (bf16[256,256]{1,0:T(8,128)(2,1)S(1)}, bf16[256,256]{1,0:T(8,128)(2,1)S(1)}, u32[]{:S(2)}, u32[]{:S(2)}) collective-permute-start(bf16[256,256]{1,0:T(8,128)(2,1)S(1)} %get-tuple-element.75), channel_id=1, source_target_pairs={{0,4},{2,6},{4,0},{6,2},{8,12},{10,14},{12,8},{14,10},{16,20},{18,... | collective-permute-start | bytes 393224 | tf_op jit(solution)/shard_map/ppermute | solution.py:559
  50.6 3.1 %collective-permute-start.10 = (bf16[512,256]{1,0:T(8,128)(2,1)S(1)}, bf16[512,256]{1,0:T(8,128)(2,1)S(1)}, u32[]{:S(2)}, u32[]{:S(2)}) collective-permute-start(bf16[512,256]{1,0:T(8,128)(2,1)S(1)} %shard_map.95), channel_id=1, source_target_pairs={{0,16},{1,25},{2,30},{3,23},{4,20},{5,29},{6,26},{7,19},{8,24},{9,... | collective-permute-start | bytes 786440 | tf_op jit(solution)/shard_map/ppermute | solution.py:570
  53.7 1.4 %collective-permute-start.16 = (bf16[512,256]{1,0:T(8,128)(2,1)S(1)}, bf16[512,256]{1,0:T(8,128)(2,1)S(1)}, u32[]{:S(2)}, u32[]{:S(2)}) collective-permute-start(bf16[512,256]{1,0:T(8,128)(2,1)S(1)} %collective-permute-done.15.a_ref.refs_0_), channel_id=1, source_target_pairs={{0,1},{1,0},{2,3},{3,2},{4,5},{5,4},{6,7},{7,6},{8,9},{9,8},{10,11... | collective-permute-start | bytes 786440 | tf_op jit(solution)/shard_map/ppermute | solution.py:562
  55.1 2.1 %collective-permute-done.19.refs_1_ = bf16[256,256]{1,0:T(8,128)(2,1)S(1)} collective-permute-done((bf16[256,256]{1,0:T(8,128)(2,1)S(1)}, bf16[256,256]{1,0:T(8,128)(2,1)S(1)}, u32[]{:S(2)}, u32[]{:S(2)}) %collective-permute-start.19) | collective-permute-done | bytes 131104 | tf_op jit(solution)/shard_map/ppermute | solution.py:559
  57.2 1.7 %collective-permute-start.20 = (bf16[256,256]{1,0:T(8,128)(2,1)S(1)}, bf16[256,256]{1,0:T(8,128)(2,1)S(1)}, u32[]{:S(2)}, u32[]{:S(2)}) collective-permute-start(bf16[256,256]{1,0:T(8,128)(2,1)S(1)} %shard_map.106.a_ref), channel_id=1, source_target_pairs={{0,8},{2,10},{4,12},{6,14},{8,0},{10,2},{12,4},{14,6},{16,24},{18,... | collective-permute-start | bytes 393224 | tf_op jit(solution)/shard_map/ppermute | solution.py:559
  58.9 6.1 %collective-permute-done.20.b_ref = bf16[256,256]{1,0:T(8,128)(2,1)S(1)} collective-permute-done((bf16[256,256]{1,0:T(8,128)(2,1)S(1)}, bf16[256,256]{1,0:T(8,128)(2,1)S(1)}, u32[]{:S(2)}, u32[]{:S(2)}) %collective-permute-start.20) | collective-permute-done | bytes 131104 | tf_op jit(solution)/shard_map/ppermute | solution.py:559
  65.1 3.0 %collective-permute-start.21 = (bf16[256,256]{1,0:T(8,128)(2,1)S(1)}, bf16[256,256]{1,0:T(8,128)(2,1)S(1)}, u32[]{:S(2)}, u32[]{:S(2)}) collective-permute-start(bf16[256,256]{1,0:T(8,128)(2,1)S(1)} %shard_map.107.a_ref), channel_id=1, source_target_pairs={{0,16},{2,18},{4,20},{6,22},{8,24},{10,26},{12,28},{14,30},{16,0},... | collective-permute-start | bytes 393224 | tf_op jit(solution)/shard_map/ppermute | solution.py:559
  68.1 0.3 collective-permute-start.11
  68.5 5.7 %collective-permute-done.21.b_ref = bf16[256,256]{1,0:T(8,128)(2,1)S(1)} collective-permute-done((bf16[256,256]{1,0:T(8,128)(2,1)S(1)}, bf16[256,256]{1,0:T(8,128)(2,1)S(1)}, u32[]{:S(2)}, u32[]{:S(2)}) %collective-permute-start.21) | collective-permute-done | bytes 131104 | tf_op jit(solution)/shard_map/ppermute | solution.py:559
  74.2 1.5 %collective-permute-start.22 = (bf16[256,256]{1,0:T(8,128)(2,1)S(1)}, bf16[256,256]{1,0:T(8,128)(2,1)S(1)}, u32[]{:S(2)}, u32[]{:S(2)}) collective-permute-start(bf16[256,256]{1,0:T(8,128)(2,1)S(1)} %shard_map.108.refs_0_), channel_id=1, source_target_pairs={{0,4},{2,6},{4,0},{6,2},{8,12},{10,14},{12,8},{14,10},{16,20},{18,... | collective-permute-start | bytes 393224 | tf_op jit(solution)/shard_map/ppermute | solution.py:559
  75.7 3.6 %collective-permute-done.22.refs_1_ = bf16[256,256]{1,0:T(8,128)(2,1)S(1)} collective-permute-done((bf16[256,256]{1,0:T(8,128)(2,1)S(1)}, bf16[256,256]{1,0:T(8,128)(2,1)S(1)}, u32[]{:S(2)}, u32[]{:S(2)}) %collective-permute-start.22) | collective-permute-done | bytes 131104 | tf_op jit(solution)/shard_map/ppermute | solution.py:559
  79.4 0.5 collective-permute-start.12
  80.0 0.4 shard_map.102.refs_2_
  80.4 0.4 shard_map.103.refs_2_
  80.8 0.4 shard_map.104.acc_ref
  81.3 1.8 %shard_map.110 = (f32[1024,256]{1,0:T(8,128)}, f32[1024,256]{1,0:T(8,128)}) custom-call(s32[16,128]{1,0:T(8,128)S(1)} %get-tuple-element.40.index_ref, bf16[512,256]{1,0:T(8,128)(2,1)S(1)} %collective-permute-done.12.a_ref.b_ref, bf16[512,256]{1,0:T(8,128)(2,1)S(1)} %collective-permute-done.12.a_ref.b_ref, f32[1024,256]{1,0:T(8,128)S(1)} %shard_map.104.acc_ref, ...), custom_call_target="tpu_custom_call" | custom-call | bytes 1 | tf_op jit(solution)/shard_map/pallas_call | solution.py:43
  (36 shorter events, 0.7 us)
Async XLA Ops:
  0.6 2.3 %collective-permute-start = (bf16[1024,256]{1,0:T(8,128)(2,1)}, bf16[1024,256]{1,0:T(8,128)(2,1)S(1)}, u32[]{:S(2)}, u32[]{:S(2)}) collective-permute-start(bf16[1024,256]{1,0:T(8,128)(2,1)} %own_ref.1), channel_id=1, source_target_pairs={{0,2},{2,0},{4,6},{6,4},{8,10},{10,8},{12,14},{14,12},{16,18},{18,... | collective-permute-start | bytes 1572872 | tf_op jit(solution)/shard_map/ppermute | solution.py:559
  1.1 1.8 %collective-permute-start.1 = (s32[1,1024]{1,0:T(1,128)}, s32[1,1024]{1,0:T(1,128)S(1)}, u32[]{:S(2)}, u32[]{:S(2)}) collective-permute-start(s32[1,1024]{1,0:T(1,128)} %bitcast.8), channel_id=1, source_target_pairs={{0,2},{2,0},{4,6},{6,4},{8,10},{10,8},{12,14},{14,12},{16,18},{18,... | collective-permute-start | bytes 12296 | tf_op jit(solution)/shard_map/ppermute | solution.py:559
  2.9 1.0 %copy-start.1 = (bf16[1024,256]{1,0:T(8,128)(2,1)S(1)}, bf16[1024,256]{1,0:T(8,128)(2,1)}, u32[]{:S(2)}) copy-start(bf16[1024,256]{1,0:T(8,128)(2,1)} %own_ref.1) | copy-start | bytes 1572868
  3.9 0.7 copy-start.3
  4.6 9.8 %copy-start = (s32[2,1024]{1,0:T(2,128)S(1)}, s32[2,1024]{1,0:T(2,128)}, u32[]{:S(2)}) copy-start(s32[2,1024]{1,0:T(2,128)} %ids_ref.5) | copy-start | bytes 24580
  4.6 9.8 %copy-start.2 = (bf16[1024,256]{1,0:T(8,128)(2,1)S(1)}, bf16[1024,256]{1,0:T(8,128)(2,1)}, u32[]{:S(2)}) copy-start(bf16[1024,256]{1,0:T(8,128)(2,1)} %emb_ref.1) | copy-start | bytes 1572868
  4.6 9.8 %copy-start.4 = (s32[1024]{0:T(1024)S(1)}, s32[1024]{0:T(1024)}, u32[]{:S(2)}) copy-start(s32[1024]{0:T(1024)} %param.11) | copy-start | bytes 12292
  6.9 14.1 %collective-permute-start.3 = (bf16[272,256]{1,0:T(8,128)(2,1)S(1)}, bf16[272,256]{1,0:T(8,128)(2,1)S(1)}, u32[]{:S(2)}, u32[]{:S(2)}) collective-permute-start(bf16[272,256]{1,0:T(8,128)(2,1)S(1)} %get-tuple-element.42), channel_id=1, source_target_pairs={{0,4},{2,6},{4,0},{6,2},{8,12},{10,14},{12,8},{14,10},{16,20},{18,... | collective-permute-start | bytes 417800 | tf_op jit(solution)/shard_map/ppermute | solution.py:559
  9.8 11.2 %collective-permute-start.4 = (bf16[272,256]{1,0:T(8,128)(2,1)S(1)}, bf16[272,256]{1,0:T(8,128)(2,1)S(1)}, u32[]{:S(2)}, u32[]{:S(2)}) collective-permute-start(bf16[272,256]{1,0:T(8,128)(2,1)S(1)} %get-tuple-element.43), channel_id=1, source_target_pairs={{0,8},{2,10},{4,12},{6,14},{8,0},{10,2},{12,4},{14,6},{16,24},{18,... | collective-permute-start | bytes 417800 | tf_op jit(solution)/shard_map/ppermute | solution.py:559
  11.4 9.6 %collective-permute-start.5 = (bf16[272,256]{1,0:T(8,128)(2,1)S(1)}, bf16[272,256]{1,0:T(8,128)(2,1)S(1)}, u32[]{:S(2)}, u32[]{:S(2)}) collective-permute-start(bf16[272,256]{1,0:T(8,128)(2,1)S(1)} %get-tuple-element.44), channel_id=1, source_target_pairs={{0,12},{2,14},{4,8},{6,10},{8,4},{10,6},{12,0},{14,2},{16,28},{18,... | collective-permute-start | bytes 417800 | tf_op jit(solution)/shard_map/ppermute | solution.py:559
  11.4 15.8 %collective-permute-start.2 = (bf16[528,256]{1,0:T(8,128)(2,1)S(1)}, bf16[528,256]{1,0:T(8,128)(2,1)S(1)}, u32[]{:S(2)}, u32[]{:S(2)}) collective-permute-start(bf16[528,256]{1,0:T(8,128)(2,1)S(1)} %get-tuple-element.41), channel_id=1, source_target_pairs={{0,16},{1,25},{2,30},{3,23},{4,20},{5,29},{6,26},{7,19},{8,24},{9,... | collective-permute-start | bytes 811016 | tf_op jit(solution)/shard_map/ppermute | solution.py:570
  27.3 7.4 %collective-permute-start.6 = (bf16[528,256]{1,0:T(8,128)(2,1)S(1)}, bf16[528,256]{1,0:T(8,128)(2,1)S(1)}, u32[]{:S(2)}, u32[]{:S(2)}) collective-permute-start(bf16[528,256]{1,0:T(8,128)(2,1)S(1)} %collective-permute-done.2.refs_1_.a_ref.refs_0_), channel_id=1, source_target_pairs={{0,1},{1,0},{2,3},{3,2},{4,5},{5,4},{6,7},{7,6},{8,9},{9,8},{10,11... | collective-permute-start | bytes 811016 | tf_op jit(solution)/shard_map/ppermute | solution.py:562
  34.7 1.6 %collective-permute-start.7 = (bf16[544,256]{1,0:T(8,128)(2,1)S(1)}, bf16[544,256]{1,0:T(8,128)(2,1)S(1)}, u32[]{:S(2)}, u32[]{:S(2)}) collective-permute-start(bf16[544,256]{1,0:T(8,128)(2,1)S(1)} %shard_map.92), channel_id=1, source_target_pairs={{0,2},{2,0},{4,6},{6,4},{8,10},{10,8},{12,14},{14,12},{16,18},{18,... | collective-permute-start | bytes 835592 | tf_op jit(solution)/shard_map/ppermute | solution.py:559
  34.8 9.2 %collective-permute-start.13 = (bf16[512,256]{1,0:T(8,128)(2,1)S(1)}, bf16[512,256]{1,0:T(8,128)(2,1)S(1)}, u32[]{:S(2)}, u32[]{:S(2)}) collective-permute-start(bf16[512,256]{1,0:T(8,128)(2,1)S(1)} %get-tuple-element.67), channel_id=1, source_target_pairs={{0,1},{1,0},{2,3},{3,2},{4,5},{5,4},{6,7},{7,6},{8,9},{9,8},{10,11... | collective-permute-start | bytes 786440 | tf_op jit(solution)/shard_map/ppermute | solution.py:562
  39.3 9.8 %collective-permute-start.8 = (bf16[512,256]{1,0:T(8,128)(2,1)S(1)}, bf16[512,256]{1,0:T(8,128)(2,1)S(1)}, u32[]{:S(2)}, u32[]{:S(2)}) collective-permute-start(bf16[512,256]{1,0:T(8,128)(2,1)S(1)} %get-tuple-element.61), channel_id=1, source_target_pairs={{0,1},{1,0},{2,3},{3,2},{4,5},{5,4},{6,7},{7,6},{8,9},{9,8},{10,11... | collective-permute-start | bytes 786440 | tf_op jit(solution)/shard_map/ppermute | solution.py:562
  44.0 1.4 %collective-permute-start.14 = (bf16[256,256]{1,0:T(8,128)(2,1)S(1)}, bf16[256,256]{1,0:T(8,128)(2,1)S(1)}, u32[]{:S(2)}, u32[]{:S(2)}) collective-permute-start(bf16[256,256]{1,0:T(8,128)(2,1)S(1)} %get-tuple-element.72), channel_id=1, source_target_pairs={{0,2},{2,0},{4,6},{6,4},{8,10},{10,8},{12,14},{14,12},{16,18},{18,... | collective-permute-start | bytes 393224 | tf_op jit(solution)/shard_map/ppermute | solution.py:559
  44.1 5.2 %collective-permute-start.18 = (bf16[512,256]{1,0:T(8,128)(2,1)S(1)}, bf16[512,256]{1,0:T(8,128)(2,1)S(1)}, u32[]{:S(2)}, u32[]{:S(2)}) collective-permute-start(bf16[512,256]{1,0:T(8,128)(2,1)S(1)} %get-tuple-element.73), channel_id=1, source_target_pairs={{0,2},{2,0},{4,6},{6,4},{8,10},{10,8},{12,14},{14,12},{16,18},{18,... | collective-permute-start | bytes 786440 | tf_op jit(solution)/shard_map/ppermute | solution.py:559
  45.4 8.3 %collective-permute-start.15 = (bf16[512,256]{1,0:T(8,128)(2,1)S(1)}, bf16[512,256]{1,0:T(8,128)(2,1)S(1)}, u32[]{:S(2)}, u32[]{:S(2)}) collective-permute-start(bf16[512,256]{1,0:T(8,128)(2,1)S(1)} %shard_map.100), channel_id=1, source_target_pairs={{0,0},{1,9},{2,14},{3,7},{4,4},{5,13},{6,10},{7,3},{8,8},{9,1},{10... | collective-permute-start | bytes 786440 | tf_op jit(solution)/shard_map/ppermute | solution.py:570
  49.2 1.4 %collective-permute-start.9 = (bf16[256,256]{1,0:T(8,128)(2,1)S(1)}, bf16[256,256]{1,0:T(8,128)(2,1)S(1)}, u32[]{:S(2)}, u32[]{:S(2)}) collective-permute-start(bf16[256,256]{1,0:T(8,128)(2,1)S(1)} %get-tuple-element.63), channel_id=1, source_target_pairs={{0,2},{2,0},{4,6},{6,4},{8,10},{10,8},{12,14},{14,12},{16,18},{18,... | collective-permute-start | bytes 393224 | tf_op jit(solution)/shard_map/ppermute | solution.py:559
  49.4 7.7 %collective-permute-start.19 = (bf16[256,256]{1,0:T(8,128)(2,1)S(1)}, bf16[256,256]{1,0:T(8,128)(2,1)S(1)}, u32[]{:S(2)}, u32[]{:S(2)}) collective-permute-start(bf16[256,256]{1,0:T(8,128)(2,1)S(1)} %get-tuple-element.75), channel_id=1, source_target_pairs={{0,4},{2,6},{4,0},{6,2},{8,12},{10,14},{12,8},{14,10},{16,20},{18,... | collective-permute-start | bytes 393224 | tf_op jit(solution)/shard_map/ppermute | solution.py:559
  50.6 17.5 %collective-permute-start.10 = (bf16[512,256]{1,0:T(8,128)(2,1)S(1)}, bf16[512,256]{1,0:T(8,128)(2,1)S(1)}, u32[]{:S(2)}, u32[]{:S(2)}) collective-permute-start(bf16[512,256]{1,0:T(8,128)(2,1)S(1)} %shard_map.95), channel_id=1, source_target_pairs={{0,16},{1,25},{2,30},{3,23},{4,20},{5,29},{6,26},{7,19},{8,24},{9,... | collective-permute-start | bytes 786440 | tf_op jit(solution)/shard_map/ppermute | solution.py:570
  53.7 14.7 %collective-permute-start.16 = (bf16[512,256]{1,0:T(8,128)(2,1)S(1)}, bf16[512,256]{1,0:T(8,128)(2,1)S(1)}, u32[]{:S(2)}, u32[]{:S(2)}) collective-permute-start(bf16[512,256]{1,0:T(8,128)(2,1)S(1)} %collective-permute-done.15.a_ref.refs_0_), channel_id=1, source_target_pairs={{0,1},{1,0},{2,3},{3,2},{4,5},{5,4},{6,7},{7,6},{8,9},{9,8},{10,11... | collective-permute-start | bytes 786440 | tf_op jit(solution)/shard_map/ppermute | solution.py:562
  57.2 7.9 %collective-permute-start.20 = (bf16[256,256]{1,0:T(8,128)(2,1)S(1)}, bf16[256,256]{1,0:T(8,128)(2,1)S(1)}, u32[]{:S(2)}, u32[]{:S(2)}) collective-permute-start(bf16[256,256]{1,0:T(8,128)(2,1)S(1)} %shard_map.106.a_ref), channel_id=1, source_target_pairs={{0,8},{2,10},{4,12},{6,14},{8,0},{10,2},{12,4},{14,6},{16,24},{18,... | collective-permute-start | bytes 393224 | tf_op jit(solution)/shard_map/ppermute | solution.py:559
  65.1 9.1 %collective-permute-start.21 = (bf16[256,256]{1,0:T(8,128)(2,1)S(1)}, bf16[256,256]{1,0:T(8,128)(2,1)S(1)}, u32[]{:S(2)}, u32[]{:S(2)}) collective-permute-start(bf16[256,256]{1,0:T(8,128)(2,1)S(1)} %shard_map.107.a_ref), channel_id=1, source_target_pairs={{0,16},{2,18},{4,20},{6,22},{8,24},{10,26},{12,28},{14,30},{16,0},... | collective-permute-start | bytes 393224 | tf_op jit(solution)/shard_map/ppermute | solution.py:559
  68.1 11.3 %collective-permute-start.11 = (bf16[512,256]{1,0:T(8,128)(2,1)S(1)}, bf16[512,256]{1,0:T(8,128)(2,1)S(1)}, u32[]{:S(2)}, u32[]{:S(2)}) collective-permute-start(bf16[512,256]{1,0:T(8,128)(2,1)S(1)} %collective-permute-done.10.a_ref.refs_0_), channel_id=1, source_target_pairs={{0,1},{1,0},{2,3},{3,2},{4,5},{5,4},{6,7},{7,6},{8,9},{9,8},{10,11... | collective-permute-start | bytes 786440 | tf_op jit(solution)/shard_map/ppermute | solution.py:562
  68.4 12.0 %collective-permute-start.17 = (bf16[512,256]{1,0:T(8,128)(2,1)S(1)}, bf16[512,256]{1,0:T(8,128)(2,1)S(1)}, u32[]{:S(2)}, u32[]{:S(2)}) collective-permute-start(bf16[512,256]{1,0:T(8,128)(2,1)S(1)} %shard_map.101), channel_id=1, source_target_pairs={{0,2},{2,0},{4,6},{6,4},{8,10},{10,8},{12,14},{14,12},{16,18},{18,... | collective-permute-start | bytes 786440 | tf_op jit(solution)/shard_map/ppermute | solution.py:559
  74.2 5.0 %collective-permute-start.22 = (bf16[256,256]{1,0:T(8,128)(2,1)S(1)}, bf16[256,256]{1,0:T(8,128)(2,1)S(1)}, u32[]{:S(2)}, u32[]{:S(2)}) collective-permute-start(bf16[256,256]{1,0:T(8,128)(2,1)S(1)} %shard_map.108.refs_0_), channel_id=1, source_target_pairs={{0,4},{2,6},{4,0},{6,2},{8,12},{10,14},{12,8},{14,10},{16,20},{18,... | collective-permute-start | bytes 393224 | tf_op jit(solution)/shard_map/ppermute | solution.py:559
  79.3 2.0 %collective-permute-start.23 = (bf16[512,256]{1,0:T(8,128)(2,1)S(1)}, bf16[512,256]{1,0:T(8,128)(2,1)S(1)}, u32[]{:S(2)}, u32[]{:S(2)}) collective-permute-start(bf16[512,256]{1,0:T(8,128)(2,1)S(1)} %shard_map.109.mine_ref), channel_id=1, source_target_pairs={{0,2},{2,0},{4,6},{6,4},{8,10},{10,8},{12,14},{14,12},{16,18},{18,... | collective-permute-start | bytes 786440 | tf_op jit(solution)/shard_map/ppermute | solution.py:559
  79.4 1.9 %collective-permute-start.12 = (bf16[512,256]{1,0:T(8,128)(2,1)S(1)}, bf16[512,256]{1,0:T(8,128)(2,1)S(1)}, u32[]{:S(2)}, u32[]{:S(2)}) collective-permute-start(bf16[512,256]{1,0:T(8,128)(2,1)S(1)} %shard_map.96), channel_id=1, source_target_pairs={{0,2},{2,0},{4,6},{6,4},{8,10},{10,8},{12,14},{14,12},{16,18},{18,... | collective-permute-start | bytes 786440 | tf_op jit(solution)/shard_map/ppermute | solution.py:559
